TPU v7x, 32 devices: a whole 2x2x4 slice. The times are simulated.
32 devices in a mesh: seq: 8 (over y, x, core), head: 4 (over z).
Axes of the slice: x: 2, y: 2, z: 4, core: 2. Of those that a mesh axis runs over, the one named last changes fastest.
Arguments:
- tokens: bfloat16 [6144, 2048], P('seq', 'head'), may hold values from -6 to 6
- cotangent: bfloat16 [6144, 2048], P('seq', 'head'), may hold values from -6 to 6
- lengths: int32 [3, 4], replicated, may hold values from 1 to 2048, as said below
- deal_order: int32 [6144], P('seq'), may hold values from 0 to 255, as said below
- norm_gain: float32 [2048], replicated, may hold values from 0.5 to 1.5
- proj_gate: bfloat16 [2048, 4096], P('seq', 'head'), may hold values from -0.125 to 0.125
- proj_inner: bfloat16 [2048, 4096], P('seq', 'head'), may hold values from -0.125 to 0.125
- proj_state: bfloat16 [2048, 256], P('seq'), may hold values from -0.125 to 0.125
- proj_step: bfloat16 [2048, 64], P('seq', 'head'), may hold values from -0.125 to 0.125
- conv_inner: float32 [4, 4096], P(None, 'head'), may hold values from -3 to 3
- conv_inner_bias: float32 [4096], P('head'), may hold values from -3 to 3
- conv_state: float32 [4, 256], replicated, may hold values from -3 to 3
- conv_state_bias: float32 [256], replicated, may hold values from -3 to 3
- step_bias: float32 [64], P('head'), may hold values from -12 to -3
- decay_log: float32 [64], P('head'), may hold values from -2 to 1
- skip_gain: float32 [64], P('head'), may hold values from 0.5 to 1.5
- inner_gain: float32 [4096], P('head'), may hold values from 0.5 to 1.5
- proj_out: bfloat16 [4096, 2048], P('head', 'seq'), may hold values from -0.09375 to 0.09375
Outputs:
- output: bfloat16 [6144, 2048], P('seq', 'head')
- grad_input: bfloat16 [6144, 2048], P('seq', 'head')
- grad_norm_gain: float32 [2048], P('head')
- grad_proj_gate: float32 [2048, 4096], P('seq', 'head')
- grad_proj_inner: float32 [2048, 4096], P('seq', 'head')
- grad_proj_state: float32 [2048, 256], P('head')
- grad_proj_step: float32 [2048, 64], P('seq', 'head')
- grad_conv_inner: float32 [4, 4096], P(None, 'head')
- grad_conv_inner_bias: float32 [4096], P('head')
- grad_conv_state: float32 [4, 256], P(None, 'head')
- grad_conv_state_bias: float32 [256], P('head')
- grad_step_bias: float32 [64], P('head')
- grad_decay_log: float32 [64], P('head')
- grad_skip_gain: float32 [64], P('head')
- grad_inner_gain: float32 [4096], P('head')
- grad_proj_out: float32 [4096, 2048], P('head', 'seq')
Inputs may be any that keep to these rules, and one draw needn't show every extreme that they name: Each row of lengths sums to 2048; its entries are positive. `deal_order`: every aligned block of 256 entries is a permutation of 0 to 255.
All inputs are finite; a program needn't handle non-finite values.
Results may differ from a plain program's by a relative error of at most 0.015.
Values may be sent and summed in bfloat16 or wider, within the bound.
No kernel may reach another device: no remote copies, remote signals or barrier semaphores. Data moves between devices by JAX's collectives and lax.ppermute only.
A program may use at most 256 MiB of HBM per device.

v0:
```python
import jax
import jax.numpy as jnp
from jax import lax
from jax.sharding import PartitionSpec as P

BLOCK = 256


epsilon = 1e-05
highest = lax.Precision.HIGHEST


def passed_along(value, axis, steps):
    count = lax.axis_size(axis)
    initial, last = (max(0, -steps), min(count, count - steps))
    return lax.ppermute(value, axis, [(source, source + steps) for source in range(initial, last)])


def prefix(shard, axis, combine, identity, reverse):
    peers, here = (lax.axis_size(axis), lax.axis_index(axis))
    everything = jax.tree.map(
        lambda part, kind: lax.all_gather(part.astype(kind), axis),
        shard,
        (jnp.bfloat16, jnp.bfloat16),
    )
    start = jax.tree.map(
        lambda part, zero: jnp.broadcast_to(jnp.asarray(zero, part.dtype), part.shape),
        shard,
        identity,
    )

    def turn(k, before):
        at = peers - 1 - k if reverse else k
        reached = at > here if reverse else at < here
        new = combine(
            before, jax.tree.map(lambda part, own: part[at].astype(own.dtype), everything, shard)
        )
        return jax.tree.map(lambda a, b: jnp.where(reached, a, b), new, before)

    return lax.fori_loop(0, peers, turn, start)


def dot_last(left, right):
    return lax.dot_general(
        left, right, (((1,), (1,)), ((), ())), preferred_element_type=jnp.float32
    )


def dot_first(left, right):
    return lax.dot_general(
        left, right, (((0,), (0,)), ((), ())), preferred_element_type=jnp.float32
    )


def exact_last(left, right):
    return lax.dot_general(
        left, right, (((1,), (1,)), ((), ())), precision=highest, preferred_element_type=jnp.float32
    )


def exact_first(left, right):
    return lax.dot_general(
        left, right, (((0,), (0,)), ((), ())), precision=highest, preferred_element_type=jnp.float32
    )


def exact_sum(form, left, right):
    return jnp.einsum(form, left, right, precision=highest, preferred_element_type=jnp.float32)


def silu_slope(values):
    logistic = jax.nn.sigmoid(values)
    return logistic * (1.0 + values * (1.0 - logistic))


def segment_ids(lengths_row, first_row, row_count):
    starts = jnp.cumsum(lengths_row) - lengths_row
    position = first_row + jnp.arange(row_count, dtype=jnp.int32)
    found_seq = jnp.sum((position[:, None] >= starts[None, :]).astype(jnp.int32), axis=1) - 1
    inside = (position >= 0) & (position < jnp.sum(lengths_row))
    return jnp.where(inside, found_seq, jnp.where(position < 0, -1, -2))


def chain_combine(earlier, following):
    return (earlier[0] * following[0], following[0][:, None, None] * earlier[1] + following[1])


def conv_forward(values, before_rows, weight, offset_bias, seg_ext, segment):
    row_count = values.shape[0]
    extended = jnp.concatenate([before_rows, values], axis=0)
    result = jnp.zeros_like(values) + offset_bias[None, :]
    for tap_index in range(weight.shape[0]):
        same_seq = (seg_ext[tap_index : tap_index + row_count] == segment).astype(jnp.float32)
        result = (
            result
            + weight[tap_index][None, :]
            * extended[tap_index : tap_index + row_count]
            * same_seq[:, None]
        )
    return (result, extended)


def conv_backward(grad_out, after_rows, weight, extended, seg_ext, seg_next, segment):
    row_count = grad_out.shape[0]
    taps_total = weight.shape[0]
    grad_ext = jnp.concatenate([grad_out, after_rows], axis=0)
    grad_in = jnp.zeros_like(grad_out)
    weight_rows = []
    for tap_index in range(taps_total):
        lag_rows = taps_total - 1 - tap_index
        ahead_same = (seg_next[lag_rows : lag_rows + row_count] == segment).astype(jnp.float32)
        grad_in = (
            grad_in
            + weight[tap_index][None, :]
            * grad_ext[lag_rows : lag_rows + row_count]
            * ahead_same[:, None]
        )
        behind = (seg_ext[tap_index : tap_index + row_count] == segment).astype(jnp.float32)
        weight_rows.append(
            jnp.sum(
                grad_out * extended[tap_index : tap_index + row_count] * behind[:, None], axis=0
            )
        )
    return (grad_in, jnp.stack(weight_rows), jnp.sum(grad_out, axis=0))


def block_terms(heads_x, step_size, rate_scale, input_map, output_map, segment, before):
    block_width = segment.shape[1]
    cumulative = jnp.cumsum(step_size * rate_scale[None, None, :], axis=1)
    cum_heads = jnp.swapaxes(cumulative, 1, 2)
    offsets = jnp.arange(block_width)
    same_seq = (
        (segment[:, :, None] == segment[:, None, :]) & (offsets[:, None] >= offsets[None, :])
    )[:, None]
    difference = cum_heads[:, :, :, None] - cum_heads[:, :, None, :]
    decay_mat = jnp.where(same_seq, jnp.exp(jnp.where(same_seq, difference, 0.0)), 0.0)
    scores = exact_sum("cin,cjn->cij", output_map, input_map)
    mixing = decay_mat * scores[:, None]
    inputs = step_size[..., None] * heads_x
    inner_out = exact_sum("chij,cjhp->cihp", mixing, inputs)
    last_seg = segment[:, -1]
    fading = (segment == last_seg[:, None]).astype(jnp.float32)[:, :, None] * jnp.exp(
        cumulative[:, -1:, :] - cumulative
    )
    fresh_state = exact_sum("cjhp,cjn->chpn", fading[..., None] * inputs, input_map)
    through = (last_seg == before).astype(jnp.float32)[:, None] * jnp.exp(cumulative[:, -1, :])
    inflow = (segment == before[:, None]).astype(jnp.float32)[:, :, None] * jnp.exp(cumulative)
    return (decay_mat, mixing, inputs, fading, through, inflow, inner_out, fresh_state)


def block_grads(
    grad_y,
    heads_x,
    step_size,
    rate_scale,
    input_map,
    output_map,
    block_parts,
    entering,
    leaving,
    weighted,
    read_back,
):
    decay_mat, mixing, inputs, fading, through, inflow, inner_out, fresh_state = block_parts
    grad_mix = exact_sum("cihp,cjhp->chij", grad_y, inputs)
    pulled = exact_sum("chpn,cjn->cjhp", leaving, input_map)
    grad_inputs = exact_sum("chij,cihp->cjhp", mixing, grad_y) + fading[..., None] * pulled
    grad_scores = jnp.sum(decay_mat * grad_mix, axis=1)
    grad_output_map = exact_sum("cij,cjn->cin", grad_scores, input_map) + exact_sum(
        "cihp,chpn->cin", weighted, entering
    )
    grad_input_map = exact_sum("cij,cin->cjn", grad_scores, output_map) + exact_sum(
        "cjhp,chpn->cjn", fading[..., None] * inputs, leaving
    )
    paired = grad_mix * mixing
    grad_cum = jnp.swapaxes(jnp.sum(paired, axis=3) - jnp.sum(paired, axis=2), 1, 2)
    grad_cum = grad_cum + inflow * jnp.sum(grad_y * read_back, axis=3)
    fade_grad = fading * jnp.sum(inputs * pulled, axis=3)
    through_grad = through * jnp.sum(leaving * entering, axis=(2, 3))
    grad_cum = grad_cum - fade_grad
    grad_cum = grad_cum.at[:, -1, :].add(jnp.sum(fade_grad, axis=1) + through_grad)
    grad_rate = jnp.flip(jnp.cumsum(jnp.flip(grad_cum, axis=1), axis=1), axis=1)
    grad_step = grad_rate * rate_scale[None, None, :] + jnp.sum(grad_inputs * heads_x, axis=3)
    grad_scale = jnp.sum(grad_rate * step_size, axis=(0, 1))
    grad_x = grad_inputs * step_size[..., None]
    return (grad_x, grad_step, grad_scale, grad_input_map, grad_output_map)


def per_device(
    tokens,
    cotangent,
    lengths,
    deal_order,
    norm_gain,
    proj_gate,
    proj_inner,
    proj_state,
    proj_step,
    conv_inner,
    conv_inner_bias,
    conv_state,
    conv_state_bias,
    step_bias,
    decay_log,
    skip_gain,
    inner_gain,
    proj_out,
):
    batch_count = lengths.shape[0]
    rows_local, width_own = tokens.shape
    tok_dev = rows_local // batch_count
    seq_index = lax.axis_index("seq")
    head_index = lax.axis_index("head")
    heads_own = proj_step.shape[1]
    inner_own = proj_inner.shape[1]
    head_width = inner_own // heads_own
    state_width = proj_state.shape[1] // 2
    taps_total = conv_inner.shape[0]
    blocks_total = tok_dev // BLOCK
    width_all = width_own * lax.axis_size("head")
    inner_all = inner_own * lax.axis_size("head")
    slot_order = deal_order.reshape(batch_count, tok_dev)

    def dealt_rows(values):
        return jnp.take_along_axis(
            values.reshape(batch_count, tok_dev, width_own), slot_order[:, :, None], axis=1
        )

    tokens_in, cot_in = (
        lax.all_to_all(dealt_rows(tokens), "seq", split_axis=1, concat_axis=1, tiled=True),
        lax.all_to_all(dealt_rows(cotangent), "seq", split_axis=1, concat_axis=1, tiled=True),
    )
    conv_weight = jnp.concatenate([conv_inner, conv_state], axis=1)
    conv_offset = jnp.concatenate([conv_inner_bias, conv_state_bias])
    rate_scale = -jnp.exp(decay_log)
    gain_own = lax.dynamic_slice_in_dim(norm_gain, head_index * width_own, width_own, 0)
    identity = (
        jnp.ones((heads_own,), jnp.float32),
        jnp.zeros((heads_own, head_width, state_width), jnp.float32),
    )
    outputs = []
    input_grads = []
    totals = None
    for batch_index in range(batch_count):
        gathered = (
            lax.all_gather(proj_gate, "seq", axis=0, tiled=True),
            lax.all_gather(proj_inner, "seq", axis=0, tiled=True),
            lax.all_gather(proj_state, "seq", axis=0, tiled=True),
            lax.all_gather(proj_step, "seq", axis=0, tiled=True),
            lax.all_gather(proj_out, "seq", axis=1, tiled=True),
        )
        full_gate, full_inner, full_state, full_step, full_out = gathered
        rows_bf, cot_full = (
            lax.all_gather(tokens_in[batch_index], "head", axis=1, tiled=True),
            lax.all_gather(cot_in[batch_index], "head", axis=1, tiled=True),
        )
        rows_full = rows_bf.astype(jnp.float32)
        first_row = seq_index * tok_dev
        lengths_row = lengths[batch_index]
        segment = segment_ids(lengths_row, first_row, tok_dev)
        seg_ext = jnp.concatenate(
            [segment_ids(lengths_row, first_row - (taps_total - 1), taps_total - 1), segment]
        )
        seg_next = jnp.concatenate(
            [segment, segment_ids(lengths_row, first_row + tok_dev, taps_total - 1)]
        )
        inv_rms = lax.rsqrt(jnp.mean(rows_full * rows_full, axis=1, keepdims=True) + epsilon)
        unit_rows = rows_full * inv_rms
        normed = (unit_rows * norm_gain[None, :]).astype(jnp.bfloat16)
        gate_pre = jnp.dot(normed, full_gate, preferred_element_type=jnp.float32)
        inner_pre = jnp.dot(normed, full_inner, preferred_element_type=jnp.float32)
        state_pre = jnp.dot(normed, full_state, preferred_element_type=jnp.float32)
        step_pre = jnp.dot(normed, full_step, preferred_element_type=jnp.float32)
        conv_in = jnp.concatenate([inner_pre, state_pre], axis=1)
        before_rows = passed_along(conv_in[tok_dev - (taps_total - 1) :], "seq", 1)
        conv_out, extended = conv_forward(
            conv_in, before_rows, conv_weight, conv_offset, seg_ext, segment
        )
        mixed_act = jax.nn.silu(conv_out)
        heads_x = mixed_act[:, :inner_own].reshape(blocks_total, BLOCK, heads_own, head_width)
        input_map = mixed_act[:, inner_own : inner_own + state_width].reshape(
            blocks_total, BLOCK, state_width
        )
        output_map = mixed_act[:, inner_own + state_width :].reshape(
            blocks_total, BLOCK, state_width
        )
        step_size = jax.nn.softplus(step_pre + step_bias[None, :]).reshape(
            blocks_total, BLOCK, heads_own
        )
        before = seg_ext[taps_total - 2 : taps_total - 2 + tok_dev].reshape(blocks_total, BLOCK)[
            :, 0
        ]
        block_parts = block_terms(
            heads_x,
            step_size,
            rate_scale,
            input_map,
            output_map,
            segment.reshape(blocks_total, BLOCK),
            before,
        )
        through = block_parts[4]
        fresh_state = block_parts[7]
        total_decay, total_state = identity
        block_index = 0
        total_state = through[block_index][:, None, None] * total_state + fresh_state[block_index]
        total_decay = total_decay * through[block_index]
        incoming = prefix((total_decay, total_state), "seq", chain_combine, identity, False)[1]
        carry_state = incoming
        block_index = 0
        entering_list = [carry_state]
        carry_state = through[block_index][:, None, None] * carry_state + fresh_state[block_index]
        entering = jnp.stack(entering_list)
        read_back = exact_sum("cin,chpn->cihp", output_map, entering)
        heads_y = (
            block_parts[6]
            + block_parts[5][..., None] * read_back
            + skip_gain[None, None, :, None] * heads_x
        )
        mixer_out = heads_y.reshape(tok_dev, inner_own)
        gate_act = jax.nn.silu(gate_pre)
        gated_y = mixer_out * gate_act
        grad_normed_y = dot_last(cot_full, full_out)
        scaled = grad_normed_y * inner_gain[None, :]
        square_sum, inner_dot = lax.psum(
            (jnp.sum(gated_y * gated_y, axis=1), jnp.sum(scaled * gated_y, axis=1)), "head"
        )
        inner_inv = lax.rsqrt(square_sum / inner_all + epsilon)[:, None]
        normed_y = (gated_y * inner_inv * inner_gain[None, :]).astype(jnp.bfloat16)
        branch = lax.psum_scatter(
            jnp.dot(normed_y, full_out, preferred_element_type=jnp.float32).astype(jnp.bfloat16),
            "head",
            scatter_dimension=1,
            tiled=True,
        ).astype(jnp.float32)
        outputs.append((tokens_in[batch_index].astype(jnp.float32) + branch).astype(jnp.bfloat16))
        grad_w_out = dot_first(normed_y, cot_full)
        grad_gated = (
            inner_inv * scaled
            - gated_y * (inner_inv * inner_inv * inner_inv) * (inner_dot / inner_all)[:, None]
        )
        grad_inner_gain = jnp.sum(grad_normed_y * gated_y * inner_inv, axis=0)
        grad_heads_y = (grad_gated * gate_act).reshape(blocks_total, BLOCK, heads_own, head_width)
        grad_gate = (grad_gated * mixer_out * silu_slope(gate_pre)).astype(jnp.bfloat16)
        grad_skip = jnp.sum(grad_heads_y * heads_x, axis=(0, 1, 3))
        weighted = block_parts[5][..., None] * grad_heads_y
        local_in = exact_sum("cihp,cin->chpn", weighted, output_map)
        carried = identity[1]
        block_index = 0
        carried = through[block_index][:, None, None] * carried + local_in[block_index]
        outgoing = prefix((total_decay, carried), "seq", chain_combine, identity, True)[1]
        leaving_list = [outgoing] * blocks_total
        carry_grad = outgoing
        block_index = 0
        leaving_list[block_index] = carry_grad
        carry_grad = through[block_index][:, None, None] * carry_grad + local_in[block_index]
        leaving = jnp.stack(leaving_list)
        grad_x, grad_step, grad_scale, grad_input_map, grad_output_map = block_grads(
            grad_heads_y,
            heads_x,
            step_size,
            rate_scale,
            input_map,
            output_map,
            block_parts,
            entering,
            leaving,
            weighted,
            read_back,
        )
        grad_x = grad_x + skip_gain[None, None, :, None] * grad_heads_y
        grad_step_pre = grad_step.reshape(tok_dev, heads_own) * jax.nn.sigmoid(
            step_pre + step_bias[None, :]
        )
        grad_mixed = jnp.concatenate(
            [
                grad_x.reshape(tok_dev, inner_own),
                grad_input_map.reshape(tok_dev, state_width),
                grad_output_map.reshape(tok_dev, state_width),
            ],
            axis=1,
        )
        grad_conv_out = grad_mixed * silu_slope(conv_out)
        after_rows = passed_along(grad_conv_out[: taps_total - 1], "seq", -1)
        grad_conv_in, grad_conv_w, grad_conv_b = conv_backward(
            grad_conv_out, after_rows, conv_weight, extended, seg_ext, seg_next, segment
        )
        grad_inner_low = grad_conv_in[:, :inner_own].astype(jnp.bfloat16)
        grad_state_pre = grad_conv_in[:, inner_own:]
        grad_step_low = grad_step_pre.astype(jnp.bfloat16)
        rows_part = (
            dot_last(grad_gate, full_gate)
            + dot_last(grad_inner_low, full_inner)
            + dot_last(grad_step_low, full_step)
            + exact_last(grad_state_pre, full_state.astype(jnp.float32))
        )
        state_part = exact_first(normed.astype(jnp.float32), grad_state_pre)
        rows_own, grad_w_state, grad_state_taps, grad_state_offset = (
            lax.psum_scatter(rows_part, "head", scatter_dimension=1, tiled=True),
            lax.psum_scatter(state_part, "head", scatter_dimension=0, tiled=True),
            lax.psum_scatter(grad_conv_w[:, inner_own:], "head", scatter_dimension=1, tiled=True),
            lax.psum_scatter(grad_conv_b[inner_own:], "head", scatter_dimension=0, tiled=True),
        )
        unit_own = lax.dynamic_slice_in_dim(unit_rows, head_index * width_own, width_own, 1)
        grad_unit_own = rows_own * gain_own[None, :]
        row_dot = lax.psum(jnp.sum(grad_unit_own * unit_own, axis=1), "head")
        grad_norm_gain = jnp.sum(rows_own * unit_own, axis=0)
        grad_own = inv_rms * (grad_unit_own - unit_own * (row_dot / width_all)[:, None])
        input_grads.append(
            (grad_own + cot_in[batch_index].astype(jnp.float32)).astype(jnp.bfloat16)
        )
        big_parts = (
            dot_first(normed, grad_gate),
            dot_first(normed, grad_inner_low),
            dot_first(normed, grad_step_low),
            grad_w_out,
        )
        small_parts = (
            grad_conv_w[:, :inner_own],
            grad_conv_b[:inner_own],
            grad_state_taps,
            grad_state_offset,
            jnp.sum(grad_step_pre, axis=0),
            grad_scale * rate_scale,
            grad_skip,
            grad_inner_gain,
            grad_norm_gain,
            grad_w_state,
        )
        reduced = (
            (
                lax.psum_scatter(
                    big_parts[0].astype(jnp.bfloat16), "seq", scatter_dimension=0, tiled=True
                ).astype(jnp.float32),
                lax.psum_scatter(
                    big_parts[1].astype(jnp.bfloat16), "seq", scatter_dimension=0, tiled=True
                ).astype(jnp.float32),
                lax.psum_scatter(
                    big_parts[2].astype(jnp.bfloat16), "seq", scatter_dimension=0, tiled=True
                ).astype(jnp.float32),
                lax.psum_scatter(
                    big_parts[3].astype(jnp.bfloat16), "seq", scatter_dimension=1, tiled=True
                ).astype(jnp.float32),
            ),
            (
                lax.psum(small_parts[0].astype(jnp.bfloat16), "seq").astype(jnp.float32),
                lax.psum(small_parts[1].astype(jnp.bfloat16), "seq").astype(jnp.float32),
                lax.psum(small_parts[2].astype(jnp.bfloat16), "seq").astype(jnp.float32),
                lax.psum(small_parts[3].astype(jnp.bfloat16), "seq").astype(jnp.float32),
                lax.psum(small_parts[4].astype(jnp.bfloat16), "seq").astype(jnp.float32),
                lax.psum(small_parts[5].astype(jnp.bfloat16), "seq").astype(jnp.float32),
                lax.psum(small_parts[6].astype(jnp.bfloat16), "seq").astype(jnp.float32),
                lax.psum(small_parts[7].astype(jnp.bfloat16), "seq").astype(jnp.float32),
                lax.psum(small_parts[8].astype(jnp.bfloat16), "seq").astype(jnp.float32),
                lax.psum(small_parts[9].astype(jnp.bfloat16), "seq").astype(jnp.float32),
            ),
        )
        totals = reduced if batch_index == 0 else jax.tree.map(jnp.add, totals, reduced)
    back_out, back_grad = (
        lax.all_to_all(jnp.stack(outputs), "seq", split_axis=1, concat_axis=1, tiled=True),
        lax.all_to_all(jnp.stack(input_grads), "seq", split_axis=1, concat_axis=1, tiled=True),
    )
    batch_rows = jnp.arange(batch_count)[:, None]
    restored_out = (
        jnp.zeros_like(back_out)
        .at[batch_rows, slot_order]
        .set(back_out)
        .reshape(rows_local, width_own)
    )
    restored_grad = (
        jnp.zeros_like(back_grad)
        .at[batch_rows, slot_order]
        .set(back_grad)
        .reshape(rows_local, width_own)
    )
    big_total, small_total = totals
    return (
        restored_out,
        restored_grad,
        small_total[8],
        big_total[0],
        big_total[1],
        small_total[9],
        big_total[2],
        small_total[0],
        small_total[1],
        small_total[2],
        small_total[3],
        small_total[4],
        small_total[5],
        small_total[6],
        small_total[7],
        big_total[3],
    )


def solution(mesh):
    return jax.shard_map(
        per_device,
        mesh=mesh,
        in_specs=(
            P("seq", "head"),
            P("seq", "head"),
            P(),
            P("seq"),
            P(),
            P("seq", "head"),
            P("seq", "head"),
            P("seq", None),
            P("seq", "head"),
            P(None, "head"),
            P("head"),
            P(),
            P(),
            P("head"),
            P("head"),
            P("head"),
            P("head"),
            P("head", "seq"),
        ),
        out_specs=(
            P("seq", "head"),
            P("seq", "head"),
            P("head"),
            P("seq", "head"),
            P("seq", "head"),
            P("head", None),
            P("seq", "head"),
            P(None, "head"),
            P("head"),
            P(None, "head"),
            P("head"),
            P("head"),
            P("head"),
            P("head"),
            P("head"),
            P("head", "seq"),
        ),
        check_vma=False,
    )
```

profile of v0, /device:TPU:0, one launch (start us, length us, event | category | flops | bytes accessed | tf_op | source)
XLA Modules:
  0.0 1736.7 jit_solution(2539566151744473244)
XLA Ops:
  135.7 21.7 %all-gather.34.cloned.1.call-done = bf16[2048,256]{1,0:T(8,128)(2,1)} async-done(((bf16[256,256]{1,0:T(8,128)(2,1)}), bf16[2048,256]{1,0:T(8,128)(2,1)}) %all-gather.34.cloned.1.call-update) | async-done | bytes 1048592 | tf_op jit(solution)/shard_map/all_gather | solution.py:248
  160.9 35.0 %all-gather.32.cloned.1.call-done = bf16[2048,1024]{1,0:T(8,128)(2,1)} async-done(((bf16[256,1024]{1,0:T(8,128)(2,1)}), bf16[2048,1024]{1,0:T(8,128)(2,1)}) %all-gather.32.cloned.1.call-update) | async-done | bytes 4194320 | tf_op jit(solution)/shard_map/all_gather | solution.py:247
  357.3 22.1 %while.93 = (s32[]{:T(128)}, f32[16,64,128]{2,1,0:T(8,128)}, s32[]{:T(128)}, bf16[8,16]{1,0:T(8,128)(2,1)}, bf16[8,16,64,128]{3,2,1,0:T(8,128)(2,1)}, /*index=5*/s32[]{:T(128)}, s32[]{:T(128)}) while((s32[]{:T(128)}, f32[16,64,128]{2,1,0:T(8,128)}, s32[]{:T(128)}, bf16[8,16]{1,0:T(8,128)(2,1)}, ...), condition=%wide.region_8.10_spmd.clone, body=%wide.region_7.9_spmd.clone.sunk | while | flops 655380 | bytes 1310985 | solution.py:40
  390.1 21.7 %while.94 = (s32[]{:T(128)}, f32[16,64,128]{2,1,0:T(8,128)}, s32[]{:T(128)}, bf16[8,16]{1,0:T(8,128)(2,1)}, bf16[8,16,64,128]{3,2,1,0:T(8,128)(2,1)}, /*index=5*/s32[]{:T(128)}, s32[]{:T(128)}) while((s32[]{:T(128)}, f32[16,64,128]{2,1,0:T(8,128)}, s32[]{:T(128)}, bf16[8,16]{1,0:T(8,128)(2,1)}, ...), condition=%wide.region_20.22_spmd.clone, body=%wide.region_19.21_spmd.clone.sunk | while | flops 655380 | bytes 1310985 | solution.py:40
  581.1 26.3 %while.98 = (s32[]{:T(128)}, f32[16,64,128]{2,1,0:T(8,128)}, s32[]{:T(128)}, bf16[8,16]{1,0:T(8,128)(2,1)}, bf16[8,16,64,128]{3,2,1,0:T(8,128)(2,1)}, /*index=5*/s32[]{:T(128)}, s32[]{:T(128)}, s32[]{:T(128)}, s32[]{:T(128)}) while((s32[]{:T(128)}, f32[16,64,128]{2,1,0:T(8,128)}, s32[]{:T(128)}, bf16[8,16]{1,0:T(8,128)(2,1)}, ...), condition=%wide.region_76.78_spmd.clone, body=%wide.region_75.77_spmd.clone.sunk | while | flops 655384 | bytes 1311047 | solution.py:40
  636.0 26.0 %while.97 = (s32[]{:T(128)}, f32[16,64,128]{2,1,0:T(8,128)}, s32[]{:T(128)}, bf16[8,16]{1,0:T(8,128)(2,1)}, bf16[8,16,64,128]{3,2,1,0:T(8,128)(2,1)}, /*index=5*/s32[]{:T(128)}, s32[]{:T(128)}, s32[]{:T(128)}, s32[]{:T(128)}) while((s32[]{:T(128)}, f32[16,64,128]{2,1,0:T(8,128)}, s32[]{:T(128)}, bf16[8,16]{1,0:T(8,128)(2,1)}, ...), condition=%wide.region_58.60_spmd.clone, body=%wide.region_57.59_spmd.clone.sunk | while | flops 655384 | bytes 1311047 | solution.py:40
  690.1 21.8 %while.96 = (s32[]{:T(128)}, f32[16,64,128]{2,1,0:T(8,128)}, s32[]{:T(128)}, bf16[8,16]{1,0:T(8,128)(2,1)}, bf16[8,16,64,128]{3,2,1,0:T(8,128)(2,1)}, /*index=5*/s32[]{:T(128)}, s32[]{:T(128)}, s32[]{:T(128)}, s32[]{:T(128)}) while((s32[]{:T(128)}, f32[16,64,128]{2,1,0:T(8,128)}, s32[]{:T(128)}, bf16[8,16]{1,0:T(8,128)(2,1)}, ...), condition=%wide.region_40.42_spmd.clone, body=%wide.region_39.41_spmd.clone.sunk | while | flops 655384 | bytes 1311047 | solution.py:40
  897.1 40.1 %scatter_fusion = bf16[3,256,512]{2,1,0:T(8,128)(2,1)S(1)} fusion(bf16[3,256,512]{2,1,0:T(8,128)(2,1)S(1)} %broadcast.1159.clone, s32[768]{0:T(1024)S(1)} %reshape.1862, bf16[768,512]{1,0:T(8,128)(2,1)S(1)} %bitcast.736), kind=kCustom, calls=%fused_computation.2 | custom fusion | bytes 2365440 | tf_op jit(solution)/shard_map/scatter | solution.py:467
  944.5 20.7 %reduce-scatter.61.cloned.1.call-done = bf16[256,16]{0,1:T(8,128)(2,1)} async-done(((bf16[2048,16]{0,1:T(8,128)(2,1)}), bf16[256,16]{0,1:T(8,128)(2,1)}) %reduce-scatter.61.cloned.1.call-update) | async-done | bytes 8208 | tf_op jit(solution)/shard_map/reduce_scatter | solution.py:438
  965.1 34.3 %reduce-scatter.63.cloned.1.call-done = bf16[256,16]{0,1:T(8,128)(2,1)} async-done(((bf16[2048,16]{0,1:T(8,128)(2,1)}), bf16[256,16]{0,1:T(8,128)(2,1)}) %reduce-scatter.63.cloned.1.call-update) | async-done | bytes 8208 | tf_op jit(solution)/shard_map/reduce_scatter | solution.py:438
  999.4 34.7 %reduce-scatter.65.cloned.1.call-done = bf16[256,16]{0,1:T(8,128)(2,1)} async-done(((bf16[2048,16]{0,1:T(8,128)(2,1)}), bf16[256,16]{0,1:T(8,128)(2,1)}) %reduce-scatter.65.cloned.1.call-update) | async-done | bytes 8208 | tf_op jit(solution)/shard_map/reduce_scatter | solution.py:438
  1035.5 53.4 %reduce-scatter.67.cloned.1.call-done = bf16[1024,256]{1,0:T(8,128)(2,1)} async-done(((bf16[1024,2048]{1,0:T(8,128)(2,1)}), bf16[1024,256]{1,0:T(8,128)(2,1)}) %reduce-scatter.67.cloned.1.call-update) | async-done | bytes 524304 | tf_op jit(solution)/shard_map/reduce_scatter | solution.py:441
  1088.9 54.9 %reduce-scatter.69.cloned.1.call-done = bf16[1024,256]{1,0:T(8,128)(2,1)} async-done(((bf16[1024,2048]{1,0:T(8,128)(2,1)}), bf16[1024,256]{1,0:T(8,128)(2,1)}) %reduce-scatter.69.cloned.1.call-update) | async-done | bytes 524304 | tf_op jit(solution)/shard_map/reduce_scatter | solution.py:441
  1143.8 54.7 %reduce-scatter.71.cloned.1.call-done = bf16[1024,256]{1,0:T(8,128)(2,1)} async-done(((bf16[1024,2048]{1,0:T(8,128)(2,1)}), bf16[1024,256]{1,0:T(8,128)(2,1)}) %reduce-scatter.71.cloned.1.call-update) | async-done | bytes 524304 | tf_op jit(solution)/shard_map/reduce_scatter | solution.py:441
  1201.0 52.6 %reduce-scatter.45.cloned.1.call-done = bf16[256,1024]{1,0:T(8,128)(2,1)} async-done(((bf16[2048,1024]{1,0:T(8,128)(2,1)}), bf16[256,1024]{1,0:T(8,128)(2,1)}) %reduce-scatter.45.cloned.1.call-update) | async-done | bytes 524304 | tf_op jit(solution)/shard_map/reduce_scatter | solution.py:432
  1253.6 54.6 %reduce-scatter.43.cloned.1.call-done = bf16[256,1024]{1,0:T(8,128)(2,1)} async-done(((bf16[2048,1024]{1,0:T(8,128)(2,1)}), bf16[256,1024]{1,0:T(8,128)(2,1)}) %reduce-scatter.43.cloned.1.call-update) | async-done | bytes 524304 | tf_op jit(solution)/shard_map/reduce_scatter | solution.py:432
  1308.2 55.1 %reduce-scatter.47.cloned.1.call-done = bf16[256,1024]{1,0:T(8,128)(2,1)} async-done(((bf16[2048,1024]{1,0:T(8,128)(2,1)}), bf16[256,1024]{1,0:T(8,128)(2,1)}) %reduce-scatter.47.cloned.1.call-update) | async-done | bytes 524304 | tf_op jit(solution)/shard_map/reduce_scatter | solution.py:432
  1365.9 43.6 %reduce-scatter.41.cloned.1.call-done = f32[256,512]{1,0:T(8,128)} async-done(((f32[256,2048]{1,0:T(8,128)}), f32[256,512]{1,0:T(8,128)}) %reduce-scatter.41.cloned.1.call-update) | async-done | bytes 524304 | tf_op jit(solution)/shard_map/reduce_scatter | solution.py:399
  1409.4 45.4 %reduce-scatter.39.cloned.1.call-done = f32[256,512]{1,0:T(8,128)} async-done(((f32[256,2048]{1,0:T(8,128)}), f32[256,512]{1,0:T(8,128)}) %reduce-scatter.39.cloned.1.call-update) | async-done | bytes 524304 | tf_op jit(solution)/shard_map/reduce_scatter | solution.py:399
  1454.9 45.4 %reduce-scatter.37.cloned.1.call-done = f32[256,512]{1,0:T(8,128)} async-done(((f32[256,2048]{1,0:T(8,128)}), f32[256,512]{1,0:T(8,128)}) %reduce-scatter.37.cloned.1.call-update) | async-done | bytes 524304 | tf_op jit(solution)/shard_map/reduce_scatter | solution.py:399
  1520.5 33.7 %all-reduce.6 = (bf16[512]{0:T(512)(128)(2,1)S(1)}, bf16[512]{0:T(512)(128)(2,1)S(1)}, bf16[512]{0:T(512)(128)(2,1)S(1)}, bf16[4,1024]{1,0:T(4,128)(2,1)S(1)}, b...) all-reduce(bf16[512]{0:T(512)(128)(2,1)S(1)} %get-tuple-element.112, ...), channel_id=1, replica_groups=mesh['seq'=8,'head'=4] {'seq'}, use_global_device_ids=true, to_apply=%region_97.99 | all-reduce | flops 21072 | bytes 84288 | tf_op jit(solution)/shard_map/psum | solution.py:454
  1565.2 40.1 %scatter_fusion.1 = bf16[3,256,512]{2,1,0:T(8,128)(2,1)S(1)} fusion(bf16[3,256,512]{2,1,0:T(8,128)(2,1)S(1)} %broadcast.1159.clone.1, s32[768]{0:T(1024)S(1)} %reshape.1862, bf16[768,512]{1,0:T(8,128)(2,1)S(1)} %bitcast.735), kind=kCustom, calls=%fused_computation.3 | custom fusion | bytes 2365440 | tf_op jit(solution)/shard_map/scatter | solution.py:473
  1617.3 54.7 %reduce-scatter.51.cloned.1.call-done = bf16[256,1024]{1,0:T(8,128)(2,1)} async-done(((bf16[2048,1024]{1,0:T(8,128)(2,1)}), bf16[256,1024]{1,0:T(8,128)(2,1)}) %reduce-scatter.51.cloned.1.call-update) | async-done | bytes 524304 | tf_op jit(solution)/shard_map/reduce_scatter | solution.py:435
  1672.0 55.1 %reduce-scatter.49.cloned.1.call-done = bf16[256,1024]{1,0:T(8,128)(2,1)} async-done(((bf16[2048,1024]{1,0:T(8,128)(2,1)}), bf16[256,1024]{1,0:T(8,128)(2,1)}) %reduce-scatter.49.cloned.1.call-update) | async-done | bytes 524304 | tf_op jit(solution)/shard_map/reduce_scatter | solution.py:435
  (1257 shorter events, 889.6 us)
Async XLA Ops:
  48.8 285.2 %all-gather.60.cloned.1.call-start = ((), (), s32[]{:S(2)}) async-start(), calls=%async_computation.63 | async-start | bytes 1310720 | tf_op jit(solution)/shard_map/all_gather | solution.py:255
  70.4 263.6 %all-gather.38.cloned.1.call-start = ((), (), s32[]{:S(2)}) async-start(), calls=%async_computation.31 | async-start | bytes 4718592 | tf_op jit(solution)/shard_map/all_gather | solution.py:250
  71.2 267.6 %all-gather.56.cloned.1.call-start = ((), (), s32[]{:S(2)}) async-start(), calls=%async_computation.61 | async-start | bytes 1310720 | tf_op jit(solution)/shard_map/all_gather | solution.py:255
  108.7 248.6 %all-gather.42.cloned.1.call-start = ((), (), s32[]{:S(2)}) async-start(), calls=%async_computation.54 | async-start | bytes 2359296 | tf_op jit(solution)/shard_map/all_gather | solution.py:22
  277.9 199.3 %all-gather.52.cloned.1.call-start = ((), (), s32[]{:S(2)}) async-start(), calls=%async_computation.59 | async-start | bytes 1310720 | tf_op jit(solution)/shard_map/all_gather | solution.py:255
  283.4 297.7 %all-gather.62.cloned.1.call-start = ((), (), s32[]{:S(2)}) async-start(), calls=%async_computation.64 | async-start | bytes 2359296 | tf_op jit(solution)/shard_map/all_gather | solution.py:22
  576.9 269.5 %reduce-scatter.59.cloned.1.call-start = ((), (), s32[]{:S(2)}) async-start(), calls=%async_computation.46 | async-start | bytes 2621440 | tf_op jit(solution)/shard_map/reduce_scatter | solution.py:400
  635.5 212.7 %reduce-scatter.57.cloned.1.call-start = ((), (), s32[]{:S(2)}) async-start(), calls=%async_computation.45 | async-start | bytes 2621440 | tf_op jit(solution)/shard_map/reduce_scatter | solution.py:400
  786.6 178.6 %reduce-scatter.61.cloned.1.call-start = ((), (), s32[]{:S(2)}) async-start(), calls=%async_computation.47 | async-start | bytes 73728 | tf_op jit(solution)/shard_map/reduce_scatter | solution.py:438
  788.6 210.8 %reduce-scatter.63.cloned.1.call-start = ((), (), s32[]{:S(2)}) async-start(), calls=%async_computation.48 | async-start | bytes 73728 | tf_op jit(solution)/shard_map/reduce_scatter | solution.py:438
  789.7 244.4 %reduce-scatter.65.cloned.1.call-start = ((), (), s32[]{:S(2)}) async-start(), calls=%async_computation.49 | async-start | bytes 73728 | tf_op jit(solution)/shard_map/reduce_scatter | solution.py:438
  792.1 296.8 %reduce-scatter.67.cloned.1.call-start = ((), (), s32[]{:S(2)}) async-start(), calls=%async_computation.50 | async-start | bytes 4718592 | tf_op jit(solution)/shard_map/reduce_scatter | solution.py:441
  797.1 346.7 %reduce-scatter.69.cloned.1.call-start = ((), (), s32[]{:S(2)}) async-start(), calls=%async_computation.51 | async-start | bytes 4718592 | tf_op jit(solution)/shard_map/reduce_scatter | solution.py:441
  802.7 395.8 %reduce-scatter.71.cloned.1.call-start = ((), (), s32[]{:S(2)}) async-start(), calls=%async_computation.52 | async-start | bytes 4718592 | tf_op jit(solution)/shard_map/reduce_scatter | solution.py:441
  808.3 445.3 %reduce-scatter.45.cloned.1.call-start = ((), (), s32[]{:S(2)}) async-start(), calls=%async_computation.39 | async-start | bytes 4718592 | tf_op jit(solution)/shard_map/reduce_scatter | solution.py:432
  812.7 495.4 %reduce-scatter.43.cloned.1.call-start = ((), (), s32[]{:S(2)}) async-start(), calls=%async_computation.38 | async-start | bytes 4718592 | tf_op jit(solution)/shard_map/reduce_scatter | solution.py:432
  817.2 546.0 %reduce-scatter.47.cloned.1.call-start = ((), (), s32[]{:S(2)}) async-start(), calls=%async_computation.40 | async-start | bytes 4718592 | tf_op jit(solution)/shard_map/reduce_scatter | solution.py:432
  822.0 587.5 %reduce-scatter.41.cloned.1.call-start = ((), (), s32[]{:S(2)}) async-start(), calls=%async_computation.37 | async-start | bytes 2621440 | tf_op jit(solution)/shard_map/reduce_scatter | solution.py:399
  830.2 624.7 %reduce-scatter.39.cloned.1.call-start = ((), (), s32[]{:S(2)}) async-start(), calls=%async_computation.36 | async-start | bytes 2621440 | tf_op jit(solution)/shard_map/reduce_scatter | solution.py:399
  838.2 662.1 %reduce-scatter.37.cloned.1.call-start = ((), (), s32[]{:S(2)}) async-start(), calls=%async_computation.35 | async-start | bytes 2621440 | tf_op jit(solution)/shard_map/reduce_scatter | solution.py:399
  846.3 716.7 %all-reduce.10.cloned.1.call-start = ((), (), s32[]{:S(2)}) async-start(), calls=%async_computation.68 | async-start | bytes 1572864 | tf_op jit(solution)/shard_map/psum | solution.py:455
  851.7 765.5 %reduce-scatter.53.cloned.1.call-start = ((), (), s32[]{:S(2)}) async-start(), calls=%async_computation.43 | async-start | bytes 4718592 | tf_op jit(solution)/shard_map/reduce_scatter | solution.py:435
  856.8 815.2 %reduce-scatter.51.cloned.1.call-start = ((), (), s32[]{:S(2)}) async-start(), calls=%async_computation.42 | async-start | bytes 4718592 | tf_op jit(solution)/shard_map/reduce_scatter | solution.py:435
  880.0 847.0 %reduce-scatter.49.cloned.1.call-start = ((), (), s32[]{:S(2)}) async-start(), calls=%async_computation.41 | async-start | bytes 4718592 | tf_op jit(solution)/shard_map/reduce_scatter | solution.py:435
  (327 other events, 7954.2 us)
Sparse Core Ops, SparseCore 0:
  159.1 36.6 all-gather.31
  197.3 27.9 all-gather.59
  227.2 36.9 all-gather.37
  265.7 27.9 all-gather.55
  384.2 36.7 all-gather.35
  635.6 43.2 reduce-scatter.58
  689.9 44.9 reduce-scatter.56
  740.7 46.0 reduce-scatter.54
  935.5 29.5 reduce-scatter.60
  968.0 31.3 reduce-scatter.62
  1002.7 31.4 reduce-scatter.64
  1037.5 51.3 reduce-scatter.66
  1092.4 51.3 reduce-scatter.68
  1147.2 51.3 reduce-scatter.70
  1202.2 51.3 reduce-scatter.44
  1256.8 51.3 reduce-scatter.42
  1311.9 51.3 reduce-scatter.46
  1365.6 43.8 reduce-scatter.40
  1411.7 43.1 reduce-scatter.38
  1457.0 43.1 reduce-scatter.36
  1504.7 58.2 all-reduce.9
  1566.6 50.6 reduce-scatter.52
  1620.6 51.2 reduce-scatter.50
  1675.7 51.3 reduce-scatter.48
  (17 shorter events, 427.0 us)
where the time goes:
time: 1750 us; the launch traced here: 1740 us
  waiting for transfers between devices  768 us (44%)
  other arithmetic  271 us (15%)
  matrix products  266 us (15%)
  local copies, waits for them, and re-layouts  238 us (14%)
  blocking collectives  138 us (8%)
  between operations  31.3 us (2%)
  starting transfers between devices  24.3 us (1%)
    reduce_scatter x3, waiting for transfers between devices, per_device(): lax.psum_scatter(big_parts[3].astype(jnp.bfloat16), 'seq', scatter_dimens...  163 us
    reduce_scatter x3, waiting for transfers between devices, per_device(): lax.psum_scatter(big_parts[0].astype(jnp.bfloat16), 'seq', scatter_dimens...  162 us
    reduce_scatter x3, waiting for transfers between devices, per_device(): lax.psum_scatter(rows_part, 'head', scatter_dimension=1, tiled=True)  134 us
    dot_general x36, matrix products, exact_sum(): jnp.einsum(form, left, right, precision=highest, preferred_element_type=j...  126 us
    reduce_scatter x3, waiting for transfers between devices, per_device(): lax.psum_scatter(big_parts[1].astype(jnp.bfloat16), 'seq', scatter_dimens...  122 us
    select_n x48, other arithmetic, turn(): return jax.tree.map(lambda a, b: jnp.where(reached, a, b), new, before)  90.3 us
    reduce_scatter x3, waiting for transfers between devices, per_device(): lax.psum_scatter(big_parts[2].astype(jnp.bfloat16), 'seq', scatter_dimens...  89.6 us
    dot_general x12, matrix products, dot_first(): lax.dot_general(left, right, (((0,), (0,)), ((), ())), preferred_element_...  44.9 us
  transfers between devices with their start and end apart: 49, of which 23 were waited for; matrix products, arithmetic and copies ran while one was open for 41% of the time, Pallas kernels for 0%

commit v1 on v0

v1 whole, which is shorter than its diff:
```python
import jax
import jax.numpy as jnp
from jax import lax
from jax.sharding import PartitionSpec as P

epsilon = 1e-05
highest = lax.Precision.HIGHEST
f32 = jnp.float32
bf16 = jnp.bfloat16


def swapped(value, axis, bit):
    return lax.ppermute(value, axis, [(i, i ^ bit) for i in range(lax.axis_size(axis))])


def axis_bits(axis):
    count = lax.axis_size(axis)
    return [1 << k for k in range(count.bit_length() - 1)]


def gather_relative(first, second):
    links = axis_bits("seq")[1:]
    grown = []
    for part, order in ((first, links), (second, links[::-1])):
        grown.append([part[None], [0], order])
    for step in range(len(links)):
        for item in grown:
            held, labels, order = item
            bit = order[step]
            item[0] = jnp.concatenate([held, swapped(held, "seq", bit)], axis=0)
            item[1] = labels + [label ^ bit for label in labels]
    (left, left_labels, _), (right, right_labels, _) = grown
    right = jnp.stack([right[right_labels.index(label)] for label in left_labels])
    own = jnp.concatenate([left, right], axis=2)
    other = swapped(own, "seq", 1)
    full = jnp.stack([own, other], axis=1)
    order = sorted(range(len(left_labels)), key=lambda at: left_labels[at])
    if order != list(range(len(order))):
        full = full[jnp.array(order)]
    return full.reshape((-1,) + own.shape[1:])


def scatter_relative(partial):
    count, rows, columns = partial.shape
    links = axis_bits("seq")[1:]
    pairs = partial.reshape(count // 2, 2, rows, columns)
    mine = added(pairs[:, 0], swapped(pairs[:, 1], "seq", 1))
    parts = []
    for piece, order in (
        (mine[:, :, : columns // 2], links[::-1]),
        (mine[:, :, columns // 2 :], links),
    ):
        parts.append([piece, [2 * at for at in range(count // 2)], order])
    for step in range(len(links)):
        for item in parts:
            held, labels, order = item
            bit = order[step]
            keep = [at for at, label in enumerate(labels) if not label & bit]
            give = [labels.index(labels[at] ^ bit) for at in keep]
            sent = jnp.concatenate([held[at : at + 1] for at in give], axis=0)
            kept = jnp.concatenate([held[at : at + 1] for at in keep], axis=0)
            got = swapped(sent, "seq", bit)
            last = step == len(links) - 1
            item[0] = kept.astype(f32) + got.astype(f32) if last else added(kept, got)
            item[1] = [labels[at] for at in keep]
    return jnp.concatenate([item[0][0] for item in parts], axis=1)


def added(left, right):
    return (left.astype(f32) + right.astype(f32)).astype(left.dtype)


def line_gather(own):
    size, here = lax.axis_size("head"), lax.axis_index("head")
    ups, downs = [], []
    up = down = own
    for step in range(1, size):
        up = lax.ppermute(up, "head", [(i, i + 1) for i in range(step - 1, size - 1)])
        down = lax.ppermute(down, "head", [(i, i - 1) for i in range(1, size - step + 1)])
        ups.append(up)
        downs.append(down)
    slots = [own]
    for step in range(1, size):
        slots.append(jnp.where(here >= step, ups[step - 1], downs[size - step - 1]))
    return slots


def line_scatter(block_of):
    size, here = lax.axis_size("head"), lax.axis_index("head")
    up = down = None
    for step in range(1, size):
        give_up = block_of(jnp.clip(here + size - step, 0, size - 1))
        give_down = block_of(jnp.clip(here - size + step, 0, size - 1))
        if up is not None:
            give_up, give_down = added(give_up, up), added(give_down, down)
        up = lax.ppermute(give_up, "head", [(i, i + 1) for i in range(step)])
        down = lax.ppermute(give_down, "head", [(i, i - 1) for i in range(size - step, size)])
    return block_of(here).astype(f32) + up.astype(f32) + down.astype(f32)


def head_sum(value):
    for bit in axis_bits("head"):
        value = value + swapped(value, "head", bit)
    return value


def seq_sum(value):
    for bit in axis_bits("seq"):
        value = value + swapped(value, "seq", bit)
    return value


def scan_before(decay, state, reverse):
    here = lax.axis_index("seq")
    m, h, p, n = state.shape
    total_decay, total = decay, state
    ahead = jnp.zeros_like(state)
    ahead_decay = jnp.ones_like(decay)
    bits = axis_bits("seq")
    for bit in bits:
        got = swapped(total.astype(bf16), "seq", bit).astype(f32)
        got_decay = swapped(total_decay, "seq", bit)
        later = ((here & bit) == 0) if reverse else ((here & bit) != 0)
        ahead = jnp.where(later, ahead_decay[..., None, None] * got + ahead, ahead)
        ahead_decay = jnp.where(later, ahead_decay * got_decay, ahead_decay)
        if bit != bits[-1]:
            total = jnp.where(
                later,
                total_decay[..., None, None] * got + total,
                got_decay[..., None, None] * total + got,
            )
            total_decay = total_decay * got_decay
    return ahead


def passed_along(value, axis, steps):
    count = lax.axis_size(axis)
    initial, last = (max(0, -steps), min(count, count - steps))
    return lax.ppermute(value, axis, [(source, source + steps) for source in range(initial, last)])


def dot_last(left, right):
    return lax.dot_general(
        left, right, (((1,), (1,)), ((), ())), preferred_element_type=f32
    )


def dot_first(left, right):
    return lax.dot_general(
        left, right, (((0,), (0,)), ((), ())), preferred_element_type=f32
    )


def exact_sum(form, left, right):
    return jnp.einsum(form, left, right, precision=highest, preferred_element_type=f32)


def silu_slope(values):
    logistic = jax.nn.sigmoid(values)
    return logistic * (1.0 + values * (1.0 - logistic))


def segment_ids(lengths_row, first_row, row_count):
    starts = jnp.cumsum(lengths_row) - lengths_row
    position = first_row + jnp.arange(row_count, dtype=jnp.int32)
    found_seq = jnp.sum((position[:, None] >= starts[None, :]).astype(jnp.int32), axis=1) - 1
    inside = (position >= 0) & (position < jnp.sum(lengths_row))
    return jnp.where(inside, found_seq, jnp.where(position < 0, -1, -2))


def block_terms(heads_x, step_size, rate_scale, input_map, output_map, segment, before):
    block_width = segment.shape[1]
    cumulative = jnp.cumsum(step_size * rate_scale[None, None, :], axis=1)
    cum_heads = jnp.swapaxes(cumulative, 1, 2)
    offsets = jnp.arange(block_width)
    same_seq = (
        (segment[:, :, None] == segment[:, None, :]) & (offsets[:, None] >= offsets[None, :])
    )[:, None]
    difference = cum_heads[:, :, :, None] - cum_heads[:, :, None, :]
    decay_mat = jnp.where(same_seq, jnp.exp(jnp.where(same_seq, difference, 0.0)), 0.0)
    scores = exact_sum("cin,cjn->cij", output_map, input_map)
    mixing = decay_mat * scores[:, None]
    inputs = step_size[..., None] * heads_x
    inner_out = exact_sum("chij,cjhp->cihp", mixing, inputs)
    last_seg = segment[:, -1]
    fading = (segment == last_seg[:, None]).astype(jnp.float32)[:, :, None] * jnp.exp(
        cumulative[:, -1:, :] - cumulative
    )
    fresh_state = exact_sum("cjhp,cjn->chpn", fading[..., None] * inputs, input_map)
    through = (last_seg == before).astype(jnp.float32)[:, None] * jnp.exp(cumulative[:, -1, :])
    inflow = (segment == before[:, None]).astype(jnp.float32)[:, :, None] * jnp.exp(cumulative)
    return (decay_mat, mixing, inputs, fading, through, inflow, inner_out, fresh_state)


def block_grads(
    grad_y,
    heads_x,
    step_size,
    rate_scale,
    input_map,
    output_map,
    block_parts,
    entering,
    leaving,
    weighted,
    read_back,
):
    decay_mat, mixing, inputs, fading, through, inflow, inner_out, fresh_state = block_parts
    grad_mix = exact_sum("cihp,cjhp->chij", grad_y, inputs)
    pulled = exact_sum("chpn,cjn->cjhp", leaving, input_map)
    grad_inputs = exact_sum("chij,cihp->cjhp", mixing, grad_y) + fading[..., None] * pulled
    grad_scores = jnp.sum(decay_mat * grad_mix, axis=1)
    grad_output_map = exact_sum("cij,cjn->cin", grad_scores, input_map) + exact_sum(
        "cihp,chpn->cin", weighted, entering
    )
    grad_input_map = exact_sum("cij,cin->cjn", grad_scores, output_map) + exact_sum(
        "cjhp,chpn->cjn", fading[..., None] * inputs, leaving
    )
    paired = grad_mix * mixing
    grad_cum = jnp.swapaxes(jnp.sum(paired, axis=3) - jnp.sum(paired, axis=2), 1, 2)
    grad_cum = grad_cum + inflow * jnp.sum(grad_y * read_back, axis=3)
    fade_grad = fading * jnp.sum(inputs * pulled, axis=3)
    through_grad = through * jnp.sum(leaving * entering, axis=(2, 3))
    grad_cum = grad_cum - fade_grad
    grad_cum = grad_cum.at[:, -1, :].add(jnp.sum(fade_grad, axis=1) + through_grad)
    grad_rate = jnp.flip(jnp.cumsum(jnp.flip(grad_cum, axis=1), axis=1), axis=1)
    grad_step = grad_rate * rate_scale[None, None, :] + jnp.sum(grad_inputs * heads_x, axis=3)
    grad_scale = jnp.sum(grad_rate * step_size, axis=(0, 1))
    grad_x = grad_inputs * step_size[..., None]
    return (grad_x, grad_step, grad_scale, grad_input_map, grad_output_map)


def per_device(
    tokens,
    cotangent,
    lengths,
    deal_order,
    norm_gain,
    proj_gate,
    proj_inner,
    proj_state,
    proj_step,
    conv_inner,
    conv_inner_bias,
    conv_state,
    conv_state_bias,
    step_bias,
    decay_log,
    skip_gain,
    inner_gain,
    proj_out,
):
    batch_count = lengths.shape[0]
    rows_local, width_own = tokens.shape
    tok_dev = rows_local // batch_count
    seq_index = lax.axis_index("seq")
    head_index = lax.axis_index("head")
    seq_size = lax.axis_size("seq")
    head_size = lax.axis_size("head")
    heads_own = proj_step.shape[1]
    inner_own = proj_inner.shape[1]
    head_width = inner_own // heads_own
    state_width = proj_state.shape[1] // 2
    taps_total = conv_inner.shape[0]
    width_all = width_own * head_size
    inner_all = inner_own * head_size
    depth = width_all // seq_size
    per_quarter = seq_size // head_size

    slot_order = deal_order.reshape(batch_count, tok_dev)
    picks = (slot_order[:, :, None] == jnp.arange(tok_dev)[None, None, :]).astype(bf16)

    def dealt(values):
        rows = jnp.einsum(
            "mij,mjf->mif", picks, values.reshape(batch_count, tok_dev, width_own),
            preferred_element_type=f32,
        ).astype(bf16)
        return lax.all_to_all(rows, "seq", split_axis=1, concat_axis=1, tiled=True)

    def returned(values):
        rows = lax.all_to_all(values, "seq", split_axis=1, concat_axis=1, tiled=True)
        rows = jnp.einsum("mij,mif->mjf", picks, rows, preferred_element_type=f32)
        return rows.astype(bf16).reshape(rows_local, width_own)

    def turn_quarter(values):
        lead = values.shape[:-1]
        values = values.reshape(lead + (per_quarter, depth))
        for bit in axis_bits("seq"):
            if bit < per_quarter:
                halves = values.reshape(lead + (per_quarter // (2 * bit), 2, bit, depth))
                turned = jnp.where((seq_index & bit) != 0, jnp.flip(halves, -3), halves)
                values = turned.reshape(lead + (per_quarter, depth))
        return values.reshape(lead + (width_own,))

    def quarter_start(quarter):
        return ((quarter * per_quarter) ^ (seq_index & ~(per_quarter - 1))) * depth

    def all_features(own):
        slots = line_gather(own)
        full = jnp.zeros(own.shape[:-1] + (width_all,), own.dtype)
        for step, slot in enumerate(slots):
            quarter = jnp.remainder(head_index - step + head_size, head_size)
            full = lax.dynamic_update_slice_in_dim(full, slot, quarter_start(quarter), 1)
        return full

    def own_features(partial):
        def block_of(quarter):
            return lax.dynamic_slice_in_dim(partial, quarter_start(quarter), width_own, 1)
        return line_scatter(block_of)

    tokens_in = dealt(tokens)
    cot_in = dealt(cotangent)
    rows = batch_count * tok_dev
    flat_tokens = tokens_in.reshape(rows, width_own)
    flat_cot = cot_in.reshape(rows, width_own)

    half = inner_own // 2
    first = jnp.concatenate([proj_inner[:, :half], proj_state[:, :state_width]], axis=1)
    second = jnp.concatenate([proj_inner[:, half:], proj_state[:, state_width:], proj_step], axis=1)
    full_main = gather_relative(first, second).reshape(width_all, -1)
    cut = half + state_width
    full_inner = jnp.concatenate([full_main[:, :half], full_main[:, cut : cut + half]], axis=1)
    full_state = jnp.concatenate(
        [full_main[:, half:cut], full_main[:, cut + half : cut + half + state_width]], axis=1
    )
    full_step = full_main[:, cut + half + state_width :]
    full_gate = gather_relative(proj_gate[:, :half], proj_gate[:, half:]).reshape(width_all, -1)
    out_t = proj_out.T
    full_out_t = gather_relative(out_t[:, :half], out_t[:, half:]).reshape(width_all, -1)

    rows_bf = all_features(turn_quarter(flat_tokens))
    cot_full = all_features(turn_quarter(flat_cot))

    gain_quarters = turn_quarter(norm_gain.reshape(head_size, width_own))
    gain_rel = jnp.zeros((width_all,), f32)
    for quarter in range(head_size):
        gain_rel = lax.dynamic_update_slice_in_dim(
            gain_rel, gain_quarters[quarter], quarter_start(quarter), 0
        )
    own_start = quarter_start(head_index)
    gain_own = lax.dynamic_slice_in_dim(gain_rel, own_start, width_own, 0)

    first_row = seq_index * tok_dev
    segs = [segment_ids(lengths[b], first_row - (taps_total - 1), tok_dev + 2 * (taps_total - 1)) for b in range(batch_count)]
    seg_all = jnp.stack(segs)
    segment = seg_all[:, taps_total - 1 : taps_total - 1 + tok_dev]
    before = seg_all[:, taps_total - 2]

    rows_full = rows_bf.astype(f32)
    inv_rms = lax.rsqrt(jnp.mean(rows_full * rows_full, axis=1, keepdims=True) + epsilon)
    unit_rows = rows_full * inv_rms
    normed = (unit_rows * gain_rel[None, :]).astype(bf16)
    inner_pre = jnp.dot(normed, full_inner, preferred_element_type=f32)
    state_pre = jnp.dot(normed, full_state, preferred_element_type=f32)
    step_pre = jnp.dot(normed, full_step, preferred_element_type=f32)
    gate_pre = jnp.dot(normed, full_gate, preferred_element_type=f32)
    conv_in = jnp.concatenate([inner_pre, state_pre], axis=1).reshape(batch_count, tok_dev, -1)
    before_rows = passed_along(conv_in[:, tok_dev - (taps_total - 1) :], "seq", 1)

    conv_weight = jnp.concatenate([conv_inner, conv_state], axis=1)
    conv_offset = jnp.concatenate([conv_inner_bias, conv_state_bias])
    rate_scale = -jnp.exp(decay_log)

    extended = jnp.concatenate([before_rows, conv_in], axis=1)
    conv_out = jnp.zeros_like(conv_in) + conv_offset
    for tap in range(taps_total):
        same = (seg_all[:, tap : tap + tok_dev] == segment).astype(f32)
        conv_out = conv_out + conv_weight[tap] * extended[:, tap : tap + tok_dev] * same[..., None]
    mixed_act = jax.nn.silu(conv_out)
    heads_x = mixed_act[:, :, :inner_own].reshape(batch_count, tok_dev, heads_own, head_width)
    input_map = mixed_act[:, :, inner_own : inner_own + state_width]
    output_map = mixed_act[:, :, inner_own + state_width :]
    step_size = jax.nn.softplus(step_pre + step_bias).reshape(batch_count, tok_dev, heads_own)
    block_parts = block_terms(heads_x, step_size, rate_scale, input_map, output_map, segment, before)
    inflow, through, fresh_state = block_parts[5], block_parts[4], block_parts[7]
    entering = scan_before(through, fresh_state, False)
    read_back = exact_sum("cin,chpn->cihp", output_map, entering)
    heads_y = block_parts[6] + inflow[..., None] * read_back + skip_gain[:, None] * heads_x
    mixer_out = heads_y.reshape(rows, inner_own)
    gate_act = jax.nn.silu(gate_pre)
    gated_y = mixer_out * gate_act
    grad_normed_y = jnp.dot(cot_full, full_out_t, preferred_element_type=f32)
    scaled = grad_normed_y * inner_gain
    stats = head_sum(jnp.stack([jnp.sum(gated_y * gated_y, axis=1), jnp.sum(scaled * gated_y, axis=1)]))
    square_sum, inner_dot = stats[0], stats[1]
    inner_inv = lax.rsqrt(square_sum / inner_all + epsilon)[:, None]
    normed_y = (gated_y * inner_inv * inner_gain).astype(bf16)
    branch = own_features(dot_last(normed_y, full_out_t).astype(bf16))
    out_rows = (flat_tokens.astype(f32) + turn_quarter(branch)).astype(bf16)
    out_back = returned(out_rows.reshape(batch_count, tok_dev, width_own))
    grad_out_t = scatter_relative(
        dot_first(cot_full, normed_y).astype(bf16).reshape(seq_size, depth, inner_own)
    )
    grad_gated = (
        inner_inv * scaled
        - gated_y * (inner_inv * inner_inv * inner_inv) * (inner_dot / inner_all)[:, None]
    )
    grad_inner_gain = jnp.sum(grad_normed_y * gated_y * inner_inv, axis=0)
    grad_heads_y = (grad_gated * gate_act).reshape(batch_count, tok_dev, heads_own, head_width)
    grad_gate = (grad_gated * mixer_out * silu_slope(gate_pre)).astype(bf16)
    grad_w_gate = scatter_relative(
        dot_first(normed, grad_gate).astype(bf16).reshape(seq_size, depth, inner_own)
    )
    grad_skip = jnp.sum(grad_heads_y * heads_x, axis=(0, 1, 3))
    weighted = inflow[..., None] * grad_heads_y
    local_in = exact_sum("cihp,cin->chpn", weighted, output_map)
    leaving = scan_before(through, local_in, True)
    grad_x, grad_step, grad_scale, grad_input_map, grad_output_map = block_grads(
        grad_heads_y, heads_x, step_size, rate_scale, input_map, output_map, block_parts,
        entering, leaving, weighted, read_back,
    )
    grad_x = grad_x + skip_gain[:, None] * grad_heads_y
    grad_step_pre = grad_step.reshape(rows, heads_own) * jax.nn.sigmoid(step_pre + step_bias)
    grad_mixed = jnp.concatenate(
        [grad_x.reshape(batch_count, tok_dev, inner_own), grad_input_map, grad_output_map], axis=2
    )
    grad_conv_out = grad_mixed * silu_slope(conv_out)
    after_rows = passed_along(grad_conv_out[:, : taps_total - 1], "seq", -1)
    grad_ext = jnp.concatenate([grad_conv_out, after_rows], axis=1)
    grad_conv_in = jnp.zeros_like(conv_in)
    weight_rows = []
    for tap in range(taps_total):
        lag = taps_total - 1 - tap
        ahead = seg_all[:, taps_total - 1 + lag : taps_total - 1 + lag + tok_dev] == segment
        grad_conv_in = grad_conv_in + conv_weight[tap] * grad_ext[:, lag : lag + tok_dev] * ahead.astype(f32)[..., None]
        behind = (seg_all[:, tap : tap + tok_dev] == segment).astype(f32)
        weight_rows.append(jnp.sum(grad_conv_out * extended[:, tap : tap + tok_dev] * behind[..., None], axis=(0, 1)))
    grad_conv_w = jnp.stack(weight_rows)
    grad_conv_b = jnp.sum(grad_conv_out, axis=(0, 1))
    grad_conv_in = grad_conv_in.reshape(rows, -1)
    grad_inner_low = grad_conv_in[:, :inner_own].astype(bf16)
    grad_state_pre = grad_conv_in[:, inner_own:]
    grad_step_low = grad_step_pre.astype(bf16)
    state_hi = grad_state_pre.astype(bf16)
    rows_part = (
        dot_last(grad_gate, full_gate)
        + dot_last(grad_inner_low, full_inner)
        + dot_last(grad_step_low, full_step)
        + dot_last(state_hi, full_state)
    )
    unit_own = lax.dynamic_slice_in_dim(unit_rows, own_start, width_own, 1)
    row_dot = head_sum(jnp.sum(rows_part * gain_rel * unit_rows, axis=1))
    rows_own = own_features(rows_part.astype(bf16))
    grad_norm_gain = turn_quarter(jnp.sum(rows_own * unit_own, axis=0))
    grad_own = inv_rms * (rows_own * gain_own - unit_own * (row_dot / width_all)[:, None])
    grad_rows_in = (turn_quarter(grad_own) + flat_cot.astype(f32)).astype(bf16)
    grad_back = returned(grad_rows_in.reshape(batch_count, tok_dev, width_own))
    grad_main = scatter_relative(
        dot_first(
            normed,
            jnp.concatenate([grad_inner_low, grad_step_low], axis=1),
        ).astype(bf16).reshape(seq_size, depth, inner_own + heads_own)
    )
    state_part = dot_first(state_hi, normed).astype(bf16)
    grad_w_state = own_features(state_part)
    packed = jnp.concatenate([
        grad_conv_w[:, :inner_own].reshape(-1), grad_conv_b[:inner_own], grad_inner_gain,
        jnp.sum(grad_step_pre, axis=0), grad_scale * rate_scale, grad_skip, grad_norm_gain,
    ])
    packed = seq_sum(packed)
    state_small = head_sum(seq_sum(jnp.concatenate([grad_conv_w[:, inner_own:], grad_conv_b[None, inner_own:]])))
    state_own = state_small.shape[1] // head_size
    state_small = lax.dynamic_slice_in_dim(state_small, head_index * state_own, state_own, 1)
    grad_w_state = seq_sum(turn_quarter(grad_w_state).T.astype(bf16)).astype(f32)
    sizes = [taps_total * inner_own, inner_own, inner_own, heads_own, heads_own, heads_own, width_own]
    pieces, at = [], 0
    for size in sizes:
        pieces.append(packed[at : at + size])
        at += size
    return (
        out_back,
        grad_back,
        pieces[6],
        grad_w_gate,
        grad_main[:, :inner_own],
        grad_w_state,
        grad_main[:, inner_own:],
        pieces[0].reshape(taps_total, inner_own),
        pieces[1],
        state_small[:taps_total],
        state_small[taps_total],
        pieces[3],
        pieces[4],
        pieces[5],
        pieces[2],
        grad_out_t.T,
    )


def solution(mesh):
    return jax.shard_map(
        per_device,
        mesh=mesh,
        in_specs=(
            P("seq", "head"),
            P("seq", "head"),
            P(),
            P("seq"),
            P(),
            P("seq", "head"),
            P("seq", "head"),
            P("seq", None),
            P("seq", "head"),
            P(None, "head"),
            P("head"),
            P(),
            P(),
            P("head"),
            P("head"),
            P("head"),
            P("head"),
            P("head", "seq"),
        ),
        out_specs=(
            P("seq", "head"),
            P("seq", "head"),
            P("head"),
            P("seq", "head"),
            P("seq", "head"),
            P("head", None),
            P("seq", "head"),
            P(None, "head"),
            P("head"),
            P(None, "head"),
            P("head"),
            P("head"),
            P("head"),
            P("head"),
            P("head"),
            P("head", "seq"),
        ),
        check_vma=False,
    )
```

time: 1750 us -> 871 us (0.50)
  waiting for transfers between devices: 768 us -> 157 us
  blocking collectives: 138 us -> 0 us
  starting transfers between devices: 24.3 us -> 158 us
  other arithmetic: 271 us -> 156 us
  matrix products: 266 us -> 173 us
  local copies, waits for them, and re-layouts: 238 us -> 210 us
  between operations: 31.3 us -> 3.91 us
    reduce_scatter x21 -> x0, waiting for transfers between devices: 676 us -> none  [the longest x3 163 us: per_device(): lax.psum_scatter(big_parts[3].astype(jnp.bfloat16), 'seq', scatter_dimens...]
    ppermute x0 -> x83, waiting for transfers between devices: none -> 157 us  [the longest x53 88.4 us: swapped(): lax.ppermute(value, axis, [(i, i ^ bit) for i in range(lax.axis_size(axis...]
    ppermute x0 -> x83, starting transfers between devices: none -> 139 us  [the longest x53 67.5 us: swapped(): lax.ppermute(value, axis, [(i, i ^ bit) for i in range(lax.axis_size(axis...]
    select_n x51 -> x7, other arithmetic: 94.9 us -> 4.29 us  [the longest x6 3.7 us: turn_quarter(): turned = jnp.where(seq_index & bit != 0, jnp.flip(halves, -3), halves)]
    scatter x2 -> x0, local copies, waits for them, and re-layouts: 80.1 us -> none  [the longest x1 40.1 us: per_device(): restored_out = jnp.zeros_like(back_out).at[batch_rows, slot_order].set(ba...]
    all_gather x16 -> x0, waiting for transfers between devices: 74.5 us -> none  [the longest x1 35 us: per_device(): lax.all_gather(proj_inner, 'seq', axis=0, tiled=True)]
    psum x4 -> x0, blocking collectives: 65.2 us -> none  [the longest x1 33.7 us: per_device(): lax.psum(small_parts[8].astype(jnp.bfloat16), 'seq').astype(jnp.float32)]
    dot_general x57 -> x21, matrix products: 183 us -> 122 us  [the longest x12 92.9 us: exact_sum(): jnp.einsum(form, left, right, precision=highest, preferred_element_type=f32)]
  transfers between devices with their start and end apart: 49 -> 89, of which waited for: 23 -> 29; matrix products, arithmetic and copies ran while one was open for 41% -> 48% of each run, Pallas kernels for 0% -> 0%
where the time goes in v1:
time: 871 us; the launch traced here: 859 us
  local copies, waits for them, and re-layouts  210 us (24%)
  matrix products  173 us (20%)
  starting transfers between devices  158 us (18%)
  waiting for transfers between devices  157 us (18%)
  other arithmetic  156 us (18%)
    dot_general x12, matrix products, exact_sum(): jnp.einsum(form, left, right, precision=highest, preferred_element_type=f32)  92.9 us
    ppermute x53, waiting for transfers between devices, swapped(): lax.ppermute(value, axis, [(i, i ^ bit) for i in range(lax.axis_size(axis...  88.4 us
    ppermute x53, starting transfers between devices, swapped(): lax.ppermute(value, axis, [(i, i ^ bit) for i in range(lax.axis_size(axis...  67.5 us
    ppermute x6, waiting for transfers between devices, line_gather(): lax.ppermute(down, 'head', [(i, i - 1) for i in range(1, size - step + 1)])  41.8 us
    ppermute x9, starting transfers between devices, line_scatter(): up = lax.ppermute(give_up, 'head', [(i, i + 1) for i in range(step)])  36.1 us
    convert_element_type x18, other arithmetic, added(): return (left.astype(f32) + right.astype(f32)).astype(left.dtype)  31.6 us
    dot_general x5, matrix products, dot_last(): lax.dot_general(left, right, (((1,), (1,)), ((), ())), preferred_element_...  31.1 us
    rev x5, local copies, waits for them, and re-layouts, turn_quarter(): turned = jnp.where(seq_index & bit != 0, jnp.flip(halves, -3), halves)  25.2 us
  transfers between devices with their start and end apart: 89, of which 29 were waited for; matrix products, arithmetic and copies ran while one was open for 48% of the time, Pallas kernels for 0%

profile of v1, /device:TPU:0, one launch (start us, length us, event | category | flops | bytes accessed | tf_op | source)
XLA Modules:
  0.0 858.8 jit_solution(916244005607396978)
XLA Ops:
  116.7 8.1 collective-permute-start.22
  133.3 28.9 %collective-permute-done.3 = bf16[768,512]{1,0:T(8,128)(2,1)S(1)} collective-permute-done((bf16[768,512]{1,0:T(8,128)(2,1)S(1)}, bf16[768,512]{1,0:T(8,128)(2,1)S(1)}, u32[]{:S(2)}, u32[]{:S(2)}) %collective-permute-start.3) | collective-permute-done | bytes 786464 | tf_op jit(solution)/shard_map/ppermute | solution.py:79
  169.4 18.7 %copy.390 = bf16[4,2,256,1296]{2,1,0,3:T(2,128)(2,1)} copy(bf16[4,2,256,1296]{2,3,0,1:T(8,128)(2,1)S(1)} %pad_maximum_fusion) | data formatting | bytes 10616832 | tf_op jit(solution)/shard_map/stack | solution.py:36
  188.1 12.4 %reshape_reshape.48 = bf16[2048,1296]{0,1:T(8,128)(2,1)} reshape(bf16[4,2,256,1296]{2,1,0,3:T(2,128)(2,1)} %copy.390) | data formatting | bytes 10616832 | tf_op jit(solution)/shard_map/reshape;reshape | solution.py:320
  221.8 11.4 %fusion.36 = (f32[3,256,1280]{2,1,0:T(8,128)S(1)}, f32[3,256,1280]{2,1,0:T(8,128)}) fusion(f32[3,256,1280]{2,1,0:T(8,128)} %bitcast.233, f32[1280]{0:T(1024)S(1)} %copy-done.100, f32[3,256]{1,0:T(4,128)S(1)} %copy-done.118, f32[3,3,1280]{2,1,0:T(4,128)S(1)} %collective-permute-done.11, f32[1280]{0:T(1024)S(1)} %copy-done.102, f32[3,256]{1,0:T(4,128)S(1)} %copy-done.120, ...), kind=kLoop, calls=%fused_computation.62 | loop fusion | flops 17694720 | bytes 11877376 | tf_op jit(solution)/shard_map/jit(silu)/mul | solution.py:369
  289.6 10.8 %collective-permute-done.16 = bf16[3,16,64,128]{3,2,1,0:T(8,128)(2,1)S(1)} collective-permute-done((bf16[3,16,64,128]{3,2,1,0:T(8,128)(2,1)}, bf16[3,16,64,128]{3,2,1,0:T(8,128)(2,1)S(1)}, u32[]{:S(2)}, u32[]{:S(2)}) %collective-permute-start.16) | collective-permute-done | bytes 786464 | tf_op jit(solution)/shard_map/ppermute | solution.py:13
  306.3 15.6 %fusion.38 = f32[3,256,16,64]{1,3,2,0:T(8,128)} fusion(f32[3,256,16,64]{1,3,2,0:T(8,128)S(1)} %bitcast.241, f32[3,256,16,64]{1,3,2,0:T(8,128)S(1)} %fusion.97, f32[3,256,256]{2,1,0:T(8,128)S(1)} %fusion.111, f32[3,16,256]{2,1,0:T(8,128)S(1)} %copy-done.93, pred[3,256,256]{2,1,0:T(8,128)(4,1)S(1)} %copy-done.96, f32[16]{0:T(128)S(1)} %copy-done.154, ...), kind=kOutput, calls=%fused_computation.71 | convolution fusion | flops 2432434176 | bytes 10567744 | tf_op jit(solution)/shard_map/chij,cjhp->cihp/dot_general | solution.py:155
  335.2 11.2 %multiply_reduce_fusion.11 = (f32[768]{0:T(1024)S(1)}, f32[768]{0:T(1024)S(1)}, f32[768,1024]{1,0:T(8,128)}, f32[768,1024]{1,0:T(8,128)}) fusion(f32[1024]{0:T(1024)S(1)} %copy-done.149, f32[768,1024]{1,0:T(8,128)} %reshape.401, f32[768,1024]{1,0:T(8,128)} %fusion.146, bf16[768,2048]{1,0:T(8,128)(2,1)} %select_dynamic-update-slice_fusion, ...), kind=kOutput, calls=%fused_computation.81 | convolution fusion | flops 3229088256 | bytes 19933184 | tf_op jit(solution)/shard_map/dot_general | solution.py:382
  346.4 8.0 collective-permute-start.33
  360.9 8.4 convolution_convert_fusion.3
  386.8 21.2 %fusion.6 = (f32[3,16,256]{2,1,0:T(8,128)}, f32[3,16,256]{2,1,0:T(8,128)}, f32[3,256,256]{2,1,0:T(8,128)}) fusion(f32[3,256,256]{2,1,0:T(8,128)S(1)} %fusion.111, f32[3,16,256]{2,1,0:T(8,128)S(1)} %copy-done.94, pred[3,256,256]{2,1,0:T(8,128)(4,1)S(1)} %copy-done.97, f32[3,256,16,64]{1,3,2,0:T(8,128)} %copy.412, f32[3,256,16,64]{1,3,2,0:T(8,128)} %bitcast.240, ...), kind=kOutput, calls=%fused_computation.6 | convolution fusion | flops 2444795904 | bytes 8257536 | tf_op jit(solution)/shard_map/cihp,cjhp->chij/dot_general | solution.py:155
  422.7 7.3 convolution_convert_fusion.1
  446.2 8.7 %fusion.86 = f32[3,256,128]{2,1,0:T(8,128)} fusion(f32[3,256,16,64]{1,3,2,0:T(8,128)} %copy.412, f32[3,256,16]{1,2,0:T(8,128)} %copy.398, bf16[3,16,64,128]{3,2,1,0:T(8,128)(2,1)S(1)} %collective-permute-done.14, bf16[3,16,64,128]{3,2,1,0:T(8,128)(2,1)} %copy-done.27, bf16[3,16,64,128]{3,2,1,0:T(8,128)(2,1)} %copy-done.50, f32[3,16]{1,0:T(4,128)} %copy-done.131, ...), kind=kOutput, calls=%fused_computation.171 | convolution fusion | flops 1212678144 | bytes 5947779 | tf_op jit(solution)/shard_map/cihp,chpn->cin/dot_general | solution.py:155
  526.6 13.4 %multiply_reduce_fusion.8 = (f32[3,256,16]{1,2,0:T(8,128)S(1)}, f32[3,256,16]{1,2,0:T(8,128)}, f32[3,256,16,64]{1,3,2,0:T(8,128)}) fusion(f32[3,256,16,64]{1,3,2,0:T(8,128)S(1)} %fusion.99, f32[3,256,16]{1,2,0:T(8,128)S(1)} %bitcast.291, f32[3,256,1024]{1,2,0:T(8,128)S(1)} %copy-done.15, f32[3,256,16,64]{1,3,2,0:T(8,128)S(1)} %copy-done.10, ...), kind=kOutput, calls=%fused_computation.74 | convolution fusion | flops 2436341760 | bytes 13811776 | tf_op jit(solution)/shard_map/chij,cihp->cjhp/dot_general | solution.py:155
  553.5 13.6 %multiply_reduce_fusion.5 = (f32[1280]{0:T(1024)S(1)}, f32[1280]{0:T(1024)S(1)}, f32[1280]{0:T(1024)S(1)}, f32[1280]{0:T(1024)S(1)}, f32[1280]{0:T(1024)S(1)}, /*index=5*/f32[3,256,1280]{2,1,0:T(8,128)}) fusion(f32[3,256]{1,0:T(4,128)} %get-tuple-element.270, f32[3,256,1280]{2,1,0:T(8,128)} %bitcast.234, f32[3,3,1280]{2,1,0:T(4,128)} %copy-done.83, ...), kind=kLoop, calls=%fused_computation.60 | loop fusion | flops 24569600 | bytes 15809536 | tf_op jit(solution)/shard_map/reduce_sum | solution.py:427
  577.9 8.8 %collective-permute-done.77 = f32[5,256]{1,0:T(8,128)S(1)} collective-permute-done((f32[5,256]{1,0:T(8,128)S(1)}, f32[5,256]{1,0:T(8,128)S(1)}, u32[]{:S(2)}, u32[]{:S(2)}) %collective-permute-start.77) | collective-permute-done | bytes 5152 | tf_op jit(solution)/shard_map/ppermute | solution.py:13
  598.1 8.4 fusion.28
  615.7 7.2 multiply_reduce_fusion.1
  631.6 10.7 %reshape_reshape.59 = bf16[4,2,256,1040]{2,1,0,3:T(2,128)(2,1)} reshape(bf16[2048,1040]{0,1:T(8,128)(2,1)} %convolution_convert_fusion) | data formatting | bytes 8519680 | tf_op jit(solution)/shard_map/reshape;reshape | solution.py:46
  642.3 10.2 %fusion.151 = (bf16[4,1,256,1040]{2,1,0,3:T(2,128)(2,1)}, bf16[4,1,256,1040]{2,1,0,3:T(2,128)(2,1)S(1)}) fusion(bf16[4,2,256,1040]{2,1,0,3:T(2,128)(2,1)} %reshape_reshape.59), kind=kLoop, calls=%fused_computation.370 | loop fusion | bytes 8519680 | tf_op jit(solution)/shard_map/slice | solution.py:47
  673.8 15.4 %collective-permute-done.66 = bf16[256,512]{1,0:T(8,128)(2,1)S(1)} collective-permute-done((bf16[256,512]{1,0:T(8,128)(2,1)S(1)}, bf16[256,512]{1,0:T(8,128)(2,1)S(1)}, u32[]{:S(2)}, u32[]{:S(2)}) %collective-permute-start.66) | collective-permute-done | bytes 262176 | tf_op jit(solution)/shard_map/ppermute | solution.py:96
  776.6 11.4 %collective-permute-done.73 = bf16[512,256]{1,0:T(8,128)(2,1)S(1)} collective-permute-done((bf16[512,256]{1,0:T(8,128)(2,1)S(1)}, bf16[512,256]{1,0:T(8,128)(2,1)S(1)}, u32[]{:S(2)}, u32[]{:S(2)}) %collective-permute-start.73) | collective-permute-done | bytes 262176 | tf_op jit(solution)/shard_map/ppermute | solution.py:13
  798.2 10.6 %collective-permute-done.62 = bf16[2,256,520]{1,2,0:T(8,128)(2,1)S(1)} collective-permute-done((bf16[2,256,520]{1,2,0:T(8,128)(2,1)S(1)}, bf16[2,256,520]{1,2,0:T(8,128)(2,1)S(1)}, u32[]{:S(2)}, u32[]{:S(2)}) %collective-permute-start.62) | collective-permute-done | bytes 532512 | tf_op jit(solution)/shard_map/ppermute | solution.py:13
  838.8 11.9 %collective-permute-done.54 = f32[6704]{0:T(1024)S(1)} collective-permute-done((f32[6704]{0:T(1024)S(1)}, f32[6704]{0:T(1024)S(1)}, u32[]{:S(2)}, u32[]{:S(2)}) %collective-permute-start.54) | collective-permute-done | bytes 26848 | tf_op jit(solution)/shard_map/ppermute | solution.py:13
  (769 shorter events, 562.3 us)
Async XLA Ops:
  9.5 46.7 %collective-permute-start.8 = (bf16[1,256,656]{1,2,0:T(8,128)(2,1)S(1)}, bf16[1,256,656]{1,2,0:T(8,128)(2,1)}, u32[]{:S(2)}, u32[]{:S(2)}) collective-permute-start(bf16[1,256,656]{1,2,0:T(8,128)(2,1)S(1)} %maximum_bitcast_fusion.1), channel_id=1, source_target_pairs={{0,16},{4,20},{8,24},{12,28},{16,0},{20,4},{24,8},{28,12},{1,17},{... | collective-permute-start | bytes 1007624 | tf_op jit(solution)/shard_map/ppermute | solution.py:13
  10.3 43.9 %collective-permute-start.6 = (bf16[1,256,640]{1,2,0:T(8,128)(2,1)S(1)}, bf16[1,256,640]{1,2,0:T(8,128)(2,1)}, u32[]{:S(2)}, u32[]{:S(2)}) collective-permute-start(bf16[1,256,640]{1,2,0:T(8,128)(2,1)S(1)} %maximum_bitcast_fusion.2), channel_id=1, source_target_pairs={{0,8},{4,12},{8,0},{12,4},{16,24},{20,28},{24,16},{28,20},{1,9},{5... | collective-permute-start | bytes 983048 | tf_op jit(solution)/shard_map/ppermute | solution.py:13
  51.9 64.8 %collective-permute-start.20 = (bf16[2,256,512]{2,1,0:T(8,128)(2,1)}, bf16[2,256,512]{2,1,0:T(8,128)(2,1)}, u32[]{:S(2)}, u32[]{:S(2)}) collective-permute-start(bf16[2,256,512]{2,1,0:T(8,128)(2,1)} %pad_maximum_fusion.18), channel_id=1, source_target_pairs={{0,8},{4,12},{8,0},{12,4},{16,24},{20,28},{24,16},{28,20},{1,9},{5... | collective-permute-start | bytes 1572872 | tf_op jit(solution)/shard_map/ppermute | solution.py:13
  56.1 50.1 %collective-permute-start.7 = (bf16[2,256,640]{1,2,0:T(8,128)(2,1)}, bf16[2,256,640]{1,2,0:T(8,128)(2,1)}, u32[]{:S(2)}, u32[]{:S(2)}) collective-permute-start(bf16[2,256,640]{1,2,0:T(8,128)(2,1)} %pad_maximum_fusion.15), channel_id=1, source_target_pairs={{0,16},{4,20},{8,24},{12,28},{16,0},{20,4},{24,8},{28,12},{1,17},{... | collective-permute-start | bytes 1966088 | tf_op jit(solution)/shard_map/ppermute | solution.py:13
  84.9 41.0 %collective-permute-start.18 = (bf16[2,256,512]{2,1,0:T(8,128)(2,1)S(1)}, bf16[2,256,512]{2,1,0:T(8,128)(2,1)S(1)}, u32[]{:S(2)}, u32[]{:S(2)}) collective-permute-start(bf16[2,256,512]{2,1,0:T(8,128)(2,1)S(1)} %copy-done.81), channel_id=1, source_target_pairs={{0,16},{4,20},{8,24},{12,28},{16,0},{20,4},{24,8},{28,12},{1,17},{... | collective-permute-start | bytes 1572872 | tf_op jit(solution)/shard_map/ppermute | solution.py:13
  107.9 61.0 %collective-permute-start.10 = (bf16[4,256,1296]{1,2,0:T(8,128)(2,1)S(1)}, bf16[4,256,1296]{1,2,0:T(8,128)(2,1)S(1)}, u32[]{:S(2)}, u32[]{:S(2)}) collective-permute-start(bf16[4,256,1296]{1,2,0:T(8,128)(2,1)S(1)} %maximum_maximum_fusion), channel_id=1, source_target_pairs={{0,4},{4,0},{8,12},{12,8},{16,20},{20,16},{24,28},{28,24},{1,5},{5... | collective-permute-start | bytes 7962632 | tf_op jit(solution)/shard_map/ppermute | solution.py:13
  116.7 46.2 %collective-permute-start.22 = (bf16[768,512]{1,0:T(8,128)(2,1)S(1)}, bf16[768,512]{1,0:T(8,128)(2,1)}, u32[]{:S(2)}, u32[]{:S(2)}) collective-permute-start(bf16[768,512]{1,0:T(8,128)(2,1)S(1)} %bitcast.268), channel_id=1, source_target_pairs={{0,1},{1,2},{2,3},{4,5},{5,6},{6,7},{8,9},{9,10},{10,11},{12,13},{... | collective-permute-start | bytes 2359304 | tf_op jit(solution)/shard_map/ppermute | solution.py:78
  162.3 87.8 %collective-permute-start.32 = (bf16[4,256,1024]{2,1,0:T(8,128)(2,1)}, bf16[4,256,1024]{2,1,0:T(8,128)(2,1)}, u32[]{:S(2)}, u32[]{:S(2)}) collective-permute-start(bf16[4,256,1024]{2,1,0:T(8,128)(2,1)} %maximum_maximum_fusion.2), channel_id=1, source_target_pairs={{0,4},{4,0},{8,12},{12,8},{16,20},{20,16},{24,28},{28,24},{1,5},{5... | collective-permute-start | bytes 6291464 | tf_op jit(solution)/shard_map/ppermute | solution.py:13
  162.8 91.4 %collective-permute-start.21 = (bf16[4,256,1024]{2,1,0:T(8,128)(2,1)}, bf16[4,256,1024]{2,1,0:T(8,128)(2,1)}, u32[]{:S(2)}, u32[]{:S(2)}) collective-permute-start(bf16[4,256,1024]{2,1,0:T(8,128)(2,1)} %maximum_maximum_fusion.1), channel_id=1, source_target_pairs={{0,4},{4,0},{8,12},{12,8},{16,20},{20,16},{24,28},{28,24},{1,5},{5... | collective-permute-start | bytes 6291464 | tf_op jit(solution)/shard_map/ppermute | solution.py:13
  163.4 84.2 %collective-permute-start.24 = (bf16[768,512]{1,0:T(8,128)(2,1)}, bf16[768,512]{1,0:T(8,128)(2,1)}, u32[]{:S(2)}, u32[]{:S(2)}) collective-permute-start(bf16[768,512]{1,0:T(8,128)(2,1)} %collective-permute-done.23), channel_id=1, source_target_pairs={{1,0},{2,1},{5,4},{6,5},{9,8},{10,9},{13,12},{14,13},{17,16},{18,1... | collective-permute-start | bytes 2359304 | tf_op jit(solution)/shard_map/ppermute | solution.py:79
  164.7 84.2 %collective-permute-start.26 = (bf16[768,512]{1,0:T(8,128)(2,1)}, bf16[768,512]{1,0:T(8,128)(2,1)}, u32[]{:S(2)}, u32[]{:S(2)}) collective-permute-start(bf16[768,512]{1,0:T(8,128)(2,1)} %collective-permute-done.22), channel_id=1, source_target_pairs={{1,2},{2,3},{5,6},{6,7},{9,10},{10,11},{13,14},{14,15},{17,18},{18... | collective-permute-start | bytes 2359304 | tf_op jit(solution)/shard_map/ppermute | solution.py:78
  436.0 42.8 %collective-permute-start.38 = (bf16[768,512]{1,0:T(8,128)(2,1)}, bf16[768,512]{1,0:T(8,128)(2,1)}, u32[]{:S(2)}, u32[]{:S(2)}) collective-permute-start(bf16[768,512]{1,0:T(8,128)(2,1)} %get-tuple-element.215), channel_id=1, source_target_pairs={{3,2},{7,6},{11,10},{15,14},{19,18},{23,22},{27,26},{31,30}} | collective-permute-start | bytes 2359304 | tf_op jit(solution)/shard_map/ppermute | solution.py:97
  439.1 52.4 %collective-permute-start.56 = (bf16[4,256,1024]{2,1,0:T(8,128)(2,1)}, bf16[4,256,1024]{2,1,0:T(8,128)(2,1)}, u32[]{:S(2)}, u32[]{:S(2)}) collective-permute-start(bf16[4,256,1024]{2,1,0:T(8,128)(2,1)} %slice_bitcast_fusion), channel_id=1, source_target_pairs={{0,4},{4,0},{8,12},{12,8},{16,20},{20,16},{24,28},{28,24},{1,5},{5... | collective-permute-start | bytes 6291464 | tf_op jit(solution)/shard_map/ppermute | solution.py:13
  446.2 51.7 %collective-permute-start.80 = (bf16[4,256,1024]{1,2,0:T(8,128)(2,1)}, bf16[4,256,1024]{1,2,0:T(8,128)(2,1)}, u32[]{:S(2)}, u32[]{:S(2)}) collective-permute-start(bf16[4,256,1024]{1,2,0:T(8,128)(2,1)} %bitcast.275), channel_id=1, source_target_pairs={{0,4},{4,0},{8,12},{12,8},{16,20},{20,16},{24,28},{28,24},{1,5},{5... | collective-permute-start | bytes 6291464 | tf_op jit(solution)/shard_map/ppermute | solution.py:13
  482.4 90.3 %collective-permute-start.39 = (bf16[768,512]{1,0:T(8,128)(2,1)}, bf16[768,512]{1,0:T(8,128)(2,1)}, u32[]{:S(2)}, u32[]{:S(2)}) collective-permute-start(bf16[768,512]{1,0:T(8,128)(2,1)} %get-tuple-element.213), channel_id=1, source_target_pairs={{2,1},{3,2},{6,5},{7,6},{10,9},{11,10},{14,13},{15,14},{18,17},{19... | collective-permute-start | bytes 2359304 | tf_op jit(solution)/shard_map/ppermute | solution.py:97
  484.0 228.3 %collective-permute-start.37 = (bf16[768,512]{1,0:T(8,128)(2,1)}, bf16[768,512]{1,0:T(8,128)(2,1)}, u32[]{:S(2)}, u32[]{:S(2)}) collective-permute-start(bf16[768,512]{1,0:T(8,128)(2,1)} %get-tuple-element.212), channel_id=1, source_target_pairs={{0,1},{1,2},{2,3},{4,5},{5,6},{6,7},{8,9},{9,10},{10,11},{12,13},{... | collective-permute-start | bytes 2359304 | tf_op jit(solution)/shard_map/ppermute | solution.py:96
  496.7 173.5 %collective-permute-start.59 = (bf16[2,256,512]{2,1,0:T(8,128)(2,1)}, bf16[2,256,512]{2,1,0:T(8,128)(2,1)}, u32[]{:S(2)}, u32[]{:S(2)}) collective-permute-start(bf16[2,256,512]{2,1,0:T(8,128)(2,1)} %pad_maximum_fusion.21), channel_id=1, source_target_pairs={{0,8},{4,12},{8,0},{12,4},{16,24},{20,28},{24,16},{28,20},{1,9},{5... | collective-permute-start | bytes 1572872 | tf_op jit(solution)/shard_map/ppermute | solution.py:13
  497.9 162.7 %collective-permute-start.57 = (bf16[2,256,512]{2,1,0:T(8,128)(2,1)}, bf16[2,256,512]{2,1,0:T(8,128)(2,1)}, u32[]{:S(2)}, u32[]{:S(2)}) collective-permute-start(bf16[2,256,512]{2,1,0:T(8,128)(2,1)} %concatenate.166), channel_id=1, source_target_pairs={{0,16},{4,20},{8,24},{12,28},{16,0},{20,4},{24,8},{28,12},{1,17},{... | collective-permute-start | bytes 1572872 | tf_op jit(solution)/shard_map/ppermute | solution.py:13
  572.0 91.2 %collective-permute-start.81 = (bf16[2,256,512]{1,2,0:T(8,128)(2,1)}, bf16[2,256,512]{1,2,0:T(8,128)(2,1)}, u32[]{:S(2)}, u32[]{:S(2)}) collective-permute-start(bf16[2,256,512]{1,2,0:T(8,128)(2,1)} %concatenate.170), channel_id=1, source_target_pairs={{0,16},{4,20},{8,24},{12,28},{16,0},{20,4},{24,8},{28,12},{1,17},{... | collective-permute-start | bytes 1572872 | tf_op jit(solution)/shard_map/ppermute | solution.py:13
  660.6 52.4 %collective-permute-start.40 = (bf16[768,512]{1,0:T(8,128)(2,1)S(1)}, bf16[768,512]{1,0:T(8,128)(2,1)S(1)}, u32[]{:S(2)}, u32[]{:S(2)}) collective-permute-start(bf16[768,512]{1,0:T(8,128)(2,1)S(1)} %add_convert_fusion.6), channel_id=1, source_target_pairs={{1,0},{2,1},{3,2},{5,4},{6,5},{7,6},{9,8},{10,9},{11,10},{13,12},{... | collective-permute-start | bytes 2359304 | tf_op jit(solution)/shard_map/ppermute | solution.py:97
  663.2 70.6 %collective-permute-start.45 = (bf16[768,512]{1,0:T(8,128)(2,1)}, bf16[768,512]{1,0:T(8,128)(2,1)}, u32[]{:S(2)}, u32[]{:S(2)}) collective-permute-start(bf16[768,512]{1,0:T(8,128)(2,1)} %get-tuple-element.210), channel_id=1, source_target_pairs={{0,1},{4,5},{8,9},{12,13},{16,17},{20,21},{24,25},{28,29}} | collective-permute-start | bytes 2359304 | tf_op jit(solution)/shard_map/ppermute | solution.py:96
  709.7 47.6 %collective-permute-start.48 = (bf16[768,512]{1,0:T(8,128)(2,1)}, bf16[768,512]{1,0:T(8,128)(2,1)}, u32[]{:S(2)}, u32[]{:S(2)}) collective-permute-start(bf16[768,512]{1,0:T(8,128)(2,1)} %get-tuple-element.211), channel_id=1, source_target_pairs={{3,2},{7,6},{11,10},{15,14},{19,18},{23,22},{27,26},{31,30}} | collective-permute-start | bytes 2359304 | tf_op jit(solution)/shard_map/ppermute | solution.py:97
  711.4 51.7 %collective-permute-start.61 = (bf16[4,256,1040]{1,2,0:T(8,128)(2,1)}, bf16[4,256,1040]{1,2,0:T(8,128)(2,1)}, u32[]{:S(2)}, u32[]{:S(2)}) collective-permute-start(bf16[4,256,1040]{1,2,0:T(8,128)(2,1)} %bitcast.212), channel_id=1, source_target_pairs={{0,4},{4,0},{8,12},{12,8},{16,20},{20,16},{24,28},{28,24},{1,5},{5... | collective-permute-start | bytes 6389768 | tf_op jit(solution)/shard_map/ppermute | solution.py:13
  772.4 41.5 %collective-permute-start.47 = (bf16[768,512]{1,0:T(8,128)(2,1)}, bf16[768,512]{1,0:T(8,128)(2,1)S(1)}, u32[]{:S(2)}, u32[]{:S(2)}) collective-permute-start(bf16[768,512]{1,0:T(8,128)(2,1)} %get-tuple-element.208), channel_id=1, source_target_pairs={{0,1},{1,2},{2,3},{4,5},{5,6},{6,7},{8,9},{9,10},{10,11},{12,13},{... | collective-permute-start | bytes 2359304 | tf_op jit(solution)/shard_map/ppermute | solution.py:96
  (226 other events, 3271.4 us)

commit v2 on v1

v2 whole, which is shorter than its diff:
```python
import functools
import jax
import jax.numpy as jnp
from jax import lax
from jax.experimental import pallas as pl
from jax.experimental.pallas import tpu as pltpu
from jax.sharding import PartitionSpec as P

epsilon = 1e-05
highest = lax.Precision.HIGHEST
f32 = jnp.float32
bf16 = jnp.bfloat16
LANES = 128
HALO = 8
STATE_PAD = 16
VMEM_BYTES = 56 * 1024 * 1024


def swapped(value, axis, bit):
    return lax.ppermute(value, axis, [(i, i ^ bit) for i in range(lax.axis_size(axis))])


def axis_bits(axis):
    count = lax.axis_size(axis)
    return [1 << k for k in range(count.bit_length() - 1)]


def added(left, right):
    return (left.astype(f32) + right.astype(f32)).astype(left.dtype)


def gathered(part, order):
    held, labels = part[None], [0]
    for bit in order:
        held = jnp.concatenate([held, swapped(held, "seq", bit)], axis=0)
        labels = labels + [label ^ bit for label in labels]
    if labels != sorted(labels):
        held = jnp.concatenate([held[at : at + 1] for at in map(labels.index, sorted(labels))])
    return held.reshape(-1, part.shape[1])


def gather_weight(first, second):
    links = axis_bits("seq")[1:]
    own = (gathered(first, links), gathered(second, links[::-1]))
    return own, tuple(swapped(half, "seq", 1) for half in own)


def scattered(keep, send, labels, order):
    rows = keep.shape[0] // len(labels)
    kept = keep.reshape(len(labels), rows, -1)
    sent = send.reshape(len(labels), rows, -1)
    for step, bit in enumerate(order):
        got = swapped(sent, "seq", bit)
        if step == len(order) - 1:
            return kept[0].astype(f32) + got[0].astype(f32)
        total = added(kept, got)
        after = order[step + 1]
        keep_at = [at for at, label in enumerate(labels) if not label & after]
        send_at = [labels.index(labels[at] ^ after) for at in keep_at]
        kept = jnp.concatenate([total[at : at + 1] for at in keep_at])
        sent = jnp.concatenate([total[at : at + 1] for at in send_at])
        labels = [labels[at] for at in keep_at]


def line_gather(own):
    size = lax.axis_size("head")
    ups, downs = [], []
    up = down = own
    for step in range(1, size):
        up = lax.ppermute(up, "head", [(i, i + 1) for i in range(step - 1, size - 1)])
        down = lax.ppermute(down, "head", [(i, i - 1) for i in range(1, size - step + 1)])
        ups.append(up)
        downs.append(down)
    return ups, downs


def line_scatter(blocks):
    size, here = lax.axis_size("head"), lax.axis_index("head")

    def block_of(at):
        return lax.dynamic_index_in_dim(blocks, jnp.clip(at, 0, size - 1), 0, keepdims=False)

    up = down = None
    for step in range(1, size):
        give_up = blocks[size - 1] if step == 1 else block_of(here + size - step)
        give_down = blocks[0] if step == 1 else block_of(here - size + step)
        if up is not None:
            give_up, give_down = added(give_up, up), added(give_down, down)
        up = lax.ppermute(give_up, "head", [(i, i + 1) for i in range(step)])
        down = lax.ppermute(give_down, "head", [(i, i - 1) for i in range(size - step, size)])
    return block_of(here).astype(f32) + up.astype(f32) + down.astype(f32)


def axis_sum(value, axis):
    for bit in axis_bits(axis):
        value = value + swapped(value, axis, bit)
    return value


def scan_before(local, states, reverse):
    here = lax.axis_index("seq")
    state_row = (jnp.arange(local.shape[1]) < states).astype(f32)[None, :, None]
    total = local.astype(f32)
    ahead = jnp.broadcast_to(1.0 - state_row, local.shape)
    bits = axis_bits("seq")
    sent = local
    for bit in bits:
        got = swapped(sent, "seq", bit).astype(f32)
        later = ((here & bit) == 0) if reverse else ((here & bit) != 0)
        ahead = jnp.where(later, ahead[:, states : states + 1] * got + state_row * ahead, ahead)
        if bit != bits[-1]:
            total = jnp.where(
                later,
                total[:, states : states + 1] * got + state_row * total,
                got[:, states : states + 1] * total + state_row * got,
            )
            sent = total.astype(bf16)
    return ahead.astype(bf16)


def passed_along(value, axis, steps):
    count = lax.axis_size(axis)
    initial, last = (max(0, -steps), min(count, count - steps))
    return lax.ppermute(value, axis, [(source, source + steps) for source in range(initial, last)])


def dot(left, right, precision=None):
    return jnp.dot(left, right, preferred_element_type=f32, precision=precision)


def dot_nt(left, right, precision=None):
    return lax.dot_general(
        left, right, (((1,), (1,)), ((), ())), preferred_element_type=f32, precision=precision
    )


def dot_tn(left, right, precision=None):
    return lax.dot_general(
        left, right, (((0,), (0,)), ((), ())), preferred_element_type=f32, precision=precision
    )


def both_parts(values):
    high = values.astype(bf16)
    return jnp.concatenate([high, (values - high.astype(f32)).astype(bf16)], axis=1)


def silu_slope(values):
    logistic = jax.nn.sigmoid(values)
    return logistic * (1.0 + values * (1.0 - logistic))


def call(kernel, grid, scalars, ins, outs, scratch=(), flops=0, bytes_accessed=0):
    return pl.pallas_call(
        kernel,
        grid_spec=pltpu.PrefetchScalarGridSpec(
            num_scalar_prefetch=len(scalars),
            grid=grid,
            in_specs=[pl.BlockSpec(block, index) for _, block, index in ins],
            out_specs=[pl.BlockSpec(block, index) for _, _, block, index in outs],
            scratch_shapes=list(scratch),
        ),
        out_shape=[jax.ShapeDtypeStruct(shape, dtype) for shape, dtype, _, _ in outs],
        compiler_params=pltpu.CompilerParams(vmem_limit_bytes=VMEM_BYTES),
        cost_estimate=pl.CostEstimate(
            flops=int(flops), bytes_accessed=int(bytes_accessed), transcendentals=0
        ),
    )(*scalars, *[array for array, _, _ in ins])


def per_row(array, rows):
    return (array, (rows,) + array.shape[1:], lambda m, *_: (m,) + (0,) * (array.ndim - 1))


def per_step(array):
    return (array, (1,) + array.shape[1:], lambda m, *_: (m,) + (0,) * (array.ndim - 1))


def entire(array):
    return (array, array.shape, lambda *_: (0,) * array.ndim)


def row_out(total, rows, width, dtype):
    return ((total, width), dtype, (rows, width), lambda m, *_: (m, 0))


def step_out(count, shape, dtype):
    return ((count,) + shape, dtype, (1,) + shape, lambda m, *_: (m,) + (0,) * len(shape))


def sum_out(shape, dtype=f32):
    return (shape, dtype, shape, lambda *_: (0,) * len(shape))


def segment_of(position, plan, place, m):
    found = jnp.full(jnp.shape(position), -1, jnp.int32)
    for k in range(plan.shape[1]):
        found = found + (position >= plan[m, k]).astype(jnp.int32)
    return jnp.where(position >= place[3], -2, found)


def column_position(rows, place, shift=0):
    return place[2] + shift + lax.broadcasted_iota(jnp.int32, (rows, 1), 0)


def row_position(rows, place):
    return place[2] + lax.broadcasted_iota(jnp.int32, (1, rows), 1)


def by_core(values, me, depth):
    count = values.shape[1] // depth
    blocks = [values[:, k * depth : (k + 1) * depth] for k in range(count)]
    odd = (me & 1) != 0
    halves = []
    for at in (0, 1):
        straight, turned = blocks[at::2], blocks[1 - at :: 2]
        half = [jnp.where(odd, b, a) for a, b in zip(straight, turned)]
        bit = 1
        while bit < count // 2:
            flip = ((me >> 1) & bit) != 0
            half = [jnp.where(flip, half[k ^ bit], half[k]) for k in range(len(half))]
            bit *= 2
        halves.append(half[0] if len(half) == 1 else jnp.concatenate(half, axis=1))
    return halves


def from_core(first, second, me, depth):
    count = 2 * first.shape[1] // depth
    odd = (me & 1) != 0
    halves = []
    for values in (first, second):
        half = [values[:, k * depth : (k + 1) * depth] for k in range(count // 2)]
        bit = 1
        while bit < count // 2:
            flip = ((me >> 1) & bit) != 0
            half = [jnp.where(flip, half[k ^ bit], half[k]) for k in range(len(half))]
            bit *= 2
        halves.append(half)
    blocks = []
    for k in range(count // 2):
        blocks.append(jnp.where(odd, halves[1][k], halves[0][k]))
        blocks.append(jnp.where(odd, halves[0][k], halves[1][k]))
    return jnp.concatenate(blocks, axis=1)


def half_start(quarter, me, width, depth):
    count = width // depth // 2
    return pl.multiple_of(((quarter * count) ^ ((me >> 1) & ~(count - 1))) * depth, width // 2)


def features_kernel(norm, size, depth, place, *refs):
    own, ups, downs = refs[0], refs[1:size], refs[size : 2 * size - 1]
    refs = refs[2 * size - 1 :]
    if norm:
        gain, even, odd, even_t, odd_t, inverse = refs
    else:
        even, odd, even_t, odd_t = refs
    z, me = place[0], place[1]
    width = own.shape[1]
    slots = [own[...].astype(f32)]
    for step in range(1, size):
        up, down = ups[step - 1][...].astype(f32), downs[size - step - 1][...].astype(f32)
        slots.append(jnp.where(z >= step, up, down))
    if norm:
        square = sum(jnp.sum(slot * slot, axis=1, keepdims=True) for slot in slots)
        inv = lax.rsqrt(square / (width * size) + epsilon)
        inverse[...] = inv
    for step, slot in enumerate(slots):
        quarter = lax.rem(z - step + size, size)
        if norm:
            start = pl.multiple_of(quarter * width, width)
            slot = slot * inv * gain[:, pl.ds(start, width)]
        first, second = by_core(slot, me, depth)
        at = pl.ds(half_start(quarter, me, width, depth), width // 2)
        even[:, at] = first.astype(bf16)
        odd[:, at] = second.astype(bf16)
        even_t[at, :] = first.T.astype(bf16)
        odd_t[at, :] = second.T.astype(bf16)


def all_features(own, place, gain, rows, depth):
    total, width = own.shape
    size = lax.axis_size("head")
    ups, downs = line_gather(own)
    half = width * size // 2
    ins = [per_row(array, rows) for array in [own] + ups + downs]
    outs = [row_out(total, rows, half, bf16)] * 2
    outs += [((half, total), bf16, (half, rows), lambda m, *_: (0, m))] * 2
    if gain is not None:
        ins.append(entire(gain))
        outs.append(row_out(total, rows, 1, f32))
    kernel = functools.partial(features_kernel, gain is not None, size, depth)
    return call(
        kernel, (total // rows,), (place,), ins, outs, bytes_accessed=total * width * 2 * 11
    )


def project_kernel(outs_of, even, odd, *refs):
    count = 2 * sum(len(group) for group in outs_of)
    weights, outs = refs[:count], refs[count:]
    at = 0
    for out, group in zip(outs, outs_of):
        start = 0
        for _ in group:
            first, second = weights[at], weights[at + 1]
            width = first.shape[1]
            out[:, start : start + width] = dot(even[...], first[...]) + dot(odd[...], second[...])
            start += width
            at += 2


def project(even, odd, groups, rows):
    total = even.shape[0]
    ins = [per_row(even, rows), per_row(odd, rows)]
    outs, moved, flops = [], 0, 0
    for group in groups:
        width = 0
        for first, second in group:
            ins += [entire(first), entire(second)]
            width += first.shape[1]
        outs.append(row_out(total, rows, width, f32))
        moved += width * (2 * even.shape[1] * 2 + total * 4)
        flops += 4 * total * even.shape[1] * width
    kernel = functools.partial(project_kernel, [len(group) * [0] for group in groups])
    return call(kernel, (total // rows,), (), ins, outs, flops=flops, bytes_accessed=moved)


def conv_kernel(
    width, heads, place, plan, first_pre, second_pre, first_halo, second_halo, taps, bias, step_bias,
    scale, spread, conv_out, small, inputs, maps, fresh, extended, padded,
):
    m = pl.program_id(0)
    rows = first_pre.shape[0]
    states = maps.shape[1] // 2
    half = width // 2
    taps_total = taps.shape[0]
    here = segment_of(column_position(rows, place), plan, place, m)
    same = [
        (segment_of(column_position(rows, place, tap + 1 - taps_total), plan, place, m) == here).astype(f32)
        for tap in range(taps_total)
    ]
    before = segment_of(place[2] - 1, plan, place, m)
    last = segment_of(place[2] + rows - 1, plan, place, m)

    padded[...] = jnp.zeros_like(padded)
    padded[:, :heads] = second_pre[:, half + states :]
    pre = padded[...] + step_bias[...]
    rest = jnp.exp(-jnp.abs(pre))
    series = rest * (
        1.0 - rest * (1 / 2 - rest * (1 / 3 - rest * (1 / 4 - rest * (1 / 5 - rest * (1 / 6)))))
    )
    step = jnp.maximum(pre, 0.0) + jnp.where(rest < 0.03, series, jnp.log(1.0 + rest))
    row = lax.broadcasted_iota(jnp.int32, (rows, rows), 0)
    col = lax.broadcasted_iota(jnp.int32, (rows, rows), 1)
    lower = (row >= col).astype(f32)
    cumulative = dot(lower, step * scale[...], highest)
    small[:, :LANES] = cumulative
    small[:, LANES : 2 * LANES] = step
    small[:, 2 * LANES :] = pre
    ending = cumulative[rows - 1 :, :]
    fading = (here == last).astype(f32) * jnp.exp(ending - cumulative)
    through = (last == before).astype(f32) * jnp.exp(ending)
    step_parts, fading_parts = both_parts(step), both_parts(fading)
    through_parts = both_parts(jnp.broadcast_to(through, (STATE_PAD, LANES)))

    def conv(source, halo, at, out_at):
        tile = slice(at, at + LANES)
        extended[:HALO, :] = halo[0, :, tile]
        extended[HALO:, :] = source[:, tile]
        out_tile = slice(out_at, out_at + LANES)
        result = jnp.broadcast_to(bias[:, out_tile], (rows, LANES))
        for tap in range(taps_total):
            start = HALO + tap + 1 - taps_total
            result = result + taps[tap : tap + 1, out_tile] * extended[start : start + rows, :] * same[tap]
        conv_out[:, out_tile] = result
        return result * jax.nn.sigmoid(result)

    for at in range(0, states, LANES):
        maps[:, at : at + LANES] = conv(first_pre, first_halo, half + at, half + at)
        maps[:, states + at : states + at + LANES] = conv(
            second_pre, second_halo, half + at, width + states + at
        )
    input_map = maps[:, :states].astype(bf16)
    for at in range(0, width, LANES):
        if at < half:
            heads_x = conv(first_pre, first_halo, at, at)
        else:
            heads_x = conv(second_pre, second_halo, at - half, at + states)
        tile = slice(at, at + LANES)
        values = heads_x * dot(step_parts, spread[:, tile])
        inputs[:, tile] = values.astype(bf16)
        faded = (values * dot(fading_parts, spread[:, tile])).astype(bf16)
        fresh[0, :states, tile] = dot_tn(input_map, faded).astype(bf16)
        fresh[0, states:, tile] = dot(through_parts, spread[:, tile]).astype(bf16)


def allowed_mask(rows, place, plan, m, transposed):
    column = segment_of(column_position(rows, place), plan, place, m)
    across = segment_of(row_position(rows, place), plan, place, m)
    row = lax.broadcasted_iota(jnp.int32, (rows, rows), 0)
    col = lax.broadcasted_iota(jnp.int32, (rows, rows), 1)
    order = (row <= col) if transposed else (row >= col)
    return jnp.where(order & (column == across), 0.0, -1e30)


def lane_select(parts, per):
    lane = lax.broadcasted_iota(jnp.int32, parts[0].shape, 1)
    result = parts[0]
    for at in range(1, per):
        result = jnp.where(lane >= at * (LANES // per), parts[at], result)
    return result


def mix_kernel(per, place, plan, small, maps, inputs, out):
    m = pl.program_id(0)
    rows, width = inputs.shape
    states = maps.shape[1] // 2
    cumulative = small[:, :LANES]
    flat = cumulative.T
    mask = allowed_mask(rows, place, plan, m, False)
    scores = dot_nt(maps[:, states:], maps[:, :states], highest)
    for at in range(0, width, LANES):
        tile = slice(at, at + LANES)
        for low in range(0, rows, LANES):
            end = low + LANES
            parts = []
            for sub in range(per):
                head = at // LANES * per + sub
                decay = jnp.exp(
                    (cumulative[low:end, head : head + 1] - flat[head : head + 1, :end])
                    + mask[low:end, :end]
                )
                mixing = (decay * scores[low:end, :end]).astype(bf16)
                parts.append(dot(mixing, inputs[:end, tile]))
            out[low:end, tile] = lane_select(parts, per)


def unmix_kernel(per, place, plan, small, maps, inputs, grads, grad_inputs, grad_maps, total):
    m = pl.program_id(0)
    rows, width = inputs.shape
    states = maps.shape[1] // 2
    cumulative = small[:, :LANES]
    flat = cumulative.T
    mask = allowed_mask(rows, place, plan, m, True)
    scores = dot_nt(maps[:, :states], maps[:, states:], highest)
    lane = lax.broadcasted_iota(jnp.int32, (LANES, LANES), 1)
    total[...] = jnp.zeros_like(total)
    for at in range(0, width, LANES):
        tile = slice(at, at + LANES)
        for low in range(0, rows, LANES):
            end = low + LANES
            later = grads[low:, tile]
            parts = []
            gathered_sum = total[low:end, low:]
            for sub in range(per):
                head = at // LANES * per + sub
                decay = jnp.exp(
                    (flat[head : head + 1, low:] - cumulative[low:end, head : head + 1])
                    + mask[low:end, low:]
                )
                mixing = (decay * scores[low:end, low:]).astype(bf16)
                parts.append(dot(mixing, later))
                inside = (lane // (LANES // per)) == sub
                own = jnp.where(inside, inputs[low:end, tile].astype(f32), 0.0).astype(bf16)
                gathered_sum = gathered_sum + decay * dot_nt(own, later)
            total[low:end, low:] = gathered_sum
            grad_inputs[low:end, tile] = lane_select(parts, per)
    grad_scores = total[...].astype(bf16)
    grad_maps[:, :states] = dot(grad_scores, maps[:, states:].astype(bf16))
    grad_maps[:, states:] = dot_tn(grad_scores, maps[:, :states].astype(bf16))


def inner_tile(ref, at, states):
    half = (ref.shape[1] - 2 * states) // 2
    start = at if at < half else at + states
    return ref[:, start : start + LANES]


def inflow_of(cumulative, rows, place, plan, m):
    here = segment_of(column_position(rows, place), plan, place, m)
    before = segment_of(place[2] - 1, plan, place, m)
    return (here == before).astype(f32) * jnp.exp(cumulative)


def gated_kernel(
    place, plan, small, maps, mixed, entering, conv_out, gate, grad_y, gain, skip, spread, scanned, sums
):
    m = pl.program_id(0)
    rows, width = mixed.shape
    states = maps.shape[1] // 2
    inflow = both_parts(inflow_of(small[:, :LANES], rows, place, plan, m))
    output_map = maps[:, states:].astype(bf16)
    square = jnp.zeros((rows, LANES), f32)
    product = jnp.zeros((rows, LANES), f32)
    for at in range(0, width, LANES):
        tile = slice(at, at + LANES)
        carried = dot(output_map, entering[0, :states, tile]) * dot(inflow, spread[:, tile])
        scan = mixed[:, tile] + carried
        scanned[:, tile] = scan
        conv = inner_tile(conv_out, at, states)
        gates = gate[:, tile]
        gated = (scan + skip[:, tile] * (conv * jax.nn.sigmoid(conv))) * (gates * jax.nn.sigmoid(gates))
        square = square + gated * gated
        product = product + grad_y[:, tile] * gain[:, tile] * gated
    ones = jnp.ones((HALO, LANES), f32)
    pick = lax.broadcasted_iota(jnp.int32, (HALO, rows), 0)
    sums[0] = jnp.where(pick == 0, dot_nt(ones, square, highest), dot_nt(ones, product, highest))


def ungated_kernel(
    inner_all, place, plan, small, maps, scanned, conv_out, gate, grad_y, sums, gain, skip, spread,
    normed_y, grads, grad_gate, local, grad_gain, grad_skip,
):
    m = pl.program_id(0)
    rows, width = scanned.shape
    states = maps.shape[1] // 2
    row = lax.broadcasted_iota(jnp.int32, (rows, rows), 0)
    col = lax.broadcasted_iota(jnp.int32, (rows, rows), 1)
    columns = dot_nt((row == col).astype(f32), sums[0], highest)
    inv = lax.rsqrt(columns[:, :1] / inner_all + epsilon)
    pull = inv * inv * inv * (columns[:, 1:2] / inner_all)
    cumulative = small[:, :LANES]
    inflow = both_parts(inflow_of(cumulative, rows, place, plan, m))
    before = segment_of(place[2] - 1, plan, place, m)
    last = segment_of(place[2] + rows - 1, plan, place, m)
    through = (last == before).astype(f32) * jnp.exp(cumulative[rows - 1 :, :])
    through_parts = both_parts(jnp.broadcast_to(through, (STATE_PAD, LANES)))
    output_map = maps[:, states:].astype(bf16)

    @pl.when(m == 0)
    def _():
        grad_gain[...] = jnp.zeros_like(grad_gain)
        grad_skip[...] = jnp.zeros_like(grad_skip)

    for at in range(0, width, LANES):
        tile = slice(at, at + LANES)
        conv = inner_tile(conv_out, at, states)
        heads_x = conv * jax.nn.sigmoid(conv)
        mixer = scanned[:, tile] + skip[:, tile] * heads_x
        gates = gate[:, tile]
        logistic = jax.nn.sigmoid(gates)
        act = gates * logistic
        gated = mixer * act
        normed = gated * inv
        normed_y[:, tile] = (normed * gain[:, tile]).astype(bf16)
        grad = grad_y[:, tile]
        grad_gain[:, tile] += jnp.sum(grad * normed, axis=0, keepdims=True)
        grad_gated = inv * (grad * gain[:, tile]) - gated * pull
        grad_mixer = grad_gated * act
        grads[:, tile] = grad_mixer.astype(bf16)
        grad_skip[:, tile] += jnp.sum(grad_mixer * heads_x, axis=0, keepdims=True)
        grad_gate[:, tile] = (
            grad_gated * mixer * (logistic * (1.0 + gates * (1.0 - logistic)))
        ).astype(bf16)
        weighted = (grad_mixer * dot(inflow, spread[:, tile])).astype(bf16)
        local[0, :states, tile] = dot_tn(output_map, weighted).astype(bf16)
        local[0, states:, tile] = dot(through_parts, spread[:, tile]).astype(bf16)


def unscan_kernel(
    place, plan, small, maps, scanned, conv_out, inputs, grads, grad_inputs, grad_maps, entering, leaving,
    skip, scale, spread, grad_conv_out, grad_step, grad_bias, grad_heads,
):
    m = pl.program_id(0)
    rows, width = scanned.shape
    states = maps.shape[1] // 2
    half = width // 2
    cumulative, step, pre = (small[:, k * LANES : (k + 1) * LANES] for k in range(3))
    here = segment_of(column_position(rows, place), plan, place, m)
    before = segment_of(place[2] - 1, plan, place, m)
    last = segment_of(place[2] + rows - 1, plan, place, m)
    ending = cumulative[rows - 1 :, :]
    fading = both_parts((here == last).astype(f32) * jnp.exp(ending - cumulative))
    inflow = both_parts((here == before).astype(f32) * jnp.exp(cumulative))
    through = (last == before).astype(f32) * jnp.exp(ending)
    step_parts = both_parts(step)
    input_map = maps[:, :states].astype(bf16)

    @pl.when(m == 0)
    def _():
        grad_bias[...] = jnp.zeros_like(grad_bias)
        grad_heads[...] = jnp.zeros_like(grad_heads)

    grad_in, grad_out = grad_maps[:, :states], grad_maps[:, states:]
    grad_cum = jnp.zeros((rows, LANES), f32)
    grad_own = jnp.zeros((rows, LANES), f32)
    ends = jnp.zeros((HALO, LANES), f32)
    for at in range(0, width, LANES):
        tile = slice(at, at + LANES)
        spread_tile = spread[:, tile]
        leave, enter = leaving[0, :states, tile], entering[0, :states, tile]
        fade = dot(fading, spread_tile)
        pulled = fade * dot(input_map, leave)
        values = inputs[:, tile].astype(f32)
        grad = grads[:, tile].astype(f32)
        total = grad_inputs[:, tile] + pulled
        faded = (values * fade).astype(bf16)
        weighted = (grad * dot(inflow, spread_tile)).astype(bf16)
        grad_in = grad_in + dot_nt(faded, leave)
        grad_out = grad_out + dot_nt(weighted, enter)
        conv = inner_tile(conv_out, at, states)
        logistic = jax.nn.sigmoid(conv)
        heads_x = conv * logistic
        first = both_parts(grad * scanned[:, tile] - values * total)
        second = both_parts(total * heads_x)
        grad_cum = grad_cum + dot_nt(first[:, :LANES], spread[:LANES, tile]) + dot_nt(
            first[:, LANES:], spread[:LANES, tile]
        )
        grad_own = grad_own + dot_nt(second[:, :LANES], spread[:LANES, tile]) + dot_nt(
            second[:, LANES:], spread[:LANES, tile]
        )
        fade_sum = jnp.sum(values * pulled, axis=0, keepdims=True)
        through_sum = jnp.sum(leave.astype(f32) * enter.astype(f32), axis=0, keepdims=True)
        pick = lax.broadcasted_iota(jnp.int32, (HALO, LANES), 0)
        edge = both_parts(jnp.where(pick == 0, fade_sum, through_sum))
        ends = ends + dot_nt(edge[:, :LANES], spread[:LANES, tile]) + dot_nt(
            edge[:, LANES:], spread[:LANES, tile]
        )
        grad_x = total * dot(step_parts, spread_tile) + skip[:, tile] * grad
        start = at if at < half else at + states
        result = grad_x * (logistic * (1.0 + conv * (1.0 - logistic)))
        grad_conv_out[:, start : start + LANES] = result
        grad_bias[:, start : start + LANES] += jnp.sum(result, axis=0, keepdims=True)
    for values, start in ((grad_in, half), (grad_out, width + states)):
        conv = conv_out[:, start : start + states]
        result = values * silu_slope(conv)
        grad_conv_out[:, start : start + states] = result
        grad_bias[:, start : start + states] += jnp.sum(result, axis=0, keepdims=True)
    row = lax.broadcasted_iota(jnp.int32, (rows, rows), 0)
    col = lax.broadcasted_iota(jnp.int32, (rows, rows), 1)
    upper = (row <= col).astype(f32)
    grad_rate = dot(upper, grad_cum, highest) + (ends[:1] + through * ends[1:2])
    rate = step * scale[...]
    grad_pre = (grad_rate * scale[...] + grad_own) * jax.nn.sigmoid(pre)
    grad_step[...] = grad_pre
    grad_heads[0:1, :] += jnp.sum(grad_rate * rate, axis=0, keepdims=True)
    grad_heads[1:2, :] += jnp.sum(grad_pre, axis=0, keepdims=True)


def unconv_kernel(
    heads, place, plan, first_pre, second_pre, first_halo, second_halo, grad_out, after, grad_step, taps,
    first_grad, second_grad, grad_taps, extended, extended_grad,
):
    m = pl.program_id(0)
    rows = first_pre.shape[0]
    first_width = first_pre.shape[1]
    channels = grad_out.shape[1]
    taps_total = taps.shape[0]
    here = segment_of(column_position(rows, place), plan, place, m)
    behind, ahead = [], []
    for tap in range(taps_total):
        lag = taps_total - 1 - tap
        behind.append((segment_of(column_position(rows, place, -lag), plan, place, m) == here).astype(f32))
        ahead.append((segment_of(column_position(rows, place, lag), plan, place, m) == here).astype(f32))

    @pl.when(m == 0)
    def _():
        grad_taps[...] = jnp.zeros_like(grad_taps)

    for at in range(0, channels, LANES):
        tile = slice(at, at + LANES)
        if at < first_width:
            source, halo, target, start = first_pre, first_halo, first_grad, at
        else:
            source, halo, target, start = second_pre, second_halo, second_grad, at - first_width
        own = slice(start, start + LANES)
        extended[:HALO, :] = halo[0, :, own]
        extended[HALO:, :] = source[:, own]
        grad = grad_out[:, tile]
        extended_grad[:rows, :] = grad
        extended_grad[rows:, :] = after[0, :, tile]
        result = jnp.zeros((rows, LANES), f32)
        for tap in range(taps_total):
            lag = taps_total - 1 - tap
            result = result + taps[tap : tap + 1, tile] * extended_grad[lag : lag + rows, :] * ahead[tap]
            begin = HALO - lag
            product = grad * extended[begin : begin + rows, :] * behind[tap]
            grad_taps[tap : tap + 1, tile] += jnp.sum(product, axis=0, keepdims=True)
        target[:, own] = result.astype(bf16)
    second_grad[:, channels - first_width :] = grad_step[:, :heads].astype(bf16)


def spread_kernel(count, with_sums, size, depth, place, *refs):
    values, refs = refs[:count], refs[count:]
    even_w, odd_w, refs = refs[:count], refs[count : 2 * count], refs[2 * count :]
    if with_sums:
        even, odd, out, sums, even_s, odd_s = refs
    else:
        out, even_s, odd_s = refs
    z, me = place[0], place[1]
    even_s[...] = sum(dot_nt(v[...], w[...]) for v, w in zip(values, even_w))
    odd_s[...] = sum(dot_nt(v[...], w[...]) for v, w in zip(values, odd_w))
    rows, half = even_s.shape
    if with_sums:
        product = jnp.zeros((rows, LANES), f32)
        for scratch, normed in ((even_s, even), (odd_s, odd)):
            for at in range(0, half, LANES):
                product = product + scratch[:, at : at + LANES] * normed[:, at : at + LANES].astype(f32)
        sums[0] = dot_nt(jnp.ones((HALO, LANES), f32), product, highest)
    width = 2 * half // size
    for quarter in range(size):
        at = pl.ds(half_start(quarter, me, width, depth), width // 2)
        out[quarter] = from_core(even_s[:, at], odd_s[:, at], me, depth).astype(bf16)


def spread_features(values, even_w, odd_w, place, rows, depth, normed=None):
    total = values[0].shape[0]
    size = lax.axis_size("head")
    half = even_w[0].shape[0]
    width = 2 * half // size
    ins = [per_row(v, rows) for v in values] + [entire(w) for w in even_w + odd_w]
    outs = [((size, total, width), bf16, (size, rows, width), lambda m, *_: (0, m, 0))]
    if normed is not None:
        ins += [per_row(array, rows) for array in normed]
        outs.append(step_out(total // rows, (HALO, rows), f32))
    kernel = functools.partial(spread_kernel, len(values), normed is not None, size, depth)
    inner = sum(v.shape[1] for v in values)
    return call(
        kernel, (total // rows,), (place,), ins, outs,
        scratch=[pltpu.VMEM((rows, half), f32)] * 2,
        flops=4 * total * inner * half,
        bytes_accessed=inner * half * 4 + total * half * 4 + total * inner * 2,
    )


def weight_kernel(count, keep_and_send, *refs):
    left, rights, refs = refs[0], refs[1 : 1 + count], refs[1 + count :]
    if not keep_and_send:
        for right, out in zip(rights, refs):
            out[...] = dot(left[...], right[...]).astype(bf16)
        return
    others, refs = refs[:count], refs[count:]
    step = pl.program_id(0)
    blocks = pl.num_programs(0)
    for at, (right, other) in enumerate(zip(rights, others)):
        keep, send = refs[2 * at], refs[2 * at + 1]
        result = (dot(left[...], right[...]) + other[...].astype(f32)).astype(bf16)
        sending = (step >= blocks // 2) if at % 2 == 0 else (lax.rem(step, 2) == 1)

        @pl.when(sending)
        def _():
            send[...] = result

        @pl.when(jnp.logical_not(sending))
        def _():
            keep[...] = result


def weight_gradient(even_t, odd_t, halves, depth):
    blocks = even_t.shape[0] // depth
    total = even_t.shape[1]
    left = lambda array: (array, (depth, total), lambda l: (l, 0))
    flops = 2 * even_t.shape[0] * total * sum(h.shape[1] for h in halves)
    moved = even_t.shape[0] * (total + sum(h.shape[1] for h in halves)) * 2
    sent = call(
        functools.partial(weight_kernel, 2, False), (blocks,), (),
        [left(odd_t)] + [entire(h) for h in halves],
        [((even_t.shape[0], h.shape[1]), bf16, (depth, h.shape[1]), lambda l: (l, 0)) for h in halves],
        flops=flops, bytes_accessed=moved,
    )
    got = [swapped(value, "seq", 1) for value in sent]
    outs = []
    top = blocks // 2
    for at, h in enumerate(halves):
        shape = (even_t.shape[0] // 2, h.shape[1])
        block = (depth, h.shape[1])
        if at == 0:
            outs.append((shape, bf16, block, lambda l: (jnp.minimum(l, top - 1), 0)))
            outs.append((shape, bf16, block, lambda l: (jnp.maximum(l - top, 0), 0)))
        else:
            outs.append((shape, bf16, block, lambda l: (l // 2, 0)))
            outs.append((shape, bf16, block, lambda l: (l // 2, 0)))
    mine = call(
        functools.partial(weight_kernel, 2, True), (blocks,), (),
        [left(even_t)] + [entire(h) for h in halves]
        + [(g, (depth, g.shape[1]), lambda l: (l, 0)) for g in got],
        outs, flops=flops, bytes_accessed=moved,
    )
    links = axis_bits("seq")[1:]
    labels = [bit << 1 for bit in range(blocks)]
    first = scattered(mine[0], mine[1], [x for x in labels if not x & links[-1]], links[::-1])
    second = scattered(mine[2], mine[3], [x for x in labels if not x & links[0]], links)
    return first, second


def per_device(
    tokens,
    cotangent,
    lengths,
    deal_order,
    norm_gain,
    proj_gate,
    proj_inner,
    proj_state,
    proj_step,
    conv_inner,
    conv_inner_bias,
    conv_state,
    conv_state_bias,
    step_bias,
    decay_log,
    skip_gain,
    inner_gain,
    proj_out,
):
    batch_count = lengths.shape[0]
    rows_local, width_own = tokens.shape
    tok_dev = rows_local // batch_count
    seq_index = lax.axis_index("seq")
    head_index = lax.axis_index("head")
    seq_size = lax.axis_size("seq")
    head_size = lax.axis_size("head")
    heads_own = proj_step.shape[1]
    inner_own = proj_inner.shape[1]
    head_width = inner_own // heads_own
    states = proj_state.shape[1] // 2
    taps_total = conv_inner.shape[0]
    width_all = width_own * head_size
    inner_all = inner_own * head_size
    depth = width_all // seq_size
    per_quarter = seq_size // head_size
    half = inner_own // 2
    channels = inner_own + 2 * states
    per = LANES // head_width
    rows = tok_dev
    grid = (batch_count,)

    place = jnp.stack(
        [head_index, seq_index, seq_index * tok_dev, jnp.int32(tok_dev * seq_size)]
    ).astype(jnp.int32)
    plan = (jnp.cumsum(lengths, axis=1) - lengths).astype(jnp.int32)
    scalars = (place, plan)

    slot_order = deal_order.reshape(batch_count, tok_dev)
    picks = (slot_order[:, :, None] == jnp.arange(tok_dev)[None, None, :]).astype(bf16)

    def dealt(values):
        values = jnp.einsum(
            "mij,mjf->mif", picks, values.reshape(batch_count, tok_dev, width_own),
            preferred_element_type=f32,
        ).astype(bf16)
        values = lax.all_to_all(values, "seq", split_axis=1, concat_axis=1, tiled=True)
        return values.reshape(rows_local, width_own)

    def returned(values):
        values = values.reshape(batch_count, tok_dev, width_own)
        values = lax.all_to_all(values, "seq", split_axis=1, concat_axis=1, tiled=True)
        values = jnp.einsum("mij,mif->mjf", picks, values, preferred_element_type=f32)
        return values.astype(bf16).reshape(rows_local, width_own)

    flat_tokens = dealt(tokens)
    flat_cot = dealt(cotangent)

    main_even, main_odd = gather_weight(
        jnp.concatenate([proj_inner[:, :half], proj_state[:, :states]], axis=1),
        jnp.concatenate([proj_inner[:, half:], proj_state[:, states:], proj_step], axis=1),
    )
    gate_even, gate_odd = gather_weight(proj_gate[:, :half], proj_gate[:, half:])
    out_t = proj_out.T
    out_even, out_odd = gather_weight(out_t[:, :half], out_t[:, half:])

    even, odd, even_t, odd_t, inv_rms = all_features(
        flat_tokens, place, norm_gain[None, :], tok_dev, depth
    )
    cot_even, cot_odd, cot_even_t, cot_odd_t = all_features(flat_cot, place, None, tok_dev, depth)

    def in_order(inner, state):
        return jnp.concatenate(
            [inner[:, :half], state[:, :states], inner[:, half:], state[:, states:]], axis=1
        )

    taps = in_order(conv_inner, conv_state)
    bias = in_order(conv_inner_bias[None, :], conv_state_bias[None, :])
    pad = LANES - heads_own
    step_bias_row = jnp.pad(step_bias, (0, pad))[None, :]
    scale = jnp.pad(-jnp.exp(decay_log), (0, pad))[None, :]
    spread = (
        jnp.arange(2 * LANES)[:, None] % LANES == jnp.arange(inner_own)[None, :] // head_width
    ).astype(bf16)
    skip = jnp.repeat(skip_gain, head_width)[None, :]
    gain = inner_gain[None, :]

    first_pre, second_pre = project(
        even, odd, [[(main_even[0], main_odd[0])], [(main_even[1], main_odd[1])]], tok_dev
    )

    def halo_before(values):
        values = values.reshape(batch_count, tok_dev, -1)[:, tok_dev - HALO :]
        return passed_along(values, "seq", 1)

    first_halo, second_halo = halo_before(first_pre), halo_before(second_pre)
    (gate,) = project(
        even, odd, [[(gate_even[0], gate_odd[0]), (gate_even[1], gate_odd[1])]], tok_dev
    )
    pres = [per_row(first_pre, rows), per_row(second_pre, rows), per_step(first_halo), per_step(second_halo)]
    conv_out, small, inputs, maps, fresh = call(
        functools.partial(conv_kernel, inner_own, heads_own), grid, scalars,
        pres + [entire(a) for a in (taps, bias, step_bias_row, scale, spread)],
        [
            row_out(rows_local, rows, channels, f32),
            row_out(rows_local, rows, 3 * LANES, f32),
            row_out(rows_local, rows, inner_own, bf16),
            row_out(rows_local, rows, 2 * states, f32),
            step_out(batch_count, (states + STATE_PAD, inner_own), bf16),
        ],
        scratch=[pltpu.VMEM((rows + HALO, LANES), f32), pltpu.VMEM((rows, LANES), f32)],
        flops=rows_local * inner_own * 2000, bytes_accessed=rows_local * inner_own * 12,
    )
    entering = scan_before(fresh, states, False)
    scan_ins = [per_row(small, rows), per_row(maps, rows)]
    (mixed,) = call(
        functools.partial(mix_kernel, per), grid, scalars, scan_ins + [per_row(inputs, rows)],
        [row_out(rows_local, rows, inner_own, f32)],
        flops=rows_local * inner_own * 6000, bytes_accessed=rows_local * inner_own * 6,
    )
    (grad_y,) = project(
        cot_even, cot_odd, [[(out_even[0], out_odd[0]), (out_even[1], out_odd[1])]], tok_dev
    )
    vectors = [entire(gain), entire(skip), entire(spread)]
    scanned, sums = call(
        gated_kernel, grid, scalars,
        scan_ins
        + [per_row(mixed, rows), per_step(entering), per_row(conv_out, rows), per_row(gate, rows)]
        + [per_row(grad_y, rows)] + vectors,
        [row_out(rows_local, rows, inner_own, f32), step_out(batch_count, (HALO, rows), f32)],
        flops=rows_local * inner_own * 1500, bytes_accessed=rows_local * inner_own * 20,
    )
    sums = axis_sum(sums, "head")
    normed_y, grads, grad_gate, local, grad_gain, grad_skip = call(
        functools.partial(ungated_kernel, inner_all), grid, scalars,
        scan_ins
        + [per_row(array, rows) for array in (scanned, conv_out, gate, grad_y)]
        + [per_step(sums)] + vectors,
        [row_out(rows_local, rows, inner_own, bf16)] * 3
        + [step_out(batch_count, (states + STATE_PAD, inner_own), bf16)]
        + [sum_out((1, inner_own))] * 2,
        flops=rows_local * inner_own * 2000, bytes_accessed=rows_local * inner_own * 24,
    )
    leaving = scan_before(local, states, True)

    (out_blocks,) = spread_features(
        [normed_y[:, :half], normed_y[:, half:]], list(out_even), list(out_odd), place, tok_dev, depth
    )
    branch = line_scatter(out_blocks)
    out_back = returned((flat_tokens.astype(f32) + branch).astype(bf16))

    grad_out_parts = weight_gradient(cot_even_t, cot_odd_t, [normed_y[:, :half], normed_y[:, half:]], depth)
    grad_gate_halves = [grad_gate[:, :half], grad_gate[:, half:]]
    grad_gate_parts = weight_gradient(even_t, odd_t, grad_gate_halves, depth)
    grad_inputs, grad_maps = call(
        functools.partial(unmix_kernel, per), grid, scalars,
        scan_ins + [per_row(inputs, rows), per_row(grads, rows)],
        [row_out(rows_local, rows, inner_own, f32), row_out(rows_local, rows, 2 * states, f32)],
        scratch=[pltpu.VMEM((rows, rows), f32)],
        flops=rows_local * inner_own * 12000, bytes_accessed=rows_local * inner_own * 8,
    )
    grad_conv_out, grad_step, grad_bias, grad_heads = call(
        unscan_kernel, grid, scalars,
        scan_ins
        + [per_row(a, rows) for a in (scanned, conv_out, inputs, grads, grad_inputs, grad_maps)]
        + [per_step(entering), per_step(leaving), entire(skip), entire(scale), entire(spread)],
        [
            row_out(rows_local, rows, channels, f32),
            row_out(rows_local, rows, LANES, f32),
            sum_out((1, channels)),
            sum_out((HALO, LANES)),
        ],
        flops=rows_local * inner_own * 4000, bytes_accessed=rows_local * inner_own * 28,
    )
    after = passed_along(grad_conv_out.reshape(batch_count, tok_dev, channels)[:, :HALO], "seq", -1)
    first_grad, second_grad, grad_taps = call(
        functools.partial(unconv_kernel, heads_own), grid, scalars,
        pres + [per_row(grad_conv_out, rows), per_step(after), per_row(grad_step, rows), entire(taps)],
        [
            row_out(rows_local, rows, first_pre.shape[1], bf16),
            row_out(rows_local, rows, second_pre.shape[1], bf16),
            sum_out((taps_total, channels)),
        ],
        scratch=[pltpu.VMEM((rows + HALO, LANES), f32)] * 2,
        flops=rows_local * inner_own * 100, bytes_accessed=rows_local * inner_own * 14,
    )
    grad_blocks, row_dots = spread_features(
        [first_grad, second_grad] + grad_gate_halves,
        list(main_even) + list(gate_even), list(main_odd) + list(gate_odd),
        place, tok_dev, depth, normed=(even, odd),
    )
    row_dots = axis_sum(row_dots, "head")[:, 0, :].reshape(rows_local, 1)
    rows_own = line_scatter(grad_blocks)
    unit_own = flat_tokens.astype(f32) * inv_rms
    gain_own = lax.dynamic_slice_in_dim(norm_gain, head_index * width_own, width_own, 0)
    grad_norm_gain = jnp.sum(rows_own * unit_own, axis=0)
    grad_rows_in = inv_rms * (rows_own * gain_own - unit_own * (row_dots / width_all))
    grad_back = returned((grad_rows_in + flat_cot.astype(f32)).astype(bf16))
    first_main, second_main = weight_gradient(even_t, odd_t, [first_grad, second_grad], depth)

    grad_w_state = axis_sum(
        jnp.concatenate([first_main[:, half:], second_main[:, half : half + states]], axis=1), "head"
    ).astype(bf16)
    mine = (seq_index // per_quarter) == head_index
    place_rows = (seq_index % per_quarter) * depth
    grad_w_state = lax.dynamic_update_slice_in_dim(
        jnp.zeros((width_own, 2 * states), bf16),
        jnp.where(mine, grad_w_state, jnp.zeros_like(grad_w_state)), place_rows, 0,
    )
    grad_w_state = axis_sum(grad_w_state, "seq").astype(f32)

    def fill(row):
        return jnp.pad(row, ((0, 0), (0, channels - row.shape[1])))

    packed = jnp.concatenate(
        [
            grad_taps,
            grad_bias,
            fill(grad_gain),
            fill(grad_skip),
            fill(jnp.concatenate([grad_heads[0:1], grad_heads[1:2], grad_norm_gain[None, :]], axis=1)),
        ]
    )
    packed = axis_sum(packed, "seq")

    def inner_of(values):
        return jnp.concatenate([values[:, :half], values[:, half + states : inner_own + states]], axis=1)

    state_sums = jnp.concatenate(
        [packed[: taps_total + 1, half : half + states], packed[: taps_total + 1, inner_own + states :]],
        axis=1,
    )
    state_sums = axis_sum(state_sums, "head")
    state_own = 2 * states // head_size
    state_sums = lax.dynamic_slice_in_dim(state_sums, head_index * state_own, state_own, 1)
    conv_sums = inner_of(packed[: taps_total + 1])
    return (
        out_back,
        grad_back,
        packed[taps_total + 3, 2 * LANES : 2 * LANES + width_own],
        jnp.concatenate(grad_gate_parts, axis=1),
        jnp.concatenate([first_main[:, :half], second_main[:, :half]], axis=1),
        grad_w_state,
        second_main[:, half + states :],
        conv_sums[:taps_total],
        conv_sums[taps_total],
        state_sums[:taps_total],
        state_sums[taps_total],
        packed[taps_total + 3, LANES : LANES + heads_own],
        packed[taps_total + 3, :heads_own],
        jnp.sum(packed[taps_total + 2, :inner_own].reshape(heads_own, head_width), axis=1),
        packed[taps_total + 1, :inner_own],
        jnp.concatenate(grad_out_parts, axis=1).T,
    )


def solution(mesh):
    return jax.shard_map(
        per_device,
        mesh=mesh,
        in_specs=(
            P("seq", "head"),
            P("seq", "head"),
            P(),
            P("seq"),
            P(),
            P("seq", "head"),
            P("seq", "head"),
            P("seq", None),
            P("seq", "head"),
            P(None, "head"),
            P("head"),
            P(),
            P(),
            P("head"),
            P("head"),
            P("head"),
            P("head"),
            P("head", "seq"),
        ),
        out_specs=(
            P("seq", "head"),
            P("seq", "head"),
            P("head"),
            P("seq", "head"),
            P("seq", "head"),
            P("head", None),
            P("seq", "head"),
            P(None, "head"),
            P("head"),
            P(None, "head"),
            P("head"),
            P("head"),
            P("head"),
            P("head"),
            P("head"),
            P("head", "seq"),
        ),
        check_vma=False,
    )
```

time: 871 us -> 659 us (0.76)
  Pallas kernels: 0 us -> 185 us
  matrix products: 173 us -> 4.63 us
  local copies, waits for them, and re-layouts: 210 us -> 71.2 us
  other arithmetic: 156 us -> 71.6 us
  starting transfers between devices: 158 us -> 145 us
  waiting for transfers between devices: 157 us -> 169 us
    pallas_call x0 -> x20, Pallas kernels: none -> 185 us  [call(): pl.pallas_call(kernel, grid_spec=pltpu.PrefetchScalarGridSpec(num_scalar_...]
    dot_general x28 -> x2, matrix products: 171 us -> 2.65 us  [returned(): jnp.einsum('mij,mif->mjf', picks, values, preferred_element_type=f32)]
    another operation x24 -> x2, local copies, waits for them, and re-layouts: 59.2 us -> 0.74 us  [the longest x1 0.67 us: per_device(): skip = jnp.repeat(skip_gain, head_width)[None, :]]
    reduce_sum x12 -> x2, other arithmetic: 31.7 us -> 4.14 us  [the longest x1 3.52 us: per_device(): grad_norm_gain = jnp.sum(rows_own * unit_own, axis=0)]
    rev x7 -> x0, local copies, waits for them, and re-layouts: 25.6 us -> none  [the longest x5 25.2 us: turn_quarter(): turned = jnp.where(seq_index & bit != 0, jnp.flip(halves, -3), halves)]
    another operation x20 -> x2, other arithmetic: 23.4 us -> 0.76 us  [the longest x1 0.59 us: per_device(): jnp.stack([head_index, seq_index, seq_index * tok_dev, jnp.int32(tok_dev...]
    slice x37 -> x46, local copies, waits for them, and re-layouts: 37.5 us -> 17.5 us  [the longest x1 2.62 us: per_device(): normed_y[:, half:]]
    unnamed x337 -> x152, local copies, waits for them, and re-layouts: 24.9 us -> 7.14 us
  transfers between devices with their start and end apart: 89 -> 87, of which waited for: 29 -> 28; matrix products, arithmetic and copies ran while one was open for 48% -> 21% of each run, Pallas kernels for 0% -> 25%
where the time goes in v2:
time: 659 us; the launch traced here: 649 us
  Pallas kernels  185 us (28%)
  waiting for transfers between devices  169 us (26%)
  starting transfers between devices  145 us (22%)
  other arithmetic  71.6 us (11%)
  local copies, waits for them, and re-layouts  71.2 us (11%)
    pallas_call x20, Pallas kernels, call(): pl.pallas_call(kernel, grid_spec=pltpu.PrefetchScalarGridSpec(num_scalar_...  185 us
    ppermute x56, waiting for transfers between devices, swapped(): lax.ppermute(value, axis, [(i, i ^ bit) for i in range(lax.axis_size(axis...  87.4 us
    ppermute x56, starting transfers between devices, swapped(): lax.ppermute(value, axis, [(i, i ^ bit) for i in range(lax.axis_size(axis...  66.9 us
    ppermute x6, waiting for transfers between devices, line_gather(): lax.ppermute(down, 'head', [(i, i - 1) for i in range(1, size - step + 1)])  30.2 us
    ppermute x6, starting transfers between devices, line_scatter(): up = lax.ppermute(give_up, 'head', [(i, i + 1) for i in range(step)])  24.2 us
    ppermute x6, waiting for transfers between devices, line_scatter(): up = lax.ppermute(give_up, 'head', [(i, i + 1) for i in range(step)])  20.8 us
    convert_element_type x12, other arithmetic, added(): return (left.astype(f32) + right.astype(f32)).astype(left.dtype)  19.5 us
    ppermute x6, starting transfers between devices, line_gather(): lax.ppermute(up, 'head', [(i, i + 1) for i in range(step - 1, size - 1)])  17.6 us
  transfers between devices with their start and end apart: 87, of which 28 were waited for; matrix products, arithmetic and copies ran while one was open for 21% of the time, Pallas kernels for 25%

profile of v2, /device:TPU:0, one launch (start us, length us, event | category | flops | bytes accessed | tf_op | source)
XLA Modules:
  0.0 648.6 jit_solution(8854462257321272715)
XLA Ops:
  21.9 9.3 %all-to-all-done = bf16[3,256,512]{2,0,1:T(4,128)(2,1)S(1)} async-done(((bf16[3,256,512]{2,0,1:T(4,128)(2,1)}), bf16[3,256,512]{2,0,1:T(4,128)(2,1)S(1)}, u32[]{:S(2)}, u32[]{:S(2)}) %all-to-all-start) | async-done | bytes 786464 | tf_op jit(solution)/shard_map/all_to_all | solution.py:842
  72.1 7.1 %collective-permute-done.4.refs_5_ = bf16[768,512]{1,0:T(8,128)(2,1)} collective-permute-done((bf16[768,512]{1,0:T(8,128)(2,1)}, bf16[768,512]{1,0:T(8,128)(2,1)}, u32[]{:S(2)}, u32[]{:S(2)}) %collective-permute-start.4) | collective-permute-done | bytes 786464 | tf_op jit(solution)/shard_map/ppermute | solution.py:71
  88.2 11.5 %collective-permute-done.5.refs_6_ = bf16[768,512]{1,0:T(8,128)(2,1)} collective-permute-done((bf16[768,512]{1,0:T(8,128)(2,1)}, bf16[768,512]{1,0:T(8,128)(2,1)}, u32[]{:S(2)}, u32[]{:S(2)}) %collective-permute-start.5) | collective-permute-done | bytes 786464 | tf_op jit(solution)/shard_map/ppermute | solution.py:71
  102.0 7.9 %shard_map.297 = (bf16[768,1024]{1,0:T(8,128)(2,1)}, bf16[768,1024]{1,0:T(8,128)(2,1)}, bf16[1024,768]{1,0:T(8,128)(2,1)}, bf16[1024,768]{1,0:T(8,128)(2,1)}, f32[768,1]{1,0:T(8,128)}) custom-call(s32[4]{0:T(128)} %pad_add_fusion.place, bf16[768,512]{1,0:T(8,128)(2,1)} %bitcast.170, bf16[768,512]{1,0:T(8,128)(2,1)} %collective-permute-done.refs_1_, ...), custom_call_target="tpu_custom_call" | custom-call | bytes 8650752 | tf_op jit(solution)/shard_map/pallas_call | solution.py:154
  110.0 9.4 %shard_map.298 = (f32[768,640]{1,0:T(8,128)}, f32[768,656]{1,0:T(8,128)}) custom-call(bf16[768,1024]{1,0:T(8,128)(2,1)} %get-tuple-element.69.even.refs_12_, bf16[768,1024]{1,0:T(8,128)(2,1)} %get-tuple-element.70.odd.refs_13_, bf16[1024,640]{1,0:T(8,128)(2,1)} %bitcast.7.refs_0_.refs_4_, bf16[1024,640]{1,0:T(8,128)(2,1)} %collective-permute-done.8.refs_1_.refs_8_, ...), custom_call_target="tpu_custom_call" | custom-call | flops 4076863488 | bytes 9289728 | tf_op jit(solution)/shard_map/pallas_call | solution.py:154
  129.4 13.2 %shard_map.299 = (f32[768,1280]{1,0:T(8,128)}, f32[768,384]{1,0:T(8,128)}, bf16[768,1024]{1,0:T(8,128)(2,1)}, f32[768,256]{1,0:T(8,128)}, bf16[3,144,1024]{2,1,0:T(8,128)(2,1)}) custom-call(s32[4]{0:T(128)} %pad_add_fusion.place, s32[3,4]{1,0:T(4,128)} %sub.55.plan, f32[768,640]{1,0:T(8,128)} %get-tuple-element.71.first_pre, ...), custom_call_target="tpu_custom_call" | custom-call | flops 1572864000 | bytes 9437184 | tf_op jit(solution)/shard_map/pallas_call | solution.py:154
  202.3 7.6 %shard_map.301.gate = f32[768,1024]{1,0:T(8,128)} custom-call(bf16[768,1024]{1,0:T(8,128)(2,1)} %get-tuple-element.69.even.refs_12_, bf16[768,1024]{1,0:T(8,128)(2,1)} %get-tuple-element.70.odd.refs_13_, bf16[1024,512]{1,0:T(8,128)(2,1)} %bitcast.18.refs_0_.refs_6_, bf16[1024,512]{1,0:T(8,128)(2,1)} %collective-permute-done.19.refs_1_.refs_10_, ...), custom_call_target="tpu_custom_call" | custom-call | flops 3221225472 | bytes 7340032 | tf_op jit(solution)/shard_map/pallas_call | solution.py:154
  212.5 7.2 %shard_map.302 = (bf16[768,1024]{1,0:T(8,128)(2,1)}, bf16[768,1024]{1,0:T(8,128)(2,1)}, bf16[1024,768]{1,0:T(8,128)(2,1)}, bf16[1024,768]{1,0:T(8,128)(2,1)}) custom-call(s32[4]{0:T(128)} %pad_add_fusion.place, bf16[768,512]{1,0:T(8,128)(2,1)} %bitcast.173, bf16[768,512]{1,0:T(8,128)(2,1)} %collective-permute-done.23.refs_1_, ...), custom_call_target="tpu_custom_call" | custom-call | bytes 8650752 | tf_op jit(solution)/shard_map/pallas_call | solution.py:154
  219.7 7.6 %shard_map.303.grad_y = f32[768,1024]{1,0:T(8,128)} custom-call(bf16[768,1024]{1,0:T(8,128)(2,1)} %get-tuple-element.78.even, bf16[768,1024]{1,0:T(8,128)(2,1)} %get-tuple-element.79.odd, bf16[1024,512]{1,0:T(8,128)(2,1)} %bitcast.186, bf16[1024,512]{1,0:T(8,128)(2,1)} %collective-permute-done.31.refs_1_.refs_4_, bf16[1024,512]{1,0:T(8,128)(2,1)} %bitcast.183, ...), custom_call_target="tpu_custom_call" | custom-call | flops 3221225472 | bytes 7340032 | tf_op jit(solution)/shard_map/pallas_call | solution.py:154
  227.3 7.4 %shard_map.300.mixed = f32[768,1024]{1,0:T(8,128)} custom-call(s32[4]{0:T(128)} %pad_add_fusion.place, s32[3,4]{1,0:T(4,128)} %sub.55.plan, f32[768,384]{1,0:T(8,128)} %get-tuple-element.73.small, f32[768,256]{1,0:T(8,128)} %get-tuple-element.74.maps, bf16[768,1024]{1,0:T(8,128)(2,1)} %get-tuple-element.75.inputs), custom_call_target="tpu_custom_call" | custom-call | flops 4718592000 | bytes 4718592 | tf_op jit(solution)/shard_map/pallas_call | solution.py:154
  236.1 10.1 %shard_map.304 = (f32[768,1024]{1,0:T(8,128)}, f32[3,8,256]{2,1,0:T(8,128)}) custom-call(s32[4]{0:T(128)} %pad_add_fusion.place, s32[3,4]{1,0:T(4,128)} %sub.55.plan, f32[768,384]{1,0:T(8,128)} %get-tuple-element.73.small, f32[768,256]{1,0:T(8,128)} %get-tuple-element.74.maps, f32[768,1024]{1,0:T(8,128)} %shard_map.300.mixed, ...), custom_call_target="tpu_custom_call" | custom-call | flops 1179648000 | bytes 15728640 | tf_op jit(solution)/shard_map/pallas_call | solution.py:154
  260.2 13.1 %shard_map.305 = (bf16[768,1024]{1,0:T(8,128)(2,1)}, bf16[768,1024]{1,0:T(8,128)(2,1)}, bf16[768,1024]{1,0:T(8,128)(2,1)}, bf16[3,144,1024]{2,1,0:T(8,128)(2,1)}, f32[1,1024]{1,0:T(1,128)}, /*index=5*/f32[1,1024]{1,0:T(1,128)}) custom-call(s32[4]{0:T(128)} %pad_add_fusion.place, s32[3,4]{1,0:T(4,128)} %sub.55.plan, f32[768,384]{1,0:T(8,128)} %get-tuple-element.73.small, ...), custom_call_target="tpu_custom_call" | custom-call | flops 1572864000 | bytes 18874368 | tf_op jit(solution)/shard_map/pallas_call | solution.py:154
  282.4 9.0 %shard_map.306 = bf16[4,768,512]{2,1,0:T(8,128)(2,1)} custom-call(s32[4]{0:T(128)} %pad_add_fusion.place, bf16[768,512]{1,0:T(8,128)(2,1)} %get-tuple-element.205.refs_0_.refs_1_, bf16[768,512]{1,0:T(8,128)(2,1)} %get-tuple-element.204.refs_1_.refs_2_, bf16[1024,512]{1,0:T(8,128)(2,1)} %bitcast.187, bf16[1024,512]{1,0:T(8,128)(2,1)} %bitcast.184, ...), custom_call_target="tpu_custom_call" | custom-call | flops 3221225472 | bytes 8912896 | tf_op jit(solution)/shard_map/pallas_call | solution.py:154
  305.5 9.4 %collective-permute-done.37 = bf16[768,512]{1,0:T(8,128)(2,1)S(1)} collective-permute-done((bf16[768,512]{1,0:T(8,128)(2,1)S(1)}, bf16[768,512]{1,0:T(8,128)(2,1)S(1)}, u32[]{:S(2)}, u32[]{:S(2)}) %collective-permute-start.37) | collective-permute-done | bytes 786464 | tf_op jit(solution)/shard_map/ppermute | solution.py:89
  316.0 9.8 %shard_map.307 = (f32[768,1024]{1,0:T(8,128)}, f32[768,256]{1,0:T(8,128)}) custom-call(s32[4]{0:T(128)} %pad_add_fusion.place, s32[3,4]{1,0:T(4,128)} %sub.55.plan, f32[768,384]{1,0:T(8,128)} %get-tuple-element.73.small, f32[768,256]{1,0:T(8,128)} %get-tuple-element.74.maps, bf16[768,1024]{1,0:T(8,128)(2,1)} %get-tuple-element.75.inputs, ...), custom_call_target="tpu_custom_call" | custom-call | flops 9437184000 | bytes 6291456 | tf_op jit(solution)/shard_map/pallas_call | solution.py:154
  369.1 16.7 %collective-permute-done.60 = bf16[2,256,512]{2,1,0:T(8,128)(2,1)S(1)} collective-permute-done((bf16[2,256,512]{2,1,0:T(8,128)(2,1)}, bf16[2,256,512]{2,1,0:T(8,128)(2,1)S(1)}, u32[]{:S(2)}, u32[]{:S(2)}) %collective-permute-start.60) | collective-permute-done | bytes 524320 | tf_op jit(solution)/shard_map/ppermute | solution.py:20
  391.4 15.8 %shard_map.308 = (f32[768,1280]{1,0:T(8,128)}, f32[768,128]{1,0:T(8,128)}, f32[1,1280]{1,0:T(1,128)}, f32[8,128]{1,0:T(8,128)}) custom-call(s32[4]{0:T(128)} %pad_add_fusion.place, s32[3,4]{1,0:T(4,128)} %sub.55.plan, f32[768,384]{1,0:T(8,128)} %get-tuple-element.73.small, f32[768,256]{1,0:T(8,128)} %get-tuple-element.74.maps, ...), custom_call_target="tpu_custom_call" | custom-call | flops 3145728000 | bytes 22020096 | tf_op jit(solution)/shard_map/pallas_call | solution.py:154
  412.0 11.1 %shard_map.309 = (bf16[768,640]{1,0:T(8,128)(2,1)}, bf16[768,656]{1,0:T(8,128)(2,1)}, f32[4,1280]{1,0:T(4,128)}) custom-call(s32[4]{0:T(128)} %pad_add_fusion.place, s32[3,4]{1,0:T(4,128)} %sub.55.plan, f32[768,640]{1,0:T(8,128)} %get-tuple-element.71.first_pre, f32[768,656]{1,0:T(8,128)} %get-tuple-element.72.second_pre, f32[3,8,640]{2,1,0:T(8,128)} %copy-done.48, ...), custom_call_target="tpu_custom_call" | custom-call | flops 78643200 | bytes 11010048 | tf_op jit(solution)/shard_map/pallas_call | solution.py:154
  434.0 17.3 %shard_map.310 = (bf16[4,768,512]{2,1,0:T(8,128)(2,1)}, f32[3,8,256]{2,1,0:T(8,128)}) custom-call(s32[4]{0:T(128)} %pad_add_fusion.place, bf16[768,640]{1,0:T(8,128)(2,1)} %get-tuple-element.90.refs_0_.refs_1_, bf16[768,656]{1,0:T(8,128)(2,1)} %get-tuple-element.91.refs_1_.refs_2_, bf16[768,512]{1,0:T(8,128)(2,1)} %get-tuple-element.203.refs_2_.refs_1_, ...), custom_call_target="tpu_custom_call" | custom-call | flops 7298088960 | bytes 16211968 | tf_op jit(solution)/shard_map/pallas_call | solution.py:154
  464.4 11.5 %collective-permute-done.47 = bf16[768,512]{1,0:T(8,128)(2,1)S(1)} collective-permute-done((bf16[768,512]{1,0:T(8,128)(2,1)S(1)}, bf16[768,512]{1,0:T(8,128)(2,1)S(1)}, u32[]{:S(2)}, u32[]{:S(2)}) %collective-permute-start.47) | collective-permute-done | bytes 786464 | tf_op jit(solution)/shard_map/ppermute | solution.py:89
  490.5 8.3 %shard_map.314 = (bf16[512,640]{1,0:T(8,128)(2,1)}, bf16[512,640]{1,0:T(8,128)(2,1)}, bf16[512,656]{1,0:T(8,128)(2,1)}, bf16[512,656]{1,0:T(8,128)(2,1)}) custom-call(bf16[1024,768]{1,0:T(8,128)(2,1)} %get-tuple-element.100.refs_0_, bf16[768,640]{1,0:T(8,128)(2,1)} %get-tuple-element.90.refs_0_.refs_1_, bf16[768,656]{1,0:T(8,128)(2,1)} %get-tuple-element.91.refs_1_.refs_2_, ...), custom_call_target="tpu_custom_call" | custom-call | flops 2038431744 | bytes 4227072 | tf_op jit(solution)/shard_map/pallas_call | solution.py:154
  547.0 9.1 %collective-permute-done.70 = f32[256,256]{0,1:T(8,128)S(1)} collective-permute-done((f32[256,256]{0,1:T(8,128)S(1)}, f32[256,256]{0,1:T(8,128)S(1)}, u32[]{:S(2)}, u32[]{:S(2)}) %collective-permute-start.70) | collective-permute-done | bytes 262176 | tf_op jit(solution)/shard_map/ppermute | solution.py:20
  564.1 24.7 %collective-permute-done.71 = f32[256,256]{0,1:T(8,128)} collective-permute-done((f32[256,256]{0,1:T(8,128)S(1)}, f32[256,256]{0,1:T(8,128)}, u32[]{:S(2)}, u32[]{:S(2)}) %collective-permute-start.71) | collective-permute-done | bytes 262176 | tf_op jit(solution)/shard_map/ppermute | solution.py:20
  635.2 11.7 %all-to-all-done.2 = bf16[3,256,512]{2,0,1:T(4,128)(2,1)S(1)} async-done(((bf16[3,256,512]{2,0,1:T(4,128)(2,1)}), bf16[3,256,512]{2,0,1:T(4,128)(2,1)S(1)}, u32[]{:S(2)}, u32[]{:S(2)}) %all-to-all-start.2) | async-done | bytes 786464 | tf_op jit(solution)/shard_map/all_to_all | solution.py:847
  (484 shorter events, 380.3 us)
Async XLA Ops:
  2.7 140.0 %collective-permute-start.20 = (bf16[1,256,512]{2,1,0:T(8,128)(2,1)}, bf16[1,256,512]{2,1,0:T(8,128)(2,1)}, u32[]{:S(2)}, u32[]{:S(2)}) collective-permute-start(bf16[1,256,512]{2,1,0:T(8,128)(2,1)} %get-tuple-element.221), channel_id=1, source_target_pairs={{0,16},{4,20},{8,24},{12,28},{16,0},{20,4},{24,8},{28,12},{1,17},{... | collective-permute-start | bytes 786440 | tf_op jit(solution)/shard_map/ppermute | solution.py:20
  31.2 95.3 %all-to-all-start.1 = ((bf16[3,256,512]{2,0,1:T(4,128)(2,1)}), bf16[3,256,512]{2,0,1:T(4,128)(2,1)S(1)}, u32[]{:S(2)}, u32[]{:S(2)}) async-start(bf16[3,256,512]{2,0,1:T(4,128)(2,1)} %copy.103), calls=%async_computation.1 | async-start | bytes 2097152 | tf_op jit(solution)/shard_map/all_to_all | solution.py:842
  53.1 56.8 %collective-permute-start.8 = (bf16[1024,640]{1,0:T(8,128)(2,1)}, bf16[1024,640]{1,0:T(8,128)(2,1)}, u32[]{:S(2)}, u32[]{:S(2)}) collective-permute-start(bf16[1024,640]{1,0:T(8,128)(2,1)} %bitcast.7.refs_0_.refs_4_), channel_id=1, source_target_pairs={{0,4},{4,0},{8,12},{12,8},{16,20},{20,16},{24,28},{28,24},{1,5},{5... | collective-permute-start | bytes 3932168 | tf_op jit(solution)/shard_map/ppermute | solution.py:20
  84.3 38.0 %collective-permute-start.17 = (bf16[1,256,512]{2,1,0:T(8,128)(2,1)S(1)}, bf16[1,256,512]{2,1,0:T(8,128)(2,1)S(1)}, u32[]{:S(2)}, u32[]{:S(2)}) collective-permute-start(bf16[1,256,512]{2,1,0:T(8,128)(2,1)S(1)} %copy-done.15), channel_id=1, source_target_pairs={{0,8},{4,12},{8,0},{12,4},{16,24},{20,28},{24,16},{28,20},{1,9},{5... | collective-permute-start | bytes 786440 | tf_op jit(solution)/shard_map/ppermute | solution.py:20
  99.7 44.9 %collective-permute-start.32 = (bf16[1,256,512]{1,2,0:T(8,128)(2,1)S(1)}, bf16[1,256,512]{1,2,0:T(8,128)(2,1)S(1)}, u32[]{:S(2)}, u32[]{:S(2)}) collective-permute-start(bf16[1,256,512]{1,2,0:T(8,128)(2,1)S(1)} %get-tuple-element.217), channel_id=1, source_target_pairs={{0,16},{4,20},{8,24},{12,28},{16,0},{20,4},{24,8},{28,12},{1,17},{... | collective-permute-start | bytes 786440 | tf_op jit(solution)/shard_map/ppermute | solution.py:20
  100.5 45.4 %collective-permute-start.29 = (bf16[1,256,512]{1,2,0:T(8,128)(2,1)S(1)}, bf16[1,256,512]{1,2,0:T(8,128)(2,1)S(1)}, u32[]{:S(2)}, u32[]{:S(2)}) collective-permute-start(bf16[1,256,512]{1,2,0:T(8,128)(2,1)S(1)} %get-tuple-element.218), channel_id=1, source_target_pairs={{0,8},{4,12},{8,0},{12,4},{16,24},{20,28},{24,16},{28,20},{1,9},{5... | collective-permute-start | bytes 786440 | tf_op jit(solution)/shard_map/ppermute | solution.py:20
  184.5 35.2 %collective-permute-start.31 = (bf16[1024,512]{1,0:T(8,128)(2,1)}, bf16[1024,512]{1,0:T(8,128)(2,1)}, u32[]{:S(2)}, u32[]{:S(2)}) collective-permute-start(bf16[1024,512]{1,0:T(8,128)(2,1)} %bitcast.185), channel_id=1, source_target_pairs={{0,4},{4,0},{8,12},{12,8},{16,20},{20,16},{24,28},{28,24},{1,5},{5... | collective-permute-start | bytes 3145736 | tf_op jit(solution)/shard_map/ppermute | solution.py:20
  281.9 46.8 %collective-permute-start.77 = (bf16[1024,512]{1,0:T(8,128)(2,1)}, bf16[1024,512]{1,0:T(8,128)(2,1)}, u32[]{:S(2)}, u32[]{:S(2)}) collective-permute-start(bf16[1024,512]{1,0:T(8,128)(2,1)} %get-tuple-element.116), channel_id=1, source_target_pairs={{0,4},{4,0},{8,12},{12,8},{16,20},{20,16},{24,28},{28,24},{1,5},{5... | collective-permute-start | bytes 3145736 | tf_op jit(solution)/shard_map/ppermute | solution.py:20
  282.4 47.9 %collective-permute-start.78 = (bf16[1024,512]{1,0:T(8,128)(2,1)}, bf16[1024,512]{1,0:T(8,128)(2,1)}, u32[]{:S(2)}, u32[]{:S(2)}) collective-permute-start(bf16[1024,512]{1,0:T(8,128)(2,1)} %get-tuple-element.117), channel_id=1, source_target_pairs={{0,4},{4,0},{8,12},{12,8},{16,20},{20,16},{24,28},{28,24},{1,5},{5... | collective-permute-start | bytes 3145736 | tf_op jit(solution)/shard_map/ppermute | solution.py:20
  304.1 43.9 %collective-permute-start.58 = (bf16[1024,512]{1,0:T(8,128)(2,1)}, bf16[1024,512]{1,0:T(8,128)(2,1)}, u32[]{:S(2)}, u32[]{:S(2)}) collective-permute-start(bf16[1024,512]{1,0:T(8,128)(2,1)} %get-tuple-element.102), channel_id=1, source_target_pairs={{0,4},{4,0},{8,12},{12,8},{16,20},{20,16},{24,28},{28,24},{1,5},{5... | collective-permute-start | bytes 3145736 | tf_op jit(solution)/shard_map/ppermute | solution.py:20
  304.3 48.9 %collective-permute-start.59 = (bf16[1024,512]{1,0:T(8,128)(2,1)}, bf16[1024,512]{1,0:T(8,128)(2,1)}, u32[]{:S(2)}, u32[]{:S(2)}) collective-permute-start(bf16[1024,512]{1,0:T(8,128)(2,1)} %get-tuple-element.103), channel_id=1, source_target_pairs={{0,4},{4,0},{8,12},{12,8},{16,20},{20,16},{24,28},{28,24},{1,5},{5... | collective-permute-start | bytes 3145736 | tf_op jit(solution)/shard_map/ppermute | solution.py:20
  328.7 125.1 %collective-permute-start.40 = (bf16[768,512]{1,0:T(8,128)(2,1)}, bf16[768,512]{1,0:T(8,128)(2,1)}, u32[]{:S(2)}, u32[]{:S(2)}) collective-permute-start(bf16[768,512]{1,0:T(8,128)(2,1)} %get-tuple-element.201), channel_id=1, source_target_pairs={{3,2},{7,6},{11,10},{15,14},{19,18},{23,22},{27,26},{31,30}} | collective-permute-start | bytes 2359304 | tf_op jit(solution)/shard_map/ppermute | solution.py:90
  348.0 105.9 %collective-permute-start.38 = (bf16[768,512]{1,0:T(8,128)(2,1)}, bf16[768,512]{1,0:T(8,128)(2,1)}, u32[]{:S(2)}, u32[]{:S(2)}) collective-permute-start(bf16[768,512]{1,0:T(8,128)(2,1)} %fusion.15), channel_id=1, source_target_pairs={{0,1},{1,2},{4,5},{5,6},{8,9},{9,10},{12,13},{13,14},{16,17},{17,1... | collective-permute-start | bytes 2359304 | tf_op jit(solution)/shard_map/ppermute | solution.py:89
  366.1 42.1 %collective-permute-start.62 = (bf16[2,256,512]{2,1,0:T(8,128)(2,1)S(1)}, bf16[2,256,512]{2,1,0:T(8,128)(2,1)S(1)}, u32[]{:S(2)}, u32[]{:S(2)}) collective-permute-start(bf16[2,256,512]{2,1,0:T(8,128)(2,1)S(1)} %bitcast.221), channel_id=1, source_target_pairs={{0,8},{4,12},{8,0},{12,4},{16,24},{20,28},{24,16},{28,20},{1,9},{5... | collective-permute-start | bytes 1572872 | tf_op jit(solution)/shard_map/ppermute | solution.py:20
  385.9 75.5 %collective-permute-start.80 = (bf16[1,256,512]{1,2,0:T(8,128)(2,1)S(1)}, bf16[1,256,512]{1,2,0:T(8,128)(2,1)}, u32[]{:S(2)}, u32[]{:S(2)}) collective-permute-start(bf16[1,256,512]{1,2,0:T(8,128)(2,1)S(1)} %slice.383), channel_id=1, source_target_pairs={{0,8},{4,12},{8,0},{12,4},{16,24},{20,28},{24,16},{28,20},{1,9},{5... | collective-permute-start | bytes 786440 | tf_op jit(solution)/shard_map/ppermute | solution.py:20
  387.2 76.1 %collective-permute-start.82 = (bf16[1,256,512]{1,2,0:T(8,128)(2,1)}, bf16[1,256,512]{1,2,0:T(8,128)(2,1)}, u32[]{:S(2)}, u32[]{:S(2)}) collective-permute-start(bf16[1,256,512]{1,2,0:T(8,128)(2,1)} %slice.385), channel_id=1, source_target_pairs={{0,16},{4,20},{8,24},{12,28},{16,0},{20,4},{24,8},{28,12},{1,17},{... | collective-permute-start | bytes 786440 | tf_op jit(solution)/shard_map/ppermute | solution.py:20
  431.7 54.0 %collective-permute-start.65 = (bf16[1024,656]{0,1:T(8,128)(2,1)}, bf16[1024,656]{0,1:T(8,128)(2,1)}, u32[]{:S(2)}, u32[]{:S(2)}) collective-permute-start(bf16[1024,656]{0,1:T(8,128)(2,1)} %copy.112), channel_id=1, source_target_pairs={{0,4},{4,0},{8,12},{12,8},{16,20},{20,16},{24,28},{28,24},{1,5},{5... | collective-permute-start | bytes 4030472 | tf_op jit(solution)/shard_map/ppermute | solution.py:20
  453.9 36.7 %collective-permute-start.64 = (bf16[1024,640]{1,0:T(8,128)(2,1)}, bf16[1024,640]{1,0:T(8,128)(2,1)}, u32[]{:S(2)}, u32[]{:S(2)}) collective-permute-start(bf16[1024,640]{1,0:T(8,128)(2,1)} %get-tuple-element.108), channel_id=1, source_target_pairs={{0,4},{4,0},{8,12},{12,8},{16,20},{20,16},{24,28},{28,24},{1,5},{5... | collective-permute-start | bytes 3932168 | tf_op jit(solution)/shard_map/ppermute | solution.py:20
  463.3 38.2 %collective-permute-start.63 = (bf16[1,256,512]{2,1,0:T(8,128)(2,1)S(1)}, bf16[1,256,512]{2,1,0:T(8,128)(2,1)S(1)}, u32[]{:S(2)}, u32[]{:S(2)}) collective-permute-start(bf16[1,256,512]{2,1,0:T(8,128)(2,1)S(1)} %slice.362), channel_id=1, source_target_pairs={{0,16},{4,20},{8,24},{12,28},{16,0},{20,4},{24,8},{28,12},{1,17},{... | collective-permute-start | bytes 786440 | tf_op jit(solution)/shard_map/ppermute | solution.py:20
  485.8 105.5 %collective-permute-start.39 = (bf16[768,512]{1,0:T(8,128)(2,1)}, bf16[768,512]{1,0:T(8,128)(2,1)}, u32[]{:S(2)}, u32[]{:S(2)}) collective-permute-start(bf16[768,512]{1,0:T(8,128)(2,1)} %get-tuple-element.198), channel_id=1, source_target_pairs={{0,1},{1,2},{2,3},{4,5},{5,6},{6,7},{8,9},{9,10},{10,11},{12,13},{... | collective-permute-start | bytes 2359304 | tf_op jit(solution)/shard_map/ppermute | solution.py:89
  525.1 66.1 %collective-permute-start.42 = (bf16[768,512]{1,0:T(8,128)(2,1)S(1)}, bf16[768,512]{1,0:T(8,128)(2,1)S(1)}, u32[]{:S(2)}, u32[]{:S(2)}) collective-permute-start(bf16[768,512]{1,0:T(8,128)(2,1)S(1)} %fusion.14), channel_id=1, source_target_pairs={{1,0},{2,1},{3,2},{5,4},{6,5},{7,6},{9,8},{10,9},{11,10},{13,12},{... | collective-permute-start | bytes 2359304 | tf_op jit(solution)/shard_map/ppermute | solution.py:90
  527.9 34.2 %collective-permute-start.54 = (f32[3,8,256]{2,1,0:T(8,128)S(1)}, f32[3,8,256]{2,1,0:T(8,128)S(1)}, u32[]{:S(2)}, u32[]{:S(2)}) collective-permute-start(f32[3,8,256]{2,1,0:T(8,128)S(1)} %add.295), channel_id=1, source_target_pairs={{0,2},{1,3},{2,0},{3,1},{4,6},{5,7},{6,4},{7,5},{8,10},{9,11},{10,... | collective-permute-start | bytes 73736 | tf_op jit(solution)/shard_map/ppermute | solution.py:20
  534.9 56.3 %collective-permute-start.49 = (bf16[768,512]{1,0:T(8,128)(2,1)}, bf16[768,512]{1,0:T(8,128)(2,1)}, u32[]{:S(2)}, u32[]{:S(2)}) collective-permute-start(bf16[768,512]{1,0:T(8,128)(2,1)} %get-tuple-element.194), channel_id=1, source_target_pairs={{0,1},{1,2},{2,3},{4,5},{5,6},{6,7},{8,9},{9,10},{10,11},{12,13},{... | collective-permute-start | bytes 2359304 | tf_op jit(solution)/shard_map/ppermute | solution.py:89
  556.1 36.0 %collective-permute-start.52 = (bf16[768,512]{1,0:T(8,128)(2,1)}, bf16[768,512]{1,0:T(8,128)(2,1)}, u32[]{:S(2)}, u32[]{:S(2)}) collective-permute-start(bf16[768,512]{1,0:T(8,128)(2,1)} %fusion.9), channel_id=1, source_target_pairs={{1,0},{2,1},{3,2},{5,4},{6,5},{7,6},{9,8},{10,9},{11,10},{13,12},{... | collective-permute-start | bytes 2359304 | tf_op jit(solution)/shard_map/ppermute | solution.py:90
  (133 other events, 1943.2 us)

commit v3 on v2

v3 whole, which is shorter than its diff:
```python
import functools
import jax
import jax.numpy as jnp
from jax import lax
from jax.experimental import pallas as pl
from jax.experimental.pallas import tpu as pltpu
from jax.sharding import PartitionSpec as P

epsilon = 1e-05
highest = lax.Precision.HIGHEST
f32 = jnp.float32
bf16 = jnp.bfloat16
LANES = 128
HALO = 8
STATE_PAD = 16
COST_SCALE = 64
VMEM_SPARE = 4 * 1024 * 1024


def swapped(value, axis, bit):
    return lax.ppermute(value, axis, [(i, i ^ bit) for i in range(lax.axis_size(axis))])


def axis_bits(axis):
    count = lax.axis_size(axis)
    return [1 << k for k in range(count.bit_length() - 1)]


def added(left, right):
    return (left.astype(f32) + right.astype(f32)).astype(left.dtype)


def after(value, *others):
    return lax.optimization_barrier((value, *others))[0]


def after_all(values, others):
    return lax.optimization_barrier((tuple(values), tuple(others)))[0]


class Scattered:
    def __init__(self, keep, send, labels, order):
        rows = keep.shape[0] // len(labels)
        self.pair = (keep.reshape(len(labels), rows, -1), send.reshape(len(labels), rows, -1))
        self.labels, self.left = labels, list(order)

    def advance(self):
        kept, sent = self.pair
        total = added(kept, swapped(sent, "seq", self.left.pop(0)))
        if not self.left:
            self.pair = (total,)
            return
        following, labels = self.left[0], self.labels
        keep_at = [at for at, label in enumerate(labels) if not label & following]
        send_at = [labels.index(labels[at] ^ following) for at in keep_at]
        kept = jnp.concatenate([total[at : at + 1] for at in keep_at])
        sent = jnp.concatenate([total[at : at + 1] for at in send_at])
        self.pair = (kept, sent)
        self.labels = [labels[at] for at in keep_at]

    def finish(self):
        return [self.pair[0][0]]


class LineGather:
    def __init__(self, own):
        self.size = lax.axis_size("head")
        self.up = self.down = own
        self.ups, self.downs = [], []

    def advance(self, *beside):
        step = len(self.ups) + 1
        if step < self.size:
            up = lax.ppermute(self.up, "head", [(i, i + 1) for i in range(step - 1, self.size - 1)])
            down = lax.ppermute(self.down, "head", [(i, i - 1) for i in range(1, self.size - step + 1)])
            if beside:
                (up, down), beside = lax.optimization_barrier(((up, down), beside))
            self.up, self.down = up, down
            self.ups.append(up)
            self.downs.append(down)
        return beside

    def finish(self):
        while len(self.ups) + 1 < self.size:
            self.advance()
        return self.ups, self.downs


class LineScatter:
    def __init__(self, edges, middle):
        self.size, self.here = lax.axis_size("head"), lax.axis_index("head")
        self.edges, self.middle = edges, middle
        self.up = self.down = None
        self.step = 0

    def block_of(self, at):
        last = self.size - 1
        inner = lax.dynamic_index_in_dim(self.middle, jnp.clip(at - 1, 0, last - 2), 0, keepdims=False)
        return jnp.where(at <= 0, self.edges[0], jnp.where(at >= last, self.edges[1], inner))

    def advance(self, *beside):
        self.step += 1
        step, size, here = self.step, self.size, self.here
        if step < size:
            if step == 1:
                up, down = self.edges[1], self.edges[0]
            else:
                up = added(self.block_of(here + size - step), self.up)
                down = added(self.block_of(here - size + step), self.down)
            up = lax.ppermute(up, "head", [(i, i + 1) for i in range(step)])
            down = lax.ppermute(down, "head", [(i, i - 1) for i in range(size - step, size)])
            if beside:
                (up, down), beside = lax.optimization_barrier(((up, down), beside))
            self.up, self.down = up, down
        return beside

    def finish(self):
        while self.step + 1 < self.size:
            self.advance()
        return self.block_of(self.here).astype(f32) + self.up.astype(f32) + self.down.astype(f32)


def axis_sum(value, axis):
    for bit in axis_bits(axis):
        value = value + swapped(value, axis, bit)
    return value


def passed_along(value, axis, steps):
    count = lax.axis_size(axis)
    initial, last = (max(0, -steps), min(count, count - steps))
    return lax.ppermute(value, axis, [(source, source + steps) for source in range(initial, last)])


def dot(left, right, precision=None):
    return jnp.dot(left, right, preferred_element_type=f32, precision=precision)


def dot_nt(left, right, precision=None):
    return lax.dot_general(
        left, right, (((1,), (1,)), ((), ())), preferred_element_type=f32, precision=precision
    )


def dot_tn(left, right, precision=None):
    return lax.dot_general(
        left, right, (((0,), (0,)), ((), ())), preferred_element_type=f32, precision=precision
    )


def both_parts(values):
    high = values.astype(bf16)
    return jnp.concatenate([high, (values - high.astype(f32)).astype(bf16)], axis=1)


def silu_slope(values):
    logistic = jax.nn.sigmoid(values)
    return logistic * (1.0 + values * (1.0 - logistic))


def tiled_bytes(shape, dtype):
    *lead, rows, lanes = shape
    size = -(-rows // 8) * 8 * -(-lanes // LANES) * LANES * jnp.dtype(dtype).itemsize
    for count in lead:
        size *= count
    return size


def call(kernel, grid, scalars, ins, outs, scratch=(), flops=0, bytes_accessed=0):
    held = [block == array.shape for array, block, _ in ins]
    need = sum(
        (1 if whole else 2) * tiled_bytes(block, array.dtype) for (array, block, _), whole in zip(ins, held)
    )
    need += sum(2 * tiled_bytes(block, dtype) for _, dtype, block, _ in outs)
    need += sum(tiled_bytes(item.shape, item.dtype) for item in scratch)
    return pl.pallas_call(
        kernel,
        grid_spec=pltpu.PrefetchScalarGridSpec(
            num_scalar_prefetch=len(scalars),
            grid=grid,
            in_specs=[
                pl.BlockSpec(block, index, pipeline_mode=pl.Buffered(1) if whole else None)
                for (_, block, index), whole in zip(ins, held)
            ],
            out_specs=[pl.BlockSpec(block, index) for _, _, block, index in outs],
            scratch_shapes=list(scratch),
        ),
        out_shape=[jax.ShapeDtypeStruct(shape, dtype) for shape, dtype, _, _ in outs],
        compiler_params=pltpu.CompilerParams(vmem_limit_bytes=need + VMEM_SPARE),
        cost_estimate=pl.CostEstimate(
            flops=int(flops) // COST_SCALE, bytes_accessed=int(bytes_accessed) // COST_SCALE, transcendentals=0
        ),
    )(*scalars, *[array for array, _, _ in ins])


def per_row(array, rows):
    return (array, (rows,) + array.shape[1:], lambda m, *_: (m,) + (0,) * (array.ndim - 1))


def per_deal(array):
    return (array, (array.shape[0], 1) + array.shape[2:], lambda m, *_: (0, m, 0, 0))


def deal_out(senders, count, rows, width, dtype):
    return ((senders, count, rows, width), dtype, (senders, 1, rows, width), lambda m, *_: (0, m, 0, 0))


def deal_rows(ref, tile):
    values = ref[:, 0, :, tile].astype(f32)
    return values.reshape(values.shape[0] * values.shape[1], values.shape[2])


def put_deal_rows(ref, tile, values):
    shape = (ref.shape[0], ref.shape[2], values.shape[1])
    ref[:, 0, :, tile] = values.reshape(shape).astype(ref.dtype)


def per_step(array):
    return (array, (1,) + array.shape[1:], lambda m, *_: (m,) + (0,) * (array.ndim - 1))


def entire(array):
    return (array, array.shape, lambda *_: (0,) * array.ndim)


def row_out(total, rows, width, dtype):
    return ((total, width), dtype, (rows, width), lambda m, *_: (m, 0))


def step_out(count, shape, dtype):
    return ((count,) + shape, dtype, (1,) + shape, lambda m, *_: (m,) + (0,) * len(shape))


def sum_out(shape, dtype=f32):
    return (shape, dtype, shape, lambda *_: (0,) * len(shape))


def joined(earlier, following, states):
    row = lax.broadcasted_iota(jnp.int32, earlier.shape, 0)
    return following[states : states + 1] * earlier + jnp.where(row < states, following, 0.0)


def chip_kernel(states, flags, own, other, total):
    for at in range(own.shape[0]):
        mine, theirs = own[at].astype(f32), other[at].astype(f32)
        later = flags[0] != 0
        first, second = jnp.where(later, theirs, mine), jnp.where(later, mine, theirs)
        total[at] = joined(first, second, states).astype(bf16)


def link_kernel(states, step, last, flags, *refs):
    total, other, refs = refs[0], refs[1], refs[2:]
    later = flags[step] != 0
    if step > 1:
        before, refs = refs[0], refs[1:]
    for at in range(total.shape[0]):
        mine, theirs = total[at].astype(f32), other[at].astype(f32)
        if step == 1:
            row = lax.broadcasted_iota(jnp.int32, mine.shape, 0)
            ahead = jnp.where(row < states, 0.0, 1.0)
            refs[0][at] = jnp.where(later, theirs, ahead).astype(bf16)
        else:
            ahead = before[at].astype(f32)
            refs[0][at] = jnp.where(later, joined(theirs, ahead, states), ahead).astype(bf16)
        if not last:
            first, second = jnp.where(later, theirs, mine), jnp.where(later, mine, theirs)
            refs[1][at] = joined(first, second, states).astype(bf16)


def enter_kernel(states, flags, ahead, ahead_other, sibling, entering):
    odd = flags[flags.shape[0] - 1] != 0
    half = ahead.shape[2]
    for at in range(ahead.shape[0]):
        mine, theirs = ahead[at], ahead_other[at]
        left, right = jnp.where(odd, theirs, mine), jnp.where(odd, mine, theirs)
        for start, values in ((0, left), (half, right)):
            values = values.astype(f32)
            near = sibling[at, :, start : start + half].astype(f32)
            entering[at, :, start : start + half] = jnp.where(
                flags[0] != 0, joined(values, near, states), values
            ).astype(bf16)


def scan_before(local, states, reverse, fillers):
    here = lax.axis_index("seq")
    bits = axis_bits("seq")
    count, height, width = local.shape
    passed = [((here & bit) == 0) if reverse else ((here & bit) != 0) for bit in bits]
    flags = jnp.stack(passed + [(here & 1) != 0]).astype(jnp.int32)
    whole = local.shape
    piece = (count, height, width // 2)
    at_step = lambda *_: (0, 0, 0)
    at_core = lambda _, flags: (0, 0, flags[len(bits)])
    half_out = (piece, bf16, piece, at_step)
    moved = local.size * 4
    sibling = swapped(local, "seq", 1)
    (total,) = call(
        functools.partial(chip_kernel, states), (1,), (flags,),
        [(local, piece, at_core), (sibling, piece, at_core)], [half_out], bytes_accessed=moved,
    )
    ahead, filled, beside = None, [], ()
    for step, bit in enumerate(bits[1:], 1):
        other = swapped(total, "seq", bit)
        if step <= len(fillers):
            other, value = lax.optimization_barrier((other, fillers[step - 1](*beside)))
            beside = (value,)
            filled.append(value)
        last = step == len(bits) - 1
        ins = [total, other] + ([] if ahead is None else [ahead])
        results = call(
            functools.partial(link_kernel, states, step, last), (1,), (flags,),
            [(array, piece, at_step) for array in ins], [half_out] * (1 if last else 2),
            bytes_accessed=moved,
        )
        ahead = results[0]
        total = None if last else results[1]
    ahead_other = swapped(ahead, "seq", 1)
    (entering,) = call(
        functools.partial(enter_kernel, states), (1,), (flags,),
        [(ahead, piece, at_step), (ahead_other, piece, at_step), (sibling, whole, at_step)],
        [(local.shape, bf16, whole, at_step)], bytes_accessed=moved * 2,
    )
    return [entering] + filled


def segment_of(position, plan, place, m):
    found = jnp.full(jnp.shape(position), -1, jnp.int32)
    for k in range(plan.shape[1]):
        found = found + (position >= plan[m, k]).astype(jnp.int32)
    return jnp.where(position >= place[3], -2, found)


def column_position(rows, place, shift=0):
    return place[2] + shift + lax.broadcasted_iota(jnp.int32, (rows, 1), 0)


def row_position(rows, place):
    return place[2] + lax.broadcasted_iota(jnp.int32, (1, rows), 1)


def by_core(values, me, depth):
    count = values.shape[1] // depth
    blocks = [values[:, k * depth : (k + 1) * depth] for k in range(count)]
    odd = (me & 1) != 0
    halves = []
    for at in (0, 1):
        straight, turned = blocks[at::2], blocks[1 - at :: 2]
        half = [jnp.where(odd, b, a) for a, b in zip(straight, turned)]
        bit = 1
        while bit < count // 2:
            flip = ((me >> 1) & bit) != 0
            half = [jnp.where(flip, half[k ^ bit], half[k]) for k in range(len(half))]
            bit *= 2
        halves.append(half[0] if len(half) == 1 else jnp.concatenate(half, axis=1))
    return halves


def half_start(quarter, me, width, depth):
    count = width // depth // 2
    return pl.multiple_of(((quarter * count) ^ ((me >> 1) & ~(count - 1))) * depth, width // 2)


def line_slot(own, ups, downs, z, step):
    if step == 0:
        return deal_rows(own, slice(None))
    up, down = ups[step - 1], downs[len(downs) - step]
    return jnp.where(z >= step, deal_rows(up, slice(None)), deal_rows(down, slice(None)))


def features_kernel(size, depth, place, *refs):
    own, ups, downs = refs[0], refs[1:size], refs[size : 2 * size - 1]
    gain, normed, even_t, odd_t, inverse = refs[2 * size - 1 :]
    z, me = place[0], place[1]
    width = own.shape[3]
    slots = [line_slot(own, ups, downs, z, step) for step in range(size)]
    square = sum(jnp.sum(slot * slot, axis=1, keepdims=True) for slot in slots)
    inv = lax.rsqrt(square / (width * size) + epsilon)
    put_deal_rows(inverse, slice(None), inv)
    for step, slot in enumerate(slots):
        quarter = lax.rem(z - step + size, size)
        place_at = pl.ds(pl.multiple_of(quarter * width, width), width)
        slot = slot * inv * gain[:, place_at]
        normed[:, place_at] = slot.astype(bf16)
        first, second = by_core(slot, me, depth)
        at = pl.ds(half_start(quarter, me, width, depth), width // 2)
        even_t[at, :] = first.T.astype(bf16)
        odd_t[at, :] = second.T.astype(bf16)


def all_features(own, lines, place, gain, depth):
    senders, count, piece, width = own.shape
    rows = senders * piece
    total = rows * count
    size = lax.axis_size("head")
    ups, downs = lines
    half = width * size // 2
    outs = [row_out(total, rows, 2 * half, bf16)]
    outs += [((half, total), bf16, (half, rows), lambda m, *_: (0, m))] * 2
    outs.append(deal_out(senders, count, piece, 1, f32))
    return call(
        functools.partial(features_kernel, size, depth), (count,), (place,),
        [per_deal(array) for array in [own] + ups + downs] + [entire(gain)], outs,
        bytes_accessed=total * width * 2 * 15,
    )


def cotangent_kernel(size, place, *refs):
    own, ups, downs = refs[0], refs[1:size], refs[size : 2 * size - 1]
    weight, every, grad_y = refs[2 * size - 1 :]
    z = place[0]
    width = own.shape[3]
    total = None
    for step in range(size):
        slot = line_slot(own, ups, downs, z, step)
        quarter = lax.rem(z - step + size, size)
        place_at = pl.ds(pl.multiple_of(quarter * width, width), width)
        every[:, place_at] = slot.astype(bf16)
        part = dot_nt(slot.astype(bf16), weight[:, place_at])
        total = part if total is None else total + part
    grad_y[...] = total


def cotangent_products(own, lines, place, weight):
    senders, count, piece, width = own.shape
    rows = senders * piece
    total = rows * count
    size = lax.axis_size("head")
    ups, downs = lines
    return call(
        functools.partial(cotangent_kernel, size), (count,), (place,),
        [per_deal(array) for array in [own] + ups + downs] + [entire(weight)],
        [
            row_out(total, rows, width * size, bf16),
            row_out(total, rows, weight.shape[0], f32),
        ],
        flops=2 * total * width * size * weight.shape[0],
        bytes_accessed=total * width * 2 * 11 + weight.size * 2 + total * weight.shape[0] * 4,
    )


def conv_kernel(
    width, place, plan, pre, halo, taps, bias, step_bias, scale, spread, conv_out, small, inputs, maps, fresh,
    extended,
):
    m = pl.program_id(0)
    rows = pre.shape[0]
    states = maps.shape[1] // 2
    taps_total = taps.shape[0]
    here = segment_of(column_position(rows, place), plan, place, m)
    same = [
        (segment_of(column_position(rows, place, tap + 1 - taps_total), plan, place, m) == here).astype(f32)
        for tap in range(taps_total)
    ]
    before = segment_of(place[2] - 1, plan, place, m)
    last = segment_of(place[2] + rows - 1, plan, place, m)

    step_pre = pre[:, width + 2 * states : width + 2 * states + LANES] + step_bias[...]
    rest = jnp.exp(-jnp.abs(step_pre))
    series = rest * (
        1.0 - rest * (1 / 2 - rest * (1 / 3 - rest * (1 / 4 - rest * (1 / 5 - rest * (1 / 6)))))
    )
    step = jnp.maximum(step_pre, 0.0) + jnp.where(rest < 0.03, series, jnp.log(1.0 + rest))
    row = lax.broadcasted_iota(jnp.int32, (rows, rows), 0)
    col = lax.broadcasted_iota(jnp.int32, (rows, rows), 1)
    lower = (row >= col).astype(f32)
    cumulative = dot(lower, step * scale[...], highest)
    small[:, :LANES] = cumulative
    small[:, LANES : 2 * LANES] = step
    small[:, 2 * LANES :] = step_pre
    ending = cumulative[rows - 1 :, :]
    fading = (here == last).astype(f32) * jnp.exp(ending - cumulative)
    through = (last == before).astype(f32) * jnp.exp(ending)
    step_parts, fading_parts = both_parts(step), both_parts(fading)
    through_parts = both_parts(jnp.broadcast_to(through, (STATE_PAD, LANES)))

    def conv(at):
        tile = slice(at, at + LANES)
        extended[:HALO, :] = halo[0, :, tile]
        extended[HALO:, :] = pre[:, tile]
        result = jnp.broadcast_to(bias[:, tile], (rows, LANES))
        for tap in range(taps_total):
            start = HALO + tap + 1 - taps_total
            result = result + taps[tap : tap + 1, tile] * extended[start : start + rows, :] * same[tap]
        conv_out[:, tile] = result
        return result * jax.nn.sigmoid(result)

    for at in range(0, 2 * states, LANES):
        maps[:, at : at + LANES] = conv(width + at)
    input_map_t = maps[:, :states].T.astype(bf16)
    for at in range(0, width, LANES):
        tile = slice(at, at + LANES)
        values = conv(at) * dot(step_parts, spread[:, tile])
        inputs[:, tile] = values.astype(bf16)
        faded = (values * dot(fading_parts, spread[:, tile])).astype(bf16)
        fresh[0, :states, tile] = dot(input_map_t, faded).astype(bf16)
        fresh[0, states:, tile] = dot(through_parts, spread[:, tile]).astype(bf16)


def allowed_mask(rows, place, plan, m, transposed):
    column = segment_of(column_position(rows, place), plan, place, m)
    across = segment_of(row_position(rows, place), plan, place, m)
    row = lax.broadcasted_iota(jnp.int32, (rows, rows), 0)
    col = lax.broadcasted_iota(jnp.int32, (rows, rows), 1)
    order = (row <= col) if transposed else (row >= col)
    return jnp.where(order & (column == across), 0.0, -1e30)


def lane_select(parts, per):
    lane = lax.broadcasted_iota(jnp.int32, parts[0].shape, 1)
    result = parts[0]
    for at in range(1, per):
        result = jnp.where(lane >= at * (LANES // per), parts[at], result)
    return result


def mix_kernel(per, place, plan, small, maps, inputs, out):
    m = pl.program_id(0)
    rows, width = inputs.shape
    states = maps.shape[1] // 2
    cumulative = small[:, :LANES]
    flat = cumulative.T
    mask = allowed_mask(rows, place, plan, m, False)
    scores = dot_nt(maps[:, states:], maps[:, :states], highest)
    for at in range(0, width, LANES):
        tile = slice(at, at + LANES)
        for low in range(0, rows, LANES):
            end = low + LANES
            parts = []
            for sub in range(per):
                head = at // LANES * per + sub
                decay = jnp.exp(
                    (cumulative[low:end, head : head + 1] - flat[head : head + 1, :end])
                    + mask[low:end, :end]
                )
                mixing = (decay * scores[low:end, :end]).astype(bf16)
                parts.append(dot(mixing, inputs[:end, tile]))
            out[low:end, tile] = lane_select(parts, per)


def unmix_kernel(per, place, plan, small, maps, inputs, grads, grad_inputs, grad_maps, total):
    m = pl.program_id(0)
    rows, width = inputs.shape
    states = maps.shape[1] // 2
    cumulative = small[:, :LANES]
    flat = cumulative.T
    mask = allowed_mask(rows, place, plan, m, True)
    scores = dot_nt(maps[:, :states], maps[:, states:], highest)
    lane = lax.broadcasted_iota(jnp.int32, (LANES, LANES), 1)
    total[...] = jnp.zeros_like(total)
    for at in range(0, width, LANES):
        tile = slice(at, at + LANES)
        for low in range(0, rows, LANES):
            end = low + LANES
            later = grads[low:, tile]
            parts = []
            gathered_sum = total[low:end, low:]
            for sub in range(per):
                head = at // LANES * per + sub
                decay = jnp.exp(
                    (flat[head : head + 1, low:] - cumulative[low:end, head : head + 1])
                    + mask[low:end, low:]
                )
                mixing = (decay * scores[low:end, low:]).astype(bf16)
                parts.append(dot(mixing, later))
                inside = (lane // (LANES // per)) == sub
                own = jnp.where(inside, inputs[low:end, tile].astype(f32), 0.0).astype(bf16)
                gathered_sum = gathered_sum + decay * dot_nt(own, later)
            total[low:end, low:] = gathered_sum
            grad_inputs[low:end, tile] = lane_select(parts, per)
    grad_scores = total[...].astype(bf16)
    grad_maps[:, :states] = dot(grad_scores, maps[:, states:].astype(bf16))
    grad_maps[:, states:] = dot_tn(grad_scores, maps[:, :states].astype(bf16))


def inflow_of(cumulative, rows, place, plan, m):
    here = segment_of(column_position(rows, place), plan, place, m)
    before = segment_of(place[2] - 1, plan, place, m)
    return (here == before).astype(f32) * jnp.exp(cumulative)


def gated_kernel(
    place, plan, small, maps, mixed, entering, conv_out, gate, grad_y, gain, skip, spread, scanned, scaled_y, sums
):
    m = pl.program_id(0)
    rows, width = mixed.shape
    states = maps.shape[1] // 2
    inflow = both_parts(inflow_of(small[:, :LANES], rows, place, plan, m))
    output_map = maps[:, states:].astype(bf16)
    square = jnp.zeros((rows, LANES), f32)
    product = jnp.zeros((rows, LANES), f32)
    for at in range(0, width, LANES):
        tile = slice(at, at + LANES)
        carried = dot(output_map, entering[0, :states, tile]) * dot(inflow, spread[:, tile])
        scan = mixed[:, tile] + carried
        scanned[:, tile] = scan
        conv = conv_out[:, tile]
        gates = gate[:, tile]
        gated = (scan + skip[:, tile] * (conv * jax.nn.sigmoid(conv))) * (gates * jax.nn.sigmoid(gates))
        square = square + gated * gated
        scaled = gain[:, tile] * gated
        put_deal_rows(scaled_y, tile, scaled)
        product = product + grad_y[:, tile] * scaled
    ones = jnp.ones((HALO, LANES), f32)
    pick = lax.broadcasted_iota(jnp.int32, (HALO, rows), 0)
    sums[0] = jnp.where(pick == 0, dot_nt(ones, square, highest), dot_nt(ones, product, highest))


def ungated_kernel(
    inner_all, place, plan, small, maps, scanned, conv_out, gate, grad_y, sums, gain, skip, spread,
    normed_y_t, grads, grad_gate, local, row_part, grad_gain, grad_skip,
):
    m = pl.program_id(0)
    rows, width = scanned.shape
    states = maps.shape[1] // 2
    row = lax.broadcasted_iota(jnp.int32, (rows, rows), 0)
    col = lax.broadcasted_iota(jnp.int32, (rows, rows), 1)
    columns = dot_nt((row == col).astype(f32), sums[0], highest)
    inv = lax.rsqrt(columns[:, :1] / inner_all + epsilon)
    pull = inv * inv * inv * (columns[:, 1:2] / inner_all)
    cumulative = small[:, :LANES]
    inflow = both_parts(inflow_of(cumulative, rows, place, plan, m))
    before = segment_of(place[2] - 1, plan, place, m)
    last = segment_of(place[2] + rows - 1, plan, place, m)
    through = (last == before).astype(f32) * jnp.exp(cumulative[rows - 1 :, :])
    through_parts = both_parts(jnp.broadcast_to(through, (STATE_PAD, LANES)))
    output_map_t = maps[:, states:].T.astype(bf16)

    @pl.when(m == 0)
    def _():
        grad_gain[...] = jnp.zeros_like(grad_gain)
        grad_skip[...] = jnp.zeros_like(grad_skip)

    product = jnp.zeros((rows, LANES), f32)
    for at in range(0, width, LANES):
        tile = slice(at, at + LANES)
        conv = conv_out[:, tile]
        heads_x = conv * jax.nn.sigmoid(conv)
        mixer = scanned[:, tile] + skip[:, tile] * heads_x
        gates = gate[:, tile]
        logistic = jax.nn.sigmoid(gates)
        act = gates * logistic
        gated = mixer * act
        normed = gated * inv
        normed_y_t[tile, :] = (normed * gain[:, tile]).T.astype(bf16)
        grad = grad_y[:, tile]
        grad_gain[:, tile] += jnp.sum(grad * normed, axis=0, keepdims=True)
        grad_gated = inv * (grad * gain[:, tile]) - gated * pull
        grad_mixer = grad_gated * act
        grads[:, tile] = grad_mixer.astype(bf16)
        grad_skip[:, tile] += jnp.sum(grad_mixer * heads_x, axis=0, keepdims=True)
        grad_gates = grad_gated * mixer * (logistic * (1.0 + gates * (1.0 - logistic)))
        grad_gate[:, tile] = grad_gates.astype(bf16)
        product = product + grad_gates * gates
        weighted = (grad_mixer * dot(inflow, spread[:, tile])).astype(bf16)
        local[0, :states, tile] = dot(output_map_t, weighted).astype(bf16)
        local[0, states:, tile] = dot(through_parts, spread[:, tile]).astype(bf16)
    row_part[0] = dot_nt(jnp.ones((HALO, LANES), f32), product, highest)


def unscan_kernel(
    place, plan, small, maps, scanned, conv_out, inputs, grads, grad_inputs, grad_maps, entering, leaving,
    skip, scale, spread, grad_conv_out, grad_step, grad_bias, grad_heads,
):
    m = pl.program_id(0)
    rows, width = scanned.shape
    states = maps.shape[1] // 2
    cumulative, step, pre = (small[:, k * LANES : (k + 1) * LANES] for k in range(3))
    here = segment_of(column_position(rows, place), plan, place, m)
    before = segment_of(place[2] - 1, plan, place, m)
    last = segment_of(place[2] + rows - 1, plan, place, m)
    ending = cumulative[rows - 1 :, :]
    fading = both_parts((here == last).astype(f32) * jnp.exp(ending - cumulative))
    inflow = both_parts((here == before).astype(f32) * jnp.exp(cumulative))
    through = (last == before).astype(f32) * jnp.exp(ending)
    step_parts = both_parts(step)
    input_map = maps[:, :states].astype(bf16)

    @pl.when(m == 0)
    def _():
        grad_bias[...] = jnp.zeros_like(grad_bias)
        grad_heads[...] = jnp.zeros_like(grad_heads)

    grad_in, grad_out = grad_maps[:, :states], grad_maps[:, states:]
    grad_cum = jnp.zeros((rows, LANES), f32)
    grad_own = jnp.zeros((rows, LANES), f32)
    ends = jnp.zeros((HALO, LANES), f32)
    for at in range(0, width, LANES):
        tile = slice(at, at + LANES)
        spread_tile = spread[:, tile]
        leave, enter = leaving[0, :states, tile], entering[0, :states, tile]
        fade = dot(fading, spread_tile)
        pulled = fade * dot(input_map, leave)
        values = inputs[:, tile].astype(f32)
        grad = grads[:, tile].astype(f32)
        total = grad_inputs[:, tile] + pulled
        faded = (values * fade).astype(bf16)
        weighted = (grad * dot(inflow, spread_tile)).astype(bf16)
        grad_in = grad_in + dot_nt(faded, leave)
        grad_out = grad_out + dot_nt(weighted, enter)
        conv = conv_out[:, tile]
        logistic = jax.nn.sigmoid(conv)
        heads_x = conv * logistic
        first = both_parts(grad * scanned[:, tile] - values * total)
        second = both_parts(total * heads_x)
        grad_cum = grad_cum + dot_nt(first[:, :LANES], spread[:LANES, tile]) + dot_nt(
            first[:, LANES:], spread[:LANES, tile]
        )
        grad_own = grad_own + dot_nt(second[:, :LANES], spread[:LANES, tile]) + dot_nt(
            second[:, LANES:], spread[:LANES, tile]
        )
        fade_sum = jnp.sum(values * pulled, axis=0, keepdims=True)
        through_sum = jnp.sum(leave.astype(f32) * enter.astype(f32), axis=0, keepdims=True)
        pick = lax.broadcasted_iota(jnp.int32, (HALO, LANES), 0)
        edge = both_parts(jnp.where(pick == 0, fade_sum, through_sum))
        ends = ends + dot_nt(edge[:, :LANES], spread[:LANES, tile]) + dot_nt(
            edge[:, LANES:], spread[:LANES, tile]
        )
        grad_x = total * dot(step_parts, spread_tile) + skip[:, tile] * grad
        result = grad_x * (logistic * (1.0 + conv * (1.0 - logistic)))
        grad_conv_out[:, tile] = result
        grad_bias[:, tile] += jnp.sum(result, axis=0, keepdims=True)
    for values, start in ((grad_in, width), (grad_out, width + states)):
        conv = conv_out[:, start : start + states]
        result = values * silu_slope(conv)
        grad_conv_out[:, start : start + states] = result
        grad_bias[:, start : start + states] += jnp.sum(result, axis=0, keepdims=True)
    row = lax.broadcasted_iota(jnp.int32, (rows, rows), 0)
    col = lax.broadcasted_iota(jnp.int32, (rows, rows), 1)
    upper = (row <= col).astype(f32)
    grad_rate = dot(upper, grad_cum, highest) + (ends[:1] + through * ends[1:2])
    rate = step * scale[...]
    grad_pre = (grad_rate * scale[...] + grad_own) * jax.nn.sigmoid(pre)
    grad_step[...] = grad_pre
    grad_heads[0:1, :] += jnp.sum(grad_rate * rate, axis=0, keepdims=True)
    grad_heads[1:2, :] += jnp.sum(grad_pre, axis=0, keepdims=True)


def unconv_kernel(
    place, plan, pre, halo, grad_out, after_rows, grad_step, row_part, taps, grad_pre, row_sums, grad_taps,
    extended, extended_grad,
):
    m = pl.program_id(0)
    rows = pre.shape[0]
    channels = grad_out.shape[1]
    taps_total = taps.shape[0]
    here = segment_of(column_position(rows, place), plan, place, m)
    behind, ahead = [], []
    for tap in range(taps_total):
        lag = taps_total - 1 - tap
        behind.append((segment_of(column_position(rows, place, -lag), plan, place, m) == here).astype(f32))
        ahead.append((segment_of(column_position(rows, place, lag), plan, place, m) == here).astype(f32))

    @pl.when(m == 0)
    def _():
        grad_taps[...] = jnp.zeros_like(grad_taps)

    total = jnp.zeros((rows, LANES), f32)
    for at in range(0, channels, LANES):
        tile = slice(at, at + LANES)
        extended[:HALO, :] = halo[0, :, tile]
        extended[HALO:, :] = pre[:, tile]
        grad = grad_out[:, tile]
        extended_grad[:rows, :] = grad
        extended_grad[rows:, :] = after_rows[0, :, tile]
        result = jnp.zeros((rows, LANES), f32)
        for tap in range(taps_total):
            lag = taps_total - 1 - tap
            result = result + taps[tap : tap + 1, tile] * extended_grad[lag : lag + rows, :] * ahead[tap]
            begin = HALO - lag
            product = grad * extended[begin : begin + rows, :] * behind[tap]
            grad_taps[tap : tap + 1, tile] += jnp.sum(product, axis=0, keepdims=True)
        grad_pre[:, tile] = result.astype(bf16)
        total = total + result * pre[:, tile]
    grad_pre[:, channels:] = grad_step[...].astype(bf16)
    total = total + grad_step[...] * pre[:, channels : channels + LANES]
    row_sums[0] = row_part[0] + dot_nt(jnp.ones((HALO, LANES), f32), total, highest)


def rows_kernel(first, second, weight, out):
    cut = weight.shape[1] - second.shape[1]
    result = dot_nt(first[...], weight[:, : first.shape[1]]) + dot_nt(second[...], weight[:, cut:])
    put_deal_rows(out.at[0], slice(None), result)


def rows_gradient(first, second, weight, quarters, senders, count):
    total = first.shape[0]
    start, stride, number = quarters
    size = lax.axis_size("head")
    width = weight.shape[0] // size
    rows = total // count
    row_block = lambda array: (array, (rows, array.shape[1]), lambda q, m: (m, 0))
    shape = (number, senders, count, rows // senders, width)
    block = (1, senders, 1, rows // senders, width)
    return call(
        rows_kernel, (number, count), (),
        [row_block(first), row_block(second)]
        + [(weight, (width, weight.shape[1]), lambda q, m: (start + stride * q, 0))],
        [(shape, bf16, block, lambda q, m: (q, 0, m, 0, 0))],
        flops=2 * total * (first.shape[1] + second.shape[1]) * width * number,
        bytes_accessed=(weight.size + (first.size + second.size) * number) * 2,
    )[0]


def state_kernel(depth, place, even_t, odd_t, grads, out):
    me = place[1]
    quarter = pl.program_id(0)
    height = out.shape[0]
    at = pl.ds(half_start(quarter, me, height, depth), height // 2)
    parts = [dot(left[at, :], grads[...]) for left in (even_t, odd_t)]
    odd = (me & 1) != 0
    count = height // depth
    halves = []
    for values in parts:
        half = [values[k * depth : (k + 1) * depth, :] for k in range(count // 2)]
        bit = 1
        while bit < count // 2:
            flip = ((me >> 1) & bit) != 0
            half = [jnp.where(flip, half[k ^ bit], half[k]) for k in range(len(half))]
            bit *= 2
        halves.append(half)
    for k in range(count // 2):
        base = 2 * k * depth
        out[base : base + depth, :] = jnp.where(odd, halves[1][k], halves[0][k]).astype(bf16)
        out[base + depth : base + 2 * depth, :] = jnp.where(odd, halves[0][k], halves[1][k]).astype(bf16)


def out_kernel(left, right, out):
    depth = out.shape[2]
    for block in range(out.shape[0]):
        out[block] = dot(left[...], right[:, block * depth : (block + 1) * depth]).astype(bf16)


def sent_kernel(columns, count, left, *refs):
    rights, out = refs[:count], refs[count]
    for which, source, target, size in columns:
        out[:, target : target + size] = dot(left[...], rights[which][:, source : source + size]).astype(bf16)


def kept_kernel(columns, count, cut, left, *refs):
    rights, other, outs = refs[:count], refs[count], refs[count + 1 :]
    step = pl.program_id(0)
    high, odd = step >= pl.num_programs(0) // 2, lax.rem(step, 2) == 1
    for which, source, target, size in columns:
        result = dot(left[...], rights[which][:, source : source + size])
        result = (result + other[:, target : target + size].astype(f32)).astype(bf16)
        if target < cut:
            keep, send, sending, start = outs[0], outs[1], high, target
        else:
            keep, send, sending, start = outs[2], outs[3], odd, target - cut
        tile = slice(start, start + size)

        @pl.when(sending)
        def _():
            send[:, tile] = result

        @pl.when(jnp.logical_not(sending))
        def _():
            keep[:, tile] = result


def total_kernel(targets, *refs):
    ins, outs = refs[:2], refs[2:]
    for out, (which, source, target, size) in zip([outs[t[0]] for t in targets], [t[1] for t in targets]):
        tile = slice(source, source + size)
        out[:, target : target + size] = ins[which][:, tile].astype(f32)


def weight_gradient_sent(odd_t, rights, columns, depth):
    total = odd_t.shape[1]
    width = max(target + size for _, _, target, size in columns)
    (sent,) = call(
        functools.partial(sent_kernel, columns, len(rights)), (odd_t.shape[0] // depth,), (),
        [(odd_t, (depth, total), lambda l: (l, 0))] + [entire(right) for right in rights],
        [((odd_t.shape[0], width), bf16, (depth, width), lambda l: (l, 0))],
        flops=2 * odd_t.shape[0] * total * width,
        bytes_accessed=odd_t.shape[0] * (total + width) * 2 + sum(right.size for right in rights) * 2,
    )
    return sent, swapped(sent, "seq", 1)


def weight_gradient(line, other, even_t, got, rights, columns, cut, results, depth):
    blocks = even_t.shape[0] // depth
    total = even_t.shape[1]
    width = got.shape[1]
    left = lambda array: (array, (depth, total), lambda l: (l, 0))
    flops = 2 * even_t.shape[0] * total * width
    moved = even_t.shape[0] * (total + width) * 2 + sum(right.size for right in rights) * 2
    top = blocks // 2
    rows = even_t.shape[0] // 2
    half = lambda size, index: ((rows, size), bf16, (depth, size), index)
    mine = call(
        functools.partial(kept_kernel, columns, len(rights), cut), (blocks,), (),
        [left(even_t)] + [entire(right) for right in rights] + [(got, (depth, width), lambda l: (l, 0))],
        [
            half(cut, lambda l: (jnp.minimum(l, top - 1), 0)),
            half(cut, lambda l: (jnp.maximum(l - top, 0), 0)),
            half(width - cut, lambda l: (l // 2, 0)),
            half(width - cut, lambda l: (l // 2, 0)),
        ],
        flops=flops, bytes_accessed=moved,
    )
    links = axis_bits("seq")[1:]
    labels = [bit << 1 for bit in range(blocks)]
    *mine, other = line.advance(*mine, other)
    parts = [
        Scattered(mine[0], mine[1], [x for x in labels if not x & links[-1]], links[::-1]),
        Scattered(mine[2], mine[3], [x for x in labels if not x & links[0]], links),
    ]
    while parts[0].left:
        for part in parts:
            part.advance()
        for part, pair in zip(parts, line.advance(*[part.pair for part in parts])):
            part.pair = pair
    first, second = [part.finish() for part in parts]
    targets = [(at, column) for at, (_, parts) in enumerate(results) for column in parts]
    return *call(
        functools.partial(total_kernel, targets), (1,), (), [entire(a) for a in first + second],
        [((depth, size), f32, (depth, size), lambda *_: (0, 0)) for size, _ in results],
        bytes_accessed=depth * width * 8,
    ), other


def per_device(
    tokens,
    cotangent,
    lengths,
    deal_order,
    norm_gain,
    proj_gate,
    proj_inner,
    proj_state,
    proj_step,
    conv_inner,
    conv_inner_bias,
    conv_state,
    conv_state_bias,
    step_bias,
    decay_log,
    skip_gain,
    inner_gain,
    proj_out,
):
    batch_count = lengths.shape[0]
    rows_local, width_own = tokens.shape
    tok_dev = rows_local // batch_count
    seq_index = lax.axis_index("seq")
    head_index = lax.axis_index("head")
    seq_size = lax.axis_size("seq")
    head_size = lax.axis_size("head")
    heads_own = proj_step.shape[1]
    inner_own = proj_inner.shape[1]
    head_width = inner_own // heads_own
    states = proj_state.shape[1] // 2
    taps_total = conv_inner.shape[0]
    width_all = width_own * head_size
    inner_all = inner_own * head_size
    depth = width_all // seq_size
    channels = inner_own + 2 * states
    per = LANES // head_width
    rows = tok_dev
    grid = (batch_count,)

    place = jnp.stack(
        [head_index, seq_index, seq_index * tok_dev, jnp.int32(tok_dev * seq_size)]
    ).astype(jnp.int32)
    plan = (jnp.cumsum(lengths, axis=1) - lengths).astype(jnp.int32)
    scalars = (place, plan)

    piece = tok_dev // seq_size
    dealt_row = deal_order.reshape(batch_count, seq_size, piece) + (
        jnp.arange(batch_count, dtype=jnp.int32) * tok_dev
    )[:, None, None]
    picks = (
        jnp.transpose(dealt_row, (1, 0, 2)).reshape(rows_local, 1) == jnp.arange(rows_local)[None, :]
    ).astype(bf16)
    deal_shape = (seq_size, batch_count, piece, width_own)

    def dealt(values):
        values = dot(picks, values).astype(bf16).reshape(seq_size, batch_count * piece, width_own)
        values = lax.all_to_all(values, "seq", split_axis=0, concat_axis=0, tiled=True)
        return values.reshape(deal_shape)

    def returned(values):
        values = values.reshape(seq_size, batch_count * piece, width_own)
        values = lax.all_to_all(values, "seq", split_axis=0, concat_axis=0, tiled=True)
        return dot_tn(picks, values.reshape(rows_local, width_own)).astype(bf16)

    deal_tokens = dealt(tokens)
    lines = LineGather(deal_tokens)
    lines.advance()
    deal_cot = dealt(cotangent)

    full_in = lax.all_gather(
        jnp.concatenate(
            [proj_inner, proj_state, proj_step, jnp.zeros((depth, 2 * LANES - heads_own), bf16), proj_gate],
            axis=1,
        ),
        "seq", axis=0, tiled=True,
    )
    full_out = lax.all_gather(after(proj_out, lines.up, lines.down), "seq", axis=1, tiled=True)

    lines = lines.finish()
    normed, even_t, odd_t, inv_rms = all_features(deal_tokens, lines, place, norm_gain[None, :], depth)
    cot_lines = LineGather(after(deal_cot, lines[0][-1], lines[1][-1]))

    taps = jnp.concatenate([conv_inner, conv_state], axis=1)
    bias = jnp.concatenate([conv_inner_bias, conv_state_bias])[None, :]
    pad = LANES - heads_own
    step_bias_row = jnp.pad(step_bias, (0, pad))[None, :]
    scale = jnp.pad(-jnp.exp(decay_log), (0, pad))[None, :]
    spread = (
        jnp.arange(2 * LANES)[:, None] % LANES == jnp.arange(inner_own)[None, :] // head_width
    ).astype(bf16)
    skip = jnp.repeat(skip_gain, head_width)[None, :]
    gain = inner_gain[None, :]

    pre_width = channels + 2 * LANES
    (pre,) = cot_lines.advance(dot(normed, full_in[:, :pre_width]))
    halo = passed_along(pre.reshape(batch_count, tok_dev, -1)[:, tok_dev - HALO :], "seq", 1)
    gate = dot(normed, full_in[:, pre_width:])
    halo, gate = lax.optimization_barrier((halo, gate))
    conv_out, small, inputs, maps, fresh = call(
        functools.partial(conv_kernel, inner_own), grid, scalars,
        [per_row(pre, rows), per_step(halo)]
        + [entire(a) for a in (taps, bias, step_bias_row, scale, spread)],
        [
            row_out(rows_local, rows, channels, f32),
            row_out(rows_local, rows, 3 * LANES, f32),
            row_out(rows_local, rows, inner_own, bf16),
            row_out(rows_local, rows, 2 * states, f32),
            step_out(batch_count, (states + STATE_PAD, inner_own), bf16),
        ],
        scratch=[pltpu.VMEM((rows + HALO, LANES), f32)],
        flops=rows_local * inner_own * 2000, bytes_accessed=rows_local * inner_own * 12,
    )
    conv_out, small, inputs, maps, fresh = cot_lines.advance(conv_out, small, inputs, maps, fresh)
    scan_ins = [per_row(small, rows), per_row(maps, rows)]
    (mixed,) = call(
        functools.partial(mix_kernel, per), grid, scalars, scan_ins + [per_row(inputs, rows)],
        [row_out(rows_local, rows, inner_own, f32)],
        flops=rows_local * inner_own * 6000, bytes_accessed=rows_local * inner_own * 6,
    )
    cot_lines.advance()

    def with_cotangent(beside):
        cot_lines.ups[-1], cot_lines.downs[-1] = cot_lines.up, cot_lines.down = beside[1:]
        return cotangent_products(deal_cot, cot_lines.finish(), place, full_out)

    entering, (mixed, _, _), (flat_cot, grad_y) = scan_before(
        fresh, states, False, [lambda: (mixed, cot_lines.up, cot_lines.down), with_cotangent]
    )
    vectors = [entire(gain), entire(skip), entire(spread)]
    scanned, scaled_y, sums = call(
        gated_kernel, grid, scalars,
        scan_ins
        + [per_row(mixed, rows), per_step(entering), per_row(conv_out, rows), per_row(gate, rows)]
        + [per_row(grad_y, rows)] + vectors,
        [
            row_out(rows_local, rows, inner_own, f32),
            deal_out(seq_size, batch_count, piece, inner_own, bf16),
            step_out(batch_count, (HALO, rows), f32),
        ],
        flops=rows_local * inner_own * 1500, bytes_accessed=rows_local * inner_own * 20,
    )
    out_rows = dot(scaled_y.reshape(rows_local, inner_own), full_out).astype(bf16)
    sums = sums + swapped(sums, "head", 1)
    for bit in axis_bits("head")[1:]:
        other, out_rows = lax.optimization_barrier((swapped(sums, "head", bit), out_rows))
        sums = sums + other
    branch = lax.psum_scatter(
        out_rows.reshape(deal_shape[:3] + (width_all,)), "head", scatter_dimension=3, tiled=True
    )

    def deal_column(values):
        return jnp.transpose(values.reshape(batch_count, seq_size, piece), (1, 0, 2))[..., None]

    inner_inv = deal_column(lax.rsqrt(sums[:, 0, :] / inner_all + epsilon))
    normed_y_t, grads, grad_gate, local, row_part, grad_gain, grad_skip = call(
        functools.partial(ungated_kernel, inner_all), grid, scalars,
        scan_ins
        + [per_row(array, rows) for array in (scanned, conv_out, gate, grad_y)]
        + [per_step(sums)] + vectors,
        [((inner_own, rows_local), bf16, (inner_own, rows), lambda m, *_: (0, m))]
        + [row_out(rows_local, rows, inner_own, bf16)] * 2
        + [step_out(batch_count, (states + STATE_PAD, inner_own), bf16)]
        + [step_out(batch_count, (HALO, rows), f32)]
        + [sum_out((1, inner_own))] * 2,
        flops=rows_local * inner_own * 2000, bytes_accessed=rows_local * inner_own * 24,
    )
    grad_inputs, grad_maps = call(
        functools.partial(unmix_kernel, per), grid, scalars,
        scan_ins + [per_row(inputs, rows), per_row(grads, rows)],
        [row_out(rows_local, rows, inner_own, f32), row_out(rows_local, rows, 2 * states, f32)],
        scratch=[pltpu.VMEM((rows, rows), f32)],
        flops=rows_local * inner_own * 12000, bytes_accessed=rows_local * inner_own * 8,
    )
    (grad_out,) = call(
        out_kernel, (1,), (), [entire(normed_y_t), entire(flat_cot)],
        [sum_out((seq_size, inner_own, depth), bf16)],
        flops=2 * rows_local * inner_own * width_all, bytes_accessed=rows_local * width_all * 6,
    )
    leaving, grad_inputs, grad_out = scan_before(
        local, states, True, [lambda: grad_inputs, lambda _: grad_out]
    )

    grad_out = lax.all_to_all(grad_out, "seq", split_axis=0, concat_axis=0, tiled=True)
    grad_conv_out, grad_step, grad_bias, grad_heads = call(
        unscan_kernel, grid, scalars,
        scan_ins
        + [per_row(a, rows) for a in (scanned, conv_out, inputs, grads, grad_inputs, grad_maps)]
        + [per_step(entering), per_step(leaving), entire(skip), entire(scale), entire(spread)],
        [
            row_out(rows_local, rows, channels, f32),
            row_out(rows_local, rows, LANES, f32),
            sum_out((1, channels)),
            sum_out((HALO, LANES)),
        ],
        flops=rows_local * inner_own * 4000, bytes_accessed=rows_local * inner_own * 28,
    )
    after_rows = passed_along(grad_conv_out.reshape(batch_count, tok_dev, channels)[:, :HALO], "seq", -1)
    after_rows, branch = lax.optimization_barrier((after_rows, branch))
    grad_pre, row_dots, grad_taps = call(
        unconv_kernel, grid, scalars,
        [per_row(pre, rows), per_step(halo), per_row(grad_conv_out, rows), per_step(after_rows)]
        + [per_row(grad_step, rows), per_step(row_part), entire(taps)],
        [
            row_out(rows_local, rows, channels + LANES, bf16),
            step_out(batch_count, (HALO, rows), f32),
            sum_out((taps_total, channels)),
        ],
        scratch=[pltpu.VMEM((rows + HALO, LANES), f32)] * 2,
        flops=rows_local * inner_own * 100, bytes_accessed=rows_local * inner_own * 14,
    )
    columns = [(0, 0, 0, inner_own), (1, 0, inner_own, inner_own), (0, channels, 2 * inner_own, LANES)]
    sent, got = weight_gradient_sent(odd_t, [grad_pre, grad_gate], columns, depth)
    (state_part,) = call(
        functools.partial(state_kernel, depth), (head_size,), (place,),
        [
            entire(even_t), entire(odd_t),
            (grad_pre, (rows_local, 2 * states), lambda m, *_: (0, inner_own // (2 * states))),
        ],
        [row_out(width_all, width_own, 2 * states, bf16)],
        flops=4 * width_all * rows_local * states, bytes_accessed=width_all * rows_local * 2,
    )
    shared_size = (taps_total + 1) * 2 * states
    headed = jnp.concatenate(
        [grad_taps[:, inner_own:].reshape(1, -1), grad_bias[:, inner_own:], row_dots[:, 0, :].reshape(1, -1)],
        axis=1,
    )
    headed = axis_sum(headed, "head")
    row_dots = deal_column(headed[0, shared_size:])
    state_part = state_part.reshape(head_size, width_own, 2 * states)
    last = head_size - 1
    state_line = LineScatter([state_part[0], state_part[last]], state_part[1:last])
    sent, got, headed = state_line.advance(sent, got, headed)
    grad_rows = lambda quarters: rows_gradient(
        after(grad_pre, sent), grad_gate, full_in, quarters, seq_size, batch_count
    )
    edges = grad_rows((0, last, 2))
    (edges,) = state_line.advance(edges)
    rows_line = LineScatter([edges[0], edges[1]], grad_rows((1, 1, last - 1)))
    grad_w_state = state_line.finish()

    lines_of = lambda values: jnp.pad(values, (0, -values.size % (2 * states))).reshape(-1, 2 * states)
    small = [
        grad_taps[:, :inner_own], grad_bias[:, :inner_own], grad_gain, grad_skip, grad_heads[:2],
        headed[0, :shared_size],
    ]
    small_rows = [lines_of(values.reshape(-1)) for values in small]
    together = jnp.concatenate([grad_w_state] + small_rows).astype(bf16)
    grad_w_state = axis_sum(together, "seq")
    grad_inner, grad_w_gate, grad_w_step, grad_w_state = weight_gradient(
        rows_line, grad_w_state, even_t, got, [grad_pre, grad_gate], columns,
        inner_own,
        [
            (inner_own, [(0, 0, 0, inner_own)]),
            (inner_own, [(1, 0, 0, inner_own)]),
            (LANES, [(1, inner_own, 0, LANES)]),
        ],
        depth,
    )
    grad_out = jnp.sum(grad_out.astype(f32), axis=0)
    out_back = returned((deal_tokens.astype(f32) + branch.astype(f32) * inner_inv).astype(bf16))
    rows_own = rows_line.finish()
    unit_own = deal_tokens.astype(f32) * inv_rms
    gain_own = lax.dynamic_slice_in_dim(norm_gain, head_index * width_own, width_own, 0)
    grad_norm_gain = jnp.sum(rows_own * unit_own, axis=(0, 1, 2))
    grad_rows_in = inv_rms * (rows_own * gain_own - unit_own * (row_dots / width_all))
    grad_back = returned((grad_rows_in + deal_cot.astype(f32)).astype(bf16))

    grad_norm_gain = axis_sum(grad_norm_gain[None, :], "seq")[0]
    summed = []
    at = width_own
    for values, lines in zip(small, small_rows):
        part = grad_w_state[at : at + lines.shape[0]].astype(f32).reshape(-1)[: values.size]
        summed.append(part.reshape(values.shape))
        at += lines.shape[0]
    state_sums = summed[5].reshape(taps_total + 1, 2 * states)
    state_own = 2 * states // head_size
    state_sums = lax.dynamic_slice_in_dim(state_sums, head_index * state_own, state_own, 1)
    return (
        out_back,
        grad_back,
        grad_norm_gain,
        grad_w_gate,
        grad_inner,
        grad_w_state[:width_own].astype(f32),
        grad_w_step[:, :heads_own],
        summed[0],
        summed[1][0],
        state_sums[:taps_total],
        state_sums[taps_total],
        summed[4][1, :heads_own],
        summed[4][0, :heads_own],
        jnp.sum(summed[3].reshape(heads_own, head_width), axis=1),
        summed[2][0],
        grad_out,
    )


def solution(mesh):
    return jax.shard_map(
        per_device,
        mesh=mesh,
        in_specs=(
            P("seq", "head"),
            P("seq", "head"),
            P(),
            P("seq"),
            P(),
            P("seq", "head"),
            P("seq", "head"),
            P("seq", None),
            P("seq", "head"),
            P(None, "head"),
            P("head"),
            P(),
            P(),
            P("head"),
            P("head"),
            P("head"),
            P("head"),
            P("head", "seq"),
        ),
        out_specs=(
            P("seq", "head"),
            P("seq", "head"),
            P("head"),
            P("seq", "head"),
            P("seq", "head"),
            P("head", None),
            P("seq", "head"),
            P(None, "head"),
            P("head"),
            P(None, "head"),
            P("head"),
            P("head"),
            P("head"),
            P("head"),
            P("head"),
            P("head", "seq"),
        ),
        check_vma=False,
    )
```

time: 659 us -> 525 us (0.80)
  Pallas kernels: 185 us -> 116 us
  starting transfers between devices: 145 us -> 92.1 us
  other arithmetic: 71.6 us -> 24.3 us
  waiting for transfers between devices: 169 us -> 129 us
  matrix products: 4.63 us -> 27.3 us
  blocking collectives: 0 us -> 22.2 us
  local copies, waits for them, and re-layouts: 71.2 us -> 87.7 us
  between operations: 2.58 us -> 15.3 us
    pallas_call x20 -> x24, Pallas kernels: 185 us -> 116 us  [call(): pl.pallas_call(kernel, grid_spec=pltpu.PrefetchScalarGridSpec(num_scalar_...]
    unnamed x152 -> x225, local copies, waits for them, and re-layouts: 7.14 us -> 74.6 us
    ppermute x56 -> x23, waiting for transfers between devices: 87.4 us -> 39.8 us  [swapped(): lax.ppermute(value, axis, [(i, i ^ bit) for i in range(lax.axis_size(axis...]
    ppermute x56 -> x23, starting transfers between devices: 66.9 us -> 22.1 us  [swapped(): lax.ppermute(value, axis, [(i, i ^ bit) for i in range(lax.axis_size(axis...]
    dot_general x4 -> x7, matrix products: 4.63 us -> 27.3 us  [the longest x5 23.5 us: dot(): return jnp.dot(left, right, preferred_element_type=f32, precision=precision)]
    all_to_all x0 -> x1, blocking collectives: none -> 22.2 us  [dealt(): lax.all_to_all(values, 'seq', split_axis=0, concat_axis=0, tiled=True)]
    concatenate x21 -> x2, other arithmetic: 21.7 us -> 0.02 us  [the longest x1 0.01 us: per_device(): jnp.concatenate([grad_taps[:, inner_own:].reshape(1, -1), grad_bias[:, in...]
    ppermute x24, waiting for transfers between devices: 55.7 us -> 73.1 us  [the longest x6 45.7 us: advance(): lax.ppermute(self.down, 'head', [(i, i - 1) for i in range(1, self.size -...]
  transfers between devices with their start and end apart: 87 -> 56, of which waited for: 28 -> 29; matrix products, arithmetic and copies ran while one was open for 21% -> 11% of each run, Pallas kernels for 25% -> 18%
where the time goes in v3:
time: 525 us; the launch traced here: 515 us
  waiting for transfers between devices  129 us (25%)
  Pallas kernels  116 us (22%)
  starting transfers between devices  92.1 us (18%)
  local copies, waits for them, and re-layouts  87.7 us (17%)
  matrix products  27.3 us (5%)
  other arithmetic  24.3 us (5%)
  blocking collectives  22.2 us (4%)
  between operations  15.3 us (3%)
    pallas_call x24, Pallas kernels, call(): pl.pallas_call(kernel, grid_spec=pltpu.PrefetchScalarGridSpec(num_scalar_...  116 us
    unnamed x225, local copies, waits for them, and re-layouts  74.6 us
    ppermute x6, waiting for transfers between devices, advance(): lax.ppermute(self.down, 'head', [(i, i - 1) for i in range(1, self.size -...  45.7 us
    ppermute x23, waiting for transfers between devices, swapped(): lax.ppermute(value, axis, [(i, i ^ bit) for i in range(lax.axis_size(axis...  39.8 us
    dot_general x5, matrix products, dot(): return jnp.dot(left, right, preferred_element_type=f32, precision=precision)  23.5 us
    all_to_all x1, blocking collectives, dealt(): lax.all_to_all(values, 'seq', split_axis=0, concat_axis=0, tiled=True)  22.2 us
    ppermute x23, starting transfers between devices, swapped(): lax.ppermute(value, axis, [(i, i ^ bit) for i in range(lax.axis_size(axis...  22.1 us
    ppermute x6, starting transfers between devices, advance(): up = lax.ppermute(up, 'head', [(i, i + 1) for i in range(step)])  21 us
  transfers between devices with their start and end apart: 56, of which 29 were waited for; matrix products, arithmetic and copies ran while one was open for 11% of the time, Pallas kernels for 18%

profile of v3, /device:TPU:0, one launch (start us, length us, event | category | flops | bytes accessed | tf_op | source)
XLA Modules:
  0.0 514.7 jit_solution(10963318114966412766)
XLA Ops:
  12.7 22.2 %all_to_all.25 = bf16[8,96,512]{2,1,0:T(8,128)(2,1)S(1)} all-to-all(bf16[8,96,512]{2,1,0:T(8,128)(2,1)S(1)} %bitcast.191), channel_id=1, replica_groups=mesh['seq'=8,'head'=4] {'seq'}, dimensions={0} | all-to-all | bytes 1572864 | tf_op jit(solution)/shard_map/all_to_all | solution.py:980
  40.8 13.2 %collective-permute-done.3.refs_4_ = bf16[8,3,32,512]{3,2,1,0:T(8,128)(2,1)S(1)} collective-permute-done((bf16[8,3,32,512]{3,2,1,0:T(8,128)(2,1)S(1)}, bf16[8,3,32,512]{3,2,1,0:T(8,128)(2,1)S(1)}, u32[]{:S(2)}, u32[]{:S(2)}) %collective-permute-start.3) | collective-permute-done | bytes 786464 | tf_op jit(solution)/shard_map/ppermute | solution.py:75
  63.7 10.4 %collective-permute-done.4.refs_5_ = bf16[8,3,32,512]{3,2,1,0:T(8,128)(2,1)} collective-permute-done((bf16[8,3,32,512]{3,2,1,0:T(8,128)(2,1)S(1)}, bf16[8,3,32,512]{3,2,1,0:T(8,128)(2,1)}, u32[]{:S(2)}, u32[]{:S(2)}) %collective-permute-start.4) | collective-permute-done | bytes 786464 | tf_op jit(solution)/shard_map/ppermute | solution.py:75
  79.5 5.4 %all-to-all-done.1 = bf16[8,96,512]{2,1,0:T(8,128)(2,1)S(1)} async-done(((bf16[8,96,512]{2,1,0:T(8,128)(2,1)}), bf16[8,96,512]{2,1,0:T(8,128)(2,1)S(1)}, u32[]{:S(2)}, u32[]{:S(2)}) %all-to-all-start.1) | async-done | bytes 786464 | tf_op jit(solution)/shard_map/all_to_all | solution.py:980
  84.8 7.2 %collective-permute-done.5.refs_6_ = bf16[8,3,32,512]{3,2,1,0:T(8,128)(2,1)} collective-permute-done((bf16[8,3,32,512]{3,2,1,0:T(8,128)(2,1)}, bf16[8,3,32,512]{3,2,1,0:T(8,128)(2,1)}, u32[]{:S(2)}, u32[]{:S(2)}) %collective-permute-start.5) | collective-permute-done | bytes 786464 | tf_op jit(solution)/shard_map/ppermute | solution.py:75
  93.3 5.4 %collective-permute-start.6 = (bf16[8,3,32,512]{3,2,1,0:T(8,128)(2,1)S(1)}, bf16[8,3,32,512]{3,2,1,0:T(8,128)(2,1)}, u32[]{:S(2)}, u32[]{:S(2)}) collective-permute-start(bf16[8,3,32,512]{3,2,1,0:T(8,128)(2,1)S(1)} %bitcast.170), channel_id=1, source_target_pairs={{0,1},{1,2},{2,3},{4,5},{5,6},{6,7},{8,9},{9,10},{10,11},{12,13},{... | collective-permute-start | bytes 2359304 | tf_op jit(solution)/shard_map/ppermute | solution.py:74
  108.4 8.8 %fusion.pre = f32[768,1536]{1,0:T(8,128)S(1)} fusion(bf16[768,2048]{1,0:T(8,128)(2,1)} %copy-done.90, bf16[2048,2560]{1,0:T(8,128)(2,1)} %all-gather.3.cloned.1.call-done.weight), kind=kOutput, calls=%fused_computation.1 | convolution fusion | flops 4831838208 | bytes 14155776 | tf_op jit(solution)/shard_map/dot_general | solution.py:136
  122.1 7.3 %fusion.2.gate = f32[768,1024]{1,0:T(8,128)} fusion(bf16[768,2048]{1,0:T(8,128)(2,1)S(1)} %copy-done.91, bf16[2048,2560]{1,0:T(8,128)(2,1)} %all-gather.3.cloned.1.call-done.weight), kind=kOutput, calls=%fused_computation.3 | convolution fusion | flops 3221225472 | bytes 10485760 | tf_op jit(solution)/shard_map/dot_general | solution.py:136
  129.4 10.8 %shard_map.298 = (f32[768,1280]{1,0:T(8,128)S(1)}, f32[768,384]{1,0:T(8,128)S(1)}, bf16[768,1024]{1,0:T(8,128)(2,1)S(1)}, f32[768,256]{1,0:T(8,128)S(1)}, bf16[3,144,1024]{2,1,0:T(8,128)(2,1)}) custom-call(s32[4]{0:T(128)S(1)} %pad_add_fusion.place, s32[3,4]{1,0:T(4,128)S(1)} %sub.44.plan, f32[768,1536]{1,0:T(8,128)S(1)} %fusion.pre, ...), custom_call_target="tpu_custom_call" | custom-call | flops 24576000 | bytes 147456 | tf_op jit(solution)/shard_map/pallas_call | solution.py:176
  157.5 11.7 %collective-permute-done.14.refs_6_ = bf16[8,3,32,512]{3,2,1,0:T(8,128)(2,1)} collective-permute-done((bf16[8,3,32,512]{3,2,1,0:T(8,128)(2,1)}, bf16[8,3,32,512]{3,2,1,0:T(8,128)(2,1)}, u32[]{:S(2)}, u32[]{:S(2)}) %collective-permute-start.14) | collective-permute-done | bytes 786464 | tf_op jit(solution)/shard_map/ppermute | solution.py:75
  176.3 6.1 %shard_map.302 = (bf16[768,2048]{1,0:T(8,128)(2,1)S(1)}, f32[768,1024]{1,0:T(8,128)S(1)}) custom-call(s32[4]{0:T(128)S(1)} %pad_add_fusion.place, bf16[8,3,32,512]{3,2,1,0:T(8,128)(2,1)S(1)} %bitcast.171, bf16[8,3,32,512]{3,2,1,0:T(8,128)(2,1)} %collective-permute-done.6.refs_1_, bf16[8,3,32,512]{3,2,1,0:T(8,128)(2,1)} %collective-permute-done.8.refs_2_, ...), custom_call_target="tpu_custom_call" | custom-call | flops 50331648 | bytes 249856 | tf_op jit(solution)/shard_map/pallas_call | solution.py:176
  225.7 11.2 %shard_map.306 = (bf16[1024,768]{1,0:T(8,128)(2,1)S(1)}, bf16[768,1024]{1,0:T(8,128)(2,1)S(1)}, bf16[768,1024]{1,0:T(8,128)(2,1)S(1)}, bf16[3,144,1024]{2,1,0:T(...) custom-call(s32[4]{0:T(128)S(1)} %pad_add_fusion.place, ...), custom_call_target="tpu_custom_call" | custom-call | flops 24576000 | bytes 294912 | tf_op jit(solution)/shard_map/pallas_call | solution.py:176
  248.0 7.8 %shard_map.308 = (f32[768,1024]{1,0:T(8,128)S(1)}, f32[768,256]{1,0:T(8,128)S(1)}) custom-call(s32[4]{0:T(128)S(1)} %pad_add_fusion.place, s32[3,4]{1,0:T(4,128)S(1)} %sub.44.plan, f32[768,384]{1,0:T(8,128)S(1)} %get-tuple-element.121.small, f32[768,256]{1,0:T(8,128)S(1)} %get-tuple-element.122.maps, bf16[768,1024]{1,0:T(8,128)(2,1)S(1)} %get-tuple-element.124.inputs, ...), custom_call_target="tpu_custom_call" | custom-call | flops 147456000 | bytes 98304 | tf_op jit(solution)/shard_map/pallas_call | solution.py:176
  276.2 11.7 %shard_map.313 = (f32[768,1280]{1,0:T(8,128)S(1)}, f32[768,128]{1,0:T(8,128)S(1)}, f32[1,1280]{1,0:T(1,128)S(1)}, f32[8,128]{1,0:T(8,128)S(1)}) custom-call(s32[4]{0:T(128)S(1)} %pad_add_fusion.place, s32[3,4]{1,0:T(4,128)S(1)} %sub.44.plan, f32[768,384]{1,0:T(8,128)S(1)} %get-tuple-element.121.small, f32[768,256]{1,0:T(8,128)S(1)} %get-tuple-element.122.maps, ...), custom_call_target="tpu_custom_call" | custom-call | flops 49152000 | bytes 344064 | tf_op jit(solution)/shard_map/pallas_call | solution.py:176
  302.3 9.3 %shard_map.314 = (bf16[768,1408]{1,0:T(8,128)(2,1)S(1)}, f32[3,8,256]{2,1,0:T(8,128)S(1)}, f32[4,1280]{1,0:T(4,128)S(1)}) custom-call(s32[4]{0:T(128)S(1)} %pad_add_fusion.place, s32[3,4]{1,0:T(4,128)S(1)} %sub.44.plan, f32[768,1536]{1,0:T(8,128)S(1)} %copy-done.16, f32[3,8,1536]{2,1,0:T(8,128)S(1)} %copy-done.64, f32[768,1280]{1,0:T(8,128)S(1)} %copy-done.54, ...), custom_call_target="tpu_custom_call" | custom-call | flops 1228800 | bytes 172032 | tf_op jit(solution)/shard_map/pallas_call | solution.py:176
  311.6 5.5 %shard_map.316 = bf16[1024,2176]{1,0:T(8,128)(2,1)} custom-call(bf16[1024,768]{1,0:T(8,128)(2,1)S(1)} %copy-done.47, bf16[768,1408]{1,0:T(8,128)(2,1)S(1)} %get-tuple-element.164.grads.refs_0_.first, bf16[768,1024]{1,0:T(8,128)(2,1)S(1)} %copy-done.11), custom_call_target="tpu_custom_call" | custom-call | flops 53477376 | bytes 152576 | tf_op jit(solution)/shard_map/pallas_call | solution.py:176
  356.0 5.5 %shard_map.317 = bf16[2,8,3,32,512]{4,3,2,1,0:T(8,128)(2,1)S(1)} custom-call(bf16[768,1408]{1,0:T(8,128)(2,1)S(1)} %get-tuple-element.164.grads.refs_0_.first, bf16[768,1024]{1,0:T(8,128)(2,1)S(1)} %copy-done.12, bf16[2048,2560]{1,0:T(8,128)(2,1)S(1)} %copy-done.2), custom_call_target="tpu_custom_call" | custom-call | flops 59768832 | bytes 280576 | tf_op jit(solution)/shard_map/pallas_call | solution.py:176
  387.1 7.4 %collective-permute-done.36 = bf16[546,256]{1,0:T(8,128)(2,1)S(1)} collective-permute-done((bf16[546,256]{1,0:T(8,128)(2,1)S(1)}, bf16[546,256]{1,0:T(8,128)(2,1)S(1)}, u32[]{:S(2)}, u32[]{:S(2)}) %collective-permute-start.36) | collective-permute-done | bytes 279584 | tf_op jit(solution)/shard_map/ppermute | solution.py:21
  396.1 8.4 %shard_map.319 = (bf16[512,1024]{1,0:T(8,128)(2,1)S(1)}, bf16[512,1024]{1,0:T(8,128)(2,1)}, bf16[512,1152]{1,0:T(8,128)(2,1)S(1)}, bf16[512,1152]{1,0:T(8,128)(2,1)S(1)}) custom-call(bf16[1024,768]{1,0:T(8,128)(2,1)S(1)} %copy-done.45, bf16[768,1408]{1,0:T(8,128)(2,1)S(1)} %get-tuple-element.164.grads.refs_0_.first, bf16[768,1024]{1,0:T(8,128)(2,1)S(1)} %copy-done.13, ...), custom_call_target="tpu_custom_call" | custom-call | flops 53477376 | bytes 152576 | tf_op jit(solution)/shard_map/pallas_call | solution.py:176
  419.6 5.4 %shard_map.318 = bf16[2,8,3,32,512]{4,3,2,1,0:T(8,128)(2,1)S(1)} custom-call(bf16[768,1408]{1,0:T(8,128)(2,1)S(1)} %get-tuple-element.164.grads.refs_0_.first, bf16[768,1024]{1,0:T(8,128)(2,1)S(1)} %copy-done.14, bf16[2048,2560]{1,0:T(8,128)(2,1)S(1)} %copy-done.3), custom_call_target="tpu_custom_call" | custom-call | flops 59768832 | bytes 280576 | tf_op jit(solution)/shard_map/pallas_call | solution.py:176
  439.1 8.3 %collective-permute-done.38 = bf16[8,3,32,512]{3,2,1,0:T(8,128)(2,1)S(1)} collective-permute-done((bf16[8,3,32,512]{3,2,1,0:T(8,128)(2,1)S(1)}, bf16[8,3,32,512]{3,2,1,0:T(8,128)(2,1)S(1)}, u32[]{:S(2)}, u32[]{:S(2)}) %collective-permute-start.38) | collective-permute-done | bytes 786464 | tf_op jit(solution)/shard_map/ppermute | solution.py:110
  451.6 5.2 %collective-permute-start.42 = (bf16[8,3,32,512]{3,2,1,0:T(8,128)(2,1)S(1)}, bf16[8,3,32,512]{3,2,1,0:T(8,128)(2,1)S(1)}, u32[]{:S(2)}, u32[]{:S(2)}) collective-permute-start(bf16[8,3,32,512]{3,2,1,0:T(8,128)(2,1)S(1)} %get-tuple-element.255), channel_id=1, source_target_pairs={{0,1},{1,2},{2,3},{4,5},{5,6},{6,7},{8,9},{9,10},{10,11},{12,13},{... | collective-permute-start | bytes 2359304 | tf_op jit(solution)/shard_map/ppermute | solution.py:110
  461.0 8.8 %collective-permute-done.43 = bf16[8,3,32,512]{3,2,1,0:T(8,128)(2,1)S(1)} collective-permute-done((bf16[8,3,32,512]{3,2,1,0:T(8,128)(2,1)S(1)}, bf16[8,3,32,512]{3,2,1,0:T(8,128)(2,1)S(1)}, u32[]{:S(2)}, u32[]{:S(2)}) %collective-permute-start.43) | collective-permute-done | bytes 786464 | tf_op jit(solution)/shard_map/ppermute | solution.py:111
  481.4 8.6 %all-to-all-done.2 = bf16[8,96,512]{2,1,0:T(8,128)(2,1)S(1)} async-done(((bf16[8,96,512]{2,1,0:T(8,128)(2,1)}), bf16[8,96,512]{2,1,0:T(8,128)(2,1)S(1)}, u32[]{:S(2)}, u32[]{:S(2)}) %all-to-all-start.2) | async-done | bytes 786464 | tf_op jit(solution)/shard_map/all_to_all | solution.py:985
  (435 shorter events, 287.8 us)
Async XLA Ops:
  7.2 101.2 %all-gather.3.cloned.1.call-start = ((), (), s32[]{:S(2)}) async-start(), calls=%async_computation.6 | async-start | bytes 11796480 | tf_op jit(solution)/shard_map/all_gather | solution.py:993
  11.5 161.5 %all-gather.5.cloned.1.call-start = ((), (), s32[]{:S(2)}) async-start(), calls=%async_computation.7 | async-start | bytes 4718592 | tf_op jit(solution)/shard_map/all_gather | solution.py:1000
  34.9 19.1 %collective-permute-start.3 = (bf16[8,3,32,512]{3,2,1,0:T(8,128)(2,1)S(1)}, bf16[8,3,32,512]{3,2,1,0:T(8,128)(2,1)S(1)}, u32[]{:S(2)}, u32[]{:S(2)}) collective-permute-start(bf16[8,3,32,512]{3,2,1,0:T(8,128)(2,1)S(1)} %bitcast.164), channel_id=1, source_target_pairs={{1,0},{2,1},{3,2},{5,4},{6,5},{7,6},{9,8},{10,9},{11,10},{13,12},{... | collective-permute-start | bytes 2359304 | tf_op jit(solution)/shard_map/ppermute | solution.py:75
  36.2 19.0 %collective-permute-start = (bf16[8,3,32,512]{3,2,1,0:T(8,128)(2,1)S(1)}, bf16[8,3,32,512]{3,2,1,0:T(8,128)(2,1)S(1)}, u32[]{:S(2)}, u32[]{:S(2)}) collective-permute-start(bf16[8,3,32,512]{3,2,1,0:T(8,128)(2,1)S(1)} %bitcast.165), channel_id=1, source_target_pairs={{0,1},{1,2},{2,3},{4,5},{5,6},{6,7},{8,9},{9,10},{10,11},{12,13},{... | collective-permute-start | bytes 2359304 | tf_op jit(solution)/shard_map/ppermute | solution.py:74
  55.2 18.9 %collective-permute-start.4 = (bf16[8,3,32,512]{3,2,1,0:T(8,128)(2,1)S(1)}, bf16[8,3,32,512]{3,2,1,0:T(8,128)(2,1)}, u32[]{:S(2)}, u32[]{:S(2)}) collective-permute-start(bf16[8,3,32,512]{3,2,1,0:T(8,128)(2,1)S(1)} %collective-permute-done.3.refs_4_), channel_id=1, source_target_pairs={{1,0},{2,1},{5,4},{6,5},{9,8},{10,9},{13,12},{14,13},{17,16},{18,1... | collective-permute-start | bytes 2359304 | tf_op jit(solution)/shard_map/ppermute | solution.py:75
  56.5 18.9 %collective-permute-start.1 = (bf16[8,3,32,512]{3,2,1,0:T(8,128)(2,1)S(1)}, bf16[8,3,32,512]{3,2,1,0:T(8,128)(2,1)}, u32[]{:S(2)}, u32[]{:S(2)}) collective-permute-start(bf16[8,3,32,512]{3,2,1,0:T(8,128)(2,1)S(1)} %collective-permute-done.refs_1_), channel_id=1, source_target_pairs={{1,2},{2,3},{5,6},{6,7},{9,10},{10,11},{13,14},{14,15},{17,18},{18... | collective-permute-start | bytes 2359304 | tf_op jit(solution)/shard_map/ppermute | solution.py:74
  59.9 24.9 %all-to-all-start.1 = ((bf16[8,96,512]{2,1,0:T(8,128)(2,1)}), bf16[8,96,512]{2,1,0:T(8,128)(2,1)S(1)}, u32[]{:S(2)}, u32[]{:S(2)}) async-start(bf16[8,96,512]{2,1,0:T(8,128)(2,1)} %bitcast.189), calls=%async_computation.1 | async-start | bytes 1572864 | tf_op jit(solution)/shard_map/all_to_all | solution.py:980
  63.6 230.9 %reduce-scatter.2.cloned.1.call-start = ((), (), s32[]{:S(2)}) async-start(), calls=%async_computation.8 | async-start | bytes 3932160 | tf_op jit(solution)/shard_map/reduce_scatter | solution.py:1070
  74.1 17.9 %collective-permute-start.5 = (bf16[8,3,32,512]{3,2,1,0:T(8,128)(2,1)}, bf16[8,3,32,512]{3,2,1,0:T(8,128)(2,1)}, u32[]{:S(2)}, u32[]{:S(2)}) collective-permute-start(bf16[8,3,32,512]{3,2,1,0:T(8,128)(2,1)} %collective-permute-done.4.refs_5_), channel_id=1, source_target_pairs={{1,0},{5,4},{9,8},{13,12},{17,16},{21,20},{25,24},{29,28}} | collective-permute-start | bytes 2359304 | tf_op jit(solution)/shard_map/ppermute | solution.py:75
  92.0 25.2 %collective-permute-start.7 = (bf16[8,3,32,512]{3,2,1,0:T(8,128)(2,1)S(1)}, bf16[8,3,32,512]{3,2,1,0:T(8,128)(2,1)}, u32[]{:S(2)}, u32[]{:S(2)}) collective-permute-start(bf16[8,3,32,512]{3,2,1,0:T(8,128)(2,1)S(1)} %bitcast.169), channel_id=1, source_target_pairs={{1,0},{2,1},{3,2},{5,4},{6,5},{7,6},{9,8},{10,9},{11,10},{13,12},{... | collective-permute-start | bytes 2359304 | tf_op jit(solution)/shard_map/ppermute | solution.py:75
  93.3 23.9 %collective-permute-start.6 = (bf16[8,3,32,512]{3,2,1,0:T(8,128)(2,1)S(1)}, bf16[8,3,32,512]{3,2,1,0:T(8,128)(2,1)}, u32[]{:S(2)}, u32[]{:S(2)}) collective-permute-start(bf16[8,3,32,512]{3,2,1,0:T(8,128)(2,1)S(1)} %bitcast.170), channel_id=1, source_target_pairs={{0,1},{1,2},{2,3},{4,5},{5,6},{6,7},{8,9},{9,10},{10,11},{12,13},{... | collective-permute-start | bytes 2359304 | tf_op jit(solution)/shard_map/ppermute | solution.py:74
  118.7 23.5 %collective-permute-start.8 = (bf16[8,3,32,512]{3,2,1,0:T(8,128)(2,1)}, bf16[8,3,32,512]{3,2,1,0:T(8,128)(2,1)}, u32[]{:S(2)}, u32[]{:S(2)}) collective-permute-start(bf16[8,3,32,512]{3,2,1,0:T(8,128)(2,1)} %collective-permute-done.6.refs_1_), channel_id=1, source_target_pairs={{1,2},{2,3},{5,6},{6,7},{9,10},{10,11},{13,14},{14,15},{17,18},{18... | collective-permute-start | bytes 2359304 | tf_op jit(solution)/shard_map/ppermute | solution.py:74
  120.3 25.1 %collective-permute-start.9 = (bf16[8,3,32,512]{3,2,1,0:T(8,128)(2,1)}, bf16[8,3,32,512]{3,2,1,0:T(8,128)(2,1)}, u32[]{:S(2)}, u32[]{:S(2)}) collective-permute-start(bf16[8,3,32,512]{3,2,1,0:T(8,128)(2,1)} %collective-permute-done.7.refs_4_), channel_id=1, source_target_pairs={{1,0},{2,1},{5,4},{6,5},{9,8},{10,9},{13,12},{14,13},{17,16},{18,1... | collective-permute-start | bytes 2359304 | tf_op jit(solution)/shard_map/ppermute | solution.py:75
  146.9 22.3 %collective-permute-start.14 = (bf16[8,3,32,512]{3,2,1,0:T(8,128)(2,1)}, bf16[8,3,32,512]{3,2,1,0:T(8,128)(2,1)}, u32[]{:S(2)}, u32[]{:S(2)}) collective-permute-start(bf16[8,3,32,512]{3,2,1,0:T(8,128)(2,1)} %collective-permute-done.9.refs_5_), channel_id=1, source_target_pairs={{1,0},{5,4},{9,8},{13,12},{17,16},{21,20},{25,24},{29,28}} | collective-permute-start | bytes 2359304 | tf_op jit(solution)/shard_map/ppermute | solution.py:75
  150.2 19.0 %collective-permute-start.12 = (bf16[3,144,512]{2,1,0:T(8,128)(2,1)S(1)}, bf16[3,144,512]{2,1,0:T(8,128)(2,1)S(1)}, u32[]{:S(2)}, u32[]{:S(2)}) collective-permute-start(bf16[3,144,512]{2,1,0:T(8,128)(2,1)S(1)} %shard_map.299.refs_0_), channel_id=1, source_target_pairs={{0,8},{4,12},{8,0},{12,4},{16,24},{20,28},{24,16},{28,20},{1,9},{5... | collective-permute-start | bytes 1327112 | tf_op jit(solution)/shard_map/ppermute | solution.py:21
  317.1 25.8 %collective-permute-start.26 = (bf16[1024,2176]{1,0:T(8,128)(2,1)}, bf16[1024,2176]{1,0:T(8,128)(2,1)}, u32[]{:S(2)}, u32[]{:S(2)}) collective-permute-start(bf16[1024,2176]{1,0:T(8,128)(2,1)} %shard_map.316), channel_id=1, source_target_pairs={{0,4},{4,0},{8,12},{12,8},{16,20},{20,16},{24,28},{28,24},{1,5},{5... | collective-permute-start | bytes 13369352 | tf_op jit(solution)/shard_map/ppermute | solution.py:21
  320.2 91.5 %all-to-all-start.4 = ((bf16[8,1024,256]{2,1,0:T(8,128)(2,1)}), bf16[8,1024,256]{2,1,0:T(8,128)(2,1)}, u32[]{:S(2)}, u32[]{:S(2)}) async-start(bf16[8,1024,256]{2,1,0:T(8,128)(2,1)} %copy-done.19), calls=%async_computation.5 | async-start | bytes 8388608 | tf_op jit(solution)/shard_map/all_to_all | solution.py:1106
  344.9 17.8 %collective-permute-start.30 = (bf16[512,256]{1,0:T(8,128)(2,1)}, bf16[512,256]{1,0:T(8,128)(2,1)S(1)}, u32[]{:S(2)}, u32[]{:S(2)}) collective-permute-start(bf16[512,256]{1,0:T(8,128)(2,1)} %get-tuple-element.262), channel_id=1, source_target_pairs={{2,1},{3,2},{6,5},{7,6},{10,9},{11,10},{14,13},{15,14},{18,17},{19... | collective-permute-start | bytes 786440 | tf_op jit(solution)/shard_map/ppermute | solution.py:111
  380.7 27.1 %collective-permute-start.32 = (bf16[8,3,32,512]{3,2,1,0:T(8,128)(2,1)S(1)}, bf16[8,3,32,512]{3,2,1,0:T(8,128)(2,1)}, u32[]{:S(2)}, u32[]{:S(2)}) collective-permute-start(bf16[8,3,32,512]{3,2,1,0:T(8,128)(2,1)S(1)} %get-tuple-element.260), channel_id=1, source_target_pairs={{3,2},{7,6},{11,10},{15,14},{19,18},{23,22},{27,26},{31,30}} | collective-permute-start | bytes 2359304 | tf_op jit(solution)/shard_map/ppermute | solution.py:111
  382.3 25.4 %collective-permute-start.31 = (bf16[8,3,32,512]{3,2,1,0:T(8,128)(2,1)S(1)}, bf16[8,3,32,512]{3,2,1,0:T(8,128)(2,1)}, u32[]{:S(2)}, u32[]{:S(2)}) collective-permute-start(bf16[8,3,32,512]{3,2,1,0:T(8,128)(2,1)S(1)} %get-tuple-element.261), channel_id=1, source_target_pairs={{0,1},{4,5},{8,9},{12,13},{16,17},{20,21},{24,25},{28,29}} | collective-permute-start | bytes 2359304 | tf_op jit(solution)/shard_map/ppermute | solution.py:110
  407.7 24.6 %collective-permute-start.40 = (bf16[2,256,1024]{2,1,0:T(8,128)(2,1)}, bf16[2,256,1024]{2,1,0:T(8,128)(2,1)}, u32[]{:S(2)}, u32[]{:S(2)}) collective-permute-start(bf16[2,256,1024]{2,1,0:T(8,128)(2,1)} %bitcast.40), channel_id=1, source_target_pairs={{0,16},{4,20},{8,24},{12,28},{16,0},{20,4},{24,8},{28,12},{1,17},{... | collective-permute-start | bytes 3145736 | tf_op jit(solution)/shard_map/ppermute | solution.py:21
  410.2 27.0 %collective-permute-start.41 = (bf16[2,256,1152]{2,1,0:T(8,128)(2,1)}, bf16[2,256,1152]{2,1,0:T(8,128)(2,1)}, u32[]{:S(2)}, u32[]{:S(2)}) collective-permute-start(bf16[2,256,1152]{2,1,0:T(8,128)(2,1)} %bitcast.183), channel_id=1, source_target_pairs={{0,8},{4,12},{8,0},{12,4},{16,24},{20,28},{24,16},{28,20},{1,9},{5... | collective-permute-start | bytes 3538952 | tf_op jit(solution)/shard_map/ppermute | solution.py:21
  450.3 19.5 %collective-permute-start.43 = (bf16[8,3,32,512]{3,2,1,0:T(8,128)(2,1)S(1)}, bf16[8,3,32,512]{3,2,1,0:T(8,128)(2,1)S(1)}, u32[]{:S(2)}, u32[]{:S(2)}) collective-permute-start(bf16[8,3,32,512]{3,2,1,0:T(8,128)(2,1)S(1)} %get-tuple-element.254), channel_id=1, source_target_pairs={{1,0},{2,1},{3,2},{5,4},{6,5},{7,6},{9,8},{10,9},{11,10},{13,12},{... | collective-permute-start | bytes 2359304 | tf_op jit(solution)/shard_map/ppermute | solution.py:111
  451.6 19.5 %collective-permute-start.42 = (bf16[8,3,32,512]{3,2,1,0:T(8,128)(2,1)S(1)}, bf16[8,3,32,512]{3,2,1,0:T(8,128)(2,1)S(1)}, u32[]{:S(2)}, u32[]{:S(2)}) collective-permute-start(bf16[8,3,32,512]{3,2,1,0:T(8,128)(2,1)S(1)} %get-tuple-element.255), channel_id=1, source_target_pairs={{0,1},{1,2},{2,3},{4,5},{5,6},{6,7},{8,9},{9,10},{10,11},{12,13},{... | collective-permute-start | bytes 2359304 | tf_op jit(solution)/shard_map/ppermute | solution.py:110
  (140 other events, 1222.8 us)
Sparse Core Ops, SparseCore 0:
  11.7 78.3 all-gather.2
  92.0 38.3 all-gather.4
  216.1 59.8 reduce-scatter.1
